TPU v7x, 32 devices: a whole 2x2x4 slice. The times are simulated.
32 devices in a mesh: img: 8 (over z, y), ch: 4 (over x, core).
Axes of the slice: x: 2, y: 2, z: 4, core: 2. Of those that a mesh axis runs over, the one named last changes fastest.
Arguments:
- x_big: bfloat16 [64, 14, 14, 1024], P('img', None, None, 'ch'), may hold values from -6 to 6
- x_small: bfloat16 [64, 10, 10, 1024], P('img', None, None, 'ch'), may hold values from -6 to 6
- cot_big: bfloat16 [64, 7, 7, 2048], P('img', None, None, 'ch'), may hold values from -6 to 6
- cot_small: bfloat16 [64, 5, 5, 2048], P('img', None, None, 'ch'), may hold values from -6 to 6
- counts: int32 [8, 2], replicated, may hold values from 1 to 8, as said below
- w_reduce: bfloat16 [1024, 256], P(None, 'ch'), may hold values from -0.1875 to 0.1875
- w_mix: bfloat16 [3, 3, 256, 256], P(None, None, None, 'ch'), may hold values from -0.125 to 0.125
- w_expand: bfloat16 [256, 1024], P(None, 'ch'), may hold values from -0.375 to 0.375
- w_narrow: bfloat16 [1024, 512], P(None, 'ch'), may hold values from -0.1875 to 0.1875
- w_stride: bfloat16 [3, 3, 512, 512], P(None, None, None, 'ch'), may hold values from -0.09375 to 0.09375
- w_widen: bfloat16 [512, 2048], P(None, 'ch'), may hold values from -0.25 to 0.25
- w_short: bfloat16 [1024, 2048], P(None, 'ch'), may hold values from -0.1875 to 0.1875
- gain_mid3: float32 [2, 256], P(None, 'ch'), may hold values from 0.1 to 1.9
- shift_mid3: float32 [2, 256], P(None, 'ch'), may hold values from -3 to 3
- gain_out3: float32 [1024], P('ch'), may hold values from 0.1 to 1.9
- shift_out3: float32 [1024], P('ch'), may hold values from -3 to 3
- gain_mid4: float32 [2, 512], P(None, 'ch'), may hold values from 0.1 to 1.9
- shift_mid4: float32 [2, 512], P(None, 'ch'), may hold values from -3 to 3
- gain_out4: float32 [2, 2048], P(None, 'ch'), may hold values from 0.1 to 1.9
- shift_out4: float32 [2, 2048], P(None, 'ch'), may hold values from -3 to 3
Outputs:
- out_big: float32 [64, 7, 7, 2048], P('img', None, None, 'ch')
- out_small: float32 [64, 5, 5, 2048], P('img', None, None, 'ch')
- grad_x_big: float32 [64, 14, 14, 1024], P('img', None, None, 'ch')
- grad_x_small: float32 [64, 10, 10, 1024], P('img', None, None, 'ch')
- grad_w_reduce: float32 [1024, 256], P(None, 'ch')
- grad_w_mix: float32 [3, 3, 256, 256], P(None, None, None, 'ch')
- grad_w_expand: float32 [256, 1024], P(None, 'ch')
- grad_w_narrow: float32 [1024, 512], P(None, 'ch')
- grad_w_stride: float32 [3, 3, 512, 512], P(None, None, None, 'ch')
- grad_w_widen: float32 [512, 2048], P(None, 'ch')
- grad_w_short: float32 [1024, 2048], P(None, 'ch')
- grad_gain_mid3: float32 [2, 256], P(None, 'ch')
- grad_shift_mid3: float32 [2, 256], P(None, 'ch')
- grad_gain_out3: float32 [1024], P('ch')
- grad_shift_out3: float32 [1024], P('ch')
- grad_gain_mid4: float32 [2, 512], P(None, 'ch')
- grad_shift_mid4: float32 [2, 512], P(None, 'ch')
- grad_gain_out4: float32 [2, 2048], P(None, 'ch')
- grad_shift_out4: float32 [2, 2048], P(None, 'ch')
Inputs may be any that keep to these rules, and one draw needn't show every extreme that they name: `counts`: column 0 lies between 1 and 8, column 1 between 1 and 8; in every draw some index is full in column 0 and some in column 1. The live views of a device are its first slots.
All inputs are finite; a program needn't handle non-finite values.
Results may differ from a plain program's by a relative error of at most 0.03.
Values may be sent and summed in bfloat16 or wider, within the bound.
No kernel may reach another device: no remote copies, remote signals or barrier semaphores. Data moves between devices by JAX's collectives and lax.ppermute only.
A program may use at most 192 MiB of HBM per device.

v0:
```python
import jax
import jax.numpy as jnp
from jax import lax
from jax.sharding import PartitionSpec as P

epsilon = 1e-05


def project(inputs, weight):
    return jnp.einsum("bhwc,cd->bhwd", inputs, weight, preferred_element_type=jnp.float32)


def flat_input(grad_out, weight):
    return jnp.einsum("bhwd,cd->bhwc", grad_out, weight, preferred_element_type=jnp.float32)


def flat_weight(inputs, grad_out):
    return jnp.einsum("bhwc,bhwd->cd", inputs, grad_out, preferred_element_type=jnp.float32)


def to_phases(values):
    return values.reshape(
        (values.shape[0], values.shape[1] // 2, 2, values.shape[2] // 2, 2, values.shape[3])
    )


def from_phases(values):
    return values.reshape(
        (values.shape[0], values.shape[1] * 2, values.shape[3] * 2, values.shape[5])
    )


def even_pixels(values):
    return to_phases(values)[:, :, 0, :, 0, :]


def add_even(values, extra):
    return from_phases(to_phases(values).at[:, :, 0, :, 0, :].add(extra))


def tap_window(padded, row_tap, col_tap, stride, height, width):
    if stride == 1:
        return padded[:, row_tap : row_tap + height, col_tap : col_tap + width, :]
    phases = to_phases(padded)
    return phases[
        :,
        row_tap // 2 : row_tap // 2 + height,
        row_tap % 2,
        col_tap // 2 : col_tap // 2 + width,
        col_tap % 2,
        :,
    ]


def conv_taps(inputs, weight, stride):
    padded = jnp.pad(inputs, ((0, 0), (1, 1), (1, 1), (0, 0)))
    height = (inputs.shape[1] - 1) // stride + 1
    width = (inputs.shape[2] - 1) // stride + 1
    result = jnp.zeros((inputs.shape[0], height, width, weight.shape[3]), jnp.float32)
    for row_tap in range(3):
        for col_tap in range(3):
            window = tap_window(padded, row_tap, col_tap, stride, height, width)
            result = result + jnp.einsum(
                "bhwc,cd->bhwd",
                window,
                weight[row_tap, col_tap],
                preferred_element_type=jnp.float32,
            )
    return result


def taps_weight(inputs, grad_out, stride):
    padded = jnp.pad(inputs, ((0, 0), (1, 1), (1, 1), (0, 0)))
    height = grad_out.shape[1]
    width = grad_out.shape[2]
    tap_grads = []
    for row_tap in range(3):
        for col_tap in range(3):
            window = tap_window(padded, row_tap, col_tap, stride, height, width)
            tap_grads.append(
                jnp.einsum("bhwc,bhwd->cd", window, grad_out, preferred_element_type=jnp.float32)
            )
    return jnp.stack(tap_grads).reshape((3, 3) + tap_grads[0].shape)


def taps_input(grad_out, weight, stride, side_len):
    height = grad_out.shape[1]
    width = grad_out.shape[2]
    views = grad_out.shape[0]
    chans = weight.shape[2]
    if stride == 1:
        grad_pad = jnp.zeros((views, side_len + 2, side_len + 2, chans), jnp.float32)
    else:
        grad_pad = jnp.zeros(
            (views, (side_len + 2) // 2, 2, (side_len + 2) // 2, 2, chans), jnp.float32
        )
    for row_tap in range(3):
        for col_tap in range(3):
            placed = jnp.einsum(
                "bhwd,cd->bhwc",
                grad_out,
                weight[row_tap, col_tap],
                preferred_element_type=jnp.float32,
            )
            if stride == 1:
                grad_pad = grad_pad.at[
                    :, row_tap : row_tap + height, col_tap : col_tap + width, :
                ].add(placed)
            else:
                grad_pad = grad_pad.at[
                    :,
                    row_tap // 2 : row_tap // 2 + height,
                    row_tap % 2,
                    col_tap // 2 : col_tap // 2 + width,
                    col_tap % 2,
                    :,
                ].add(placed)
    if stride != 1:
        grad_pad = from_phases(grad_pad)
    return grad_pad[:, 1:-1, 1:-1, :]


def gather_pair(pair):
    return (
        lax.all_gather(pair[0], "ch", axis=3, tiled=True),
        lax.all_gather(pair[1], "ch", axis=3, tiled=True),
    )


def scatter_pair(pair):
    return (
        lax.psum_scatter(
            pair[0].astype(jnp.bfloat16), "ch", scatter_dimension=3, tiled=True
        ).astype(jnp.float32),
        lax.psum_scatter(
            pair[1].astype(jnp.bfloat16), "ch", scatter_dimension=3, tiled=True
        ).astype(jnp.float32),
    )


def back_flat(inputs, weight, grads):
    grad_weight = flat_weight(inputs[0], grads[0]) + flat_weight(inputs[1], grads[1])
    grad_in = scatter_pair([flat_input(value, weight) for value in grads])
    return (grad_in, grad_weight)


def back_taps(inputs, weight, grads, stride):
    grad_weight = taps_weight(inputs[0], grads[0], stride) + taps_weight(
        inputs[1], grads[1], stride
    )
    grad_in = scatter_pair(
        [taps_input(grads[index], weight, stride, inputs[index].shape[1]) for index in range(2)]
    )
    return (grad_in, grad_weight)


def live_sum(values, lives):
    return jnp.sum(values[0] * lives[0], axis=(0, 1, 2)) + jnp.sum(
        values[1] * lives[1], axis=(0, 1, 2)
    )


def norm_forward(pre, gain_vec, shift_vec, lives, count):
    first = lax.psum(live_sum(pre, lives), "img")
    center = first / count
    devs = [value - center for value in pre]
    second = lax.psum(live_sum([devs[0] * devs[0], devs[1] * devs[1]], lives), "img")
    variance = second / count
    inv_std = lax.rsqrt(variance + epsilon)
    hats = [(value - center) * inv_std for value in pre]
    return ([hat * gain_vec + shift_vec for hat in hats], hats, inv_std)


def norm_backward(grads, hats, inv_std, gain_vec, lives, count):
    sum_grad = jnp.sum(grads[0], axis=(0, 1, 2)) + jnp.sum(grads[1], axis=(0, 1, 2))
    sum_hat = jnp.sum(grads[0] * hats[0], axis=(0, 1, 2)) + jnp.sum(
        grads[1] * hats[1], axis=(0, 1, 2)
    )
    sum_grad, sum_hat = lax.psum((sum_grad, sum_hat), "img")
    factor = gain_vec * inv_std
    result = [
        (
            factor * (grads[index] - lives[index] * (sum_grad + hats[index] * sum_hat) / count)
        ).astype(jnp.bfloat16)
        for index in range(2)
    ]
    return (result, sum_hat, sum_grad)


def gelu_back(values, grads):
    return jax.vjp(jax.nn.gelu, values)[1](grads)[0]


def per_device(
    x_big,
    x_small,
    cot_big,
    cot_small,
    counts,
    w_reduce,
    w_mix,
    w_expand,
    w_narrow,
    w_stride,
    w_widen,
    w_short,
    gain_mid3,
    shift_mid3,
    gain_out3,
    shift_out3,
    gain_mid4,
    shift_mid4,
    gain_out4,
    shift_out4,
):
    side_big = x_big.shape[1]
    side_small = x_small.shape[1]
    mine = lax.dynamic_slice_in_dim(counts, lax.axis_index("img"), 1, 0)[0]
    live_big = (jnp.arange(x_big.shape[0]) < mine[0]).astype(jnp.float32)
    live_small = (jnp.arange(x_small.shape[0]) < mine[1]).astype(jnp.float32)
    lives = [live_big[:, None, None, None], live_small[:, None, None, None]]
    views_big = jnp.sum(counts[:, 0]).astype(jnp.float32)
    views_small = jnp.sum(counts[:, 1]).astype(jnp.float32)
    count3 = views_big * (side_big * side_big) + views_small * (side_small * side_small)
    count4 = views_big * (side_big // 2 * (side_big // 2)) + views_small * (
        side_small // 2 * (side_small // 2)
    )
    inputs = [x_big, x_small]
    full_x = gather_pair(inputs)
    pre1 = [project(value, w_reduce) for value in full_x]
    norm1, hats1, istd1 = norm_forward(pre1, gain_mid3[0], shift_mid3[0], lives, count3)
    full1 = gather_pair([jax.nn.gelu(value).astype(jnp.bfloat16) for value in norm1])
    pre2 = [conv_taps(value, w_mix, 1) for value in full1]
    norm2, hats2, istd2 = norm_forward(pre2, gain_mid3[1], shift_mid3[1], lives, count3)
    full2 = gather_pair([jax.nn.gelu(value).astype(jnp.bfloat16) for value in norm2])
    pre3 = [project(value, w_expand) for value in full2]
    norm3, hats3, istd3 = norm_forward(pre3, gain_out3, shift_out3, lives, count3)
    sum3 = [norm3[index] + inputs[index].astype(jnp.float32) for index in range(2)]
    full_mid = gather_pair([jax.nn.gelu(value).astype(jnp.bfloat16) for value in sum3])
    pre4 = [project(value, w_narrow) for value in full_mid]
    norm4, hats4, istd4 = norm_forward(pre4, gain_mid4[0], shift_mid4[0], lives, count3)
    full4 = gather_pair([jax.nn.gelu(value).astype(jnp.bfloat16) for value in norm4])
    pre5 = [conv_taps(value, w_stride, 2) for value in full4]
    norm5, hats5, istd5 = norm_forward(pre5, gain_mid4[1], shift_mid4[1], lives, count4)
    full5 = gather_pair([jax.nn.gelu(value).astype(jnp.bfloat16) for value in norm5])
    strided = [even_pixels(value) for value in full_mid]
    pre6 = [project(value, w_widen) for value in full5]
    pre_side = [project(value, w_short) for value in strided]
    norm6, hats6, istd6 = norm_forward(pre6, gain_out4[0], shift_out4[0], lives, count4)
    norm_side, hats_side, istd_side = norm_forward(
        pre_side, gain_out4[1], shift_out4[1], lives, count4
    )
    totals = [norm6[index] + norm_side[index] for index in range(2)]
    outputs = [jax.nn.gelu(totals[index]) * lives[index] for index in range(2)]
    cots = [cot_big.astype(jnp.float32), cot_small.astype(jnp.float32)]
    d_total = [gelu_back(totals[index], cots[index] * lives[index]) for index in range(2)]
    d_pre6, dgain6, dshift6 = norm_backward(d_total, hats6, istd6, gain_out4[0], lives, count4)
    d_side, dgain_side, dshift_side = norm_backward(
        d_total, hats_side, istd_side, gain_out4[1], lives, count4
    )
    grad_short = flat_weight(strided[0], d_side[0]) + flat_weight(strided[1], d_side[1])
    d_act5, grad_widen = back_flat(full5, w_widen, d_pre6)
    d_pre5, dgain5, dshift5 = norm_backward(
        [gelu_back(norm5[index], d_act5[index]) for index in range(2)],
        hats5,
        istd5,
        gain_mid4[1],
        lives,
        count4,
    )
    d_act4, grad_stride = back_taps(full4, w_stride, d_pre5, 2)
    d_pre4, dgain4, dshift4 = norm_backward(
        [gelu_back(norm4[index], d_act4[index]) for index in range(2)],
        hats4,
        istd4,
        gain_mid4[0],
        lives,
        count3,
    )
    grad_narrow = flat_weight(full_mid[0], d_pre4[0]) + flat_weight(full_mid[1], d_pre4[1])
    mid_parts = [
        add_even(flat_input(d_pre4[index], w_narrow), flat_input(d_side[index], w_short))
        for index in range(2)
    ]
    d_mid = scatter_pair(mid_parts)
    d_sum3 = [gelu_back(sum3[index], d_mid[index]) for index in range(2)]
    d_pre3, dgain3, dshift3 = norm_backward(d_sum3, hats3, istd3, gain_out3, lives, count3)
    d_act2, grad_expand = back_flat(full2, w_expand, d_pre3)
    d_pre2, dgain2, dshift2 = norm_backward(
        [gelu_back(norm2[index], d_act2[index]) for index in range(2)],
        hats2,
        istd2,
        gain_mid3[1],
        lives,
        count3,
    )
    d_act1, grad_mix = back_taps(full1, w_mix, d_pre2, 1)
    d_pre1, dgain1, dshift1 = norm_backward(
        [gelu_back(norm1[index], d_act1[index]) for index in range(2)],
        hats1,
        istd1,
        gain_mid3[0],
        lives,
        count3,
    )
    d_input, grad_reduce = back_flat(full_x, w_reduce, d_pre1)
    grad_reduce, grad_mix, grad_expand, grad_narrow, grad_stride, grad_widen, grad_short = lax.psum(
        (grad_reduce, grad_mix, grad_expand, grad_narrow, grad_stride, grad_widen, grad_short),
        "img",
    )
    grad_big = d_input[0] + d_sum3[0]
    grad_small = d_input[1] + d_sum3[1]
    return (
        outputs[0],
        outputs[1],
        grad_big,
        grad_small,
        grad_reduce,
        grad_mix,
        grad_expand,
        grad_narrow,
        grad_stride,
        grad_widen,
        grad_short,
        jnp.stack([dgain1, dgain2]),
        jnp.stack([dshift1, dshift2]),
        dgain3,
        dshift3,
        jnp.stack([dgain4, dgain5]),
        jnp.stack([dshift4, dshift5]),
        jnp.stack([dgain6, dgain_side]),
        jnp.stack([dshift6, dshift_side]),
    )


def solution(mesh):
    in_specs = (
        P("img", None, None, "ch"),
        P("img", None, None, "ch"),
        P("img", None, None, "ch"),
        P("img", None, None, "ch"),
        P(),
        P(None, "ch"),
        P(None, None, None, "ch"),
        P(None, "ch"),
        P(None, "ch"),
        P(None, None, None, "ch"),
        P(None, "ch"),
        P(None, "ch"),
        P(None, "ch"),
        P(None, "ch"),
        P("ch"),
        P("ch"),
        P(None, "ch"),
        P(None, "ch"),
        P(None, "ch"),
        P(None, "ch"),
    )
    out_specs = (
        P("img", None, None, "ch"),
        P("img", None, None, "ch"),
        P("img", None, None, "ch"),
        P("img", None, None, "ch"),
        P(None, "ch"),
        P(None, None, None, "ch"),
        P(None, "ch"),
        P(None, "ch"),
        P(None, None, None, "ch"),
        P(None, "ch"),
        P(None, "ch"),
        P(None, "ch"),
        P(None, "ch"),
        P("ch"),
        P("ch"),
        P(None, "ch"),
        P(None, "ch"),
        P(None, "ch"),
        P(None, "ch"),
    )
    return jax.shard_map(
        per_device, mesh=mesh, in_specs=in_specs, out_specs=out_specs, check_vma=False
    )
```

profile of v0, /device:TPU:0, one launch (start us, length us, event | category | flops | bytes accessed | tf_op | source)
XLA Modules:
  0.0 1828.6 jit_solution(17735961693965271056)
XLA Ops:
  14.6 24.2 %all-gather.8.cloned.1.call-done = bf16[8,10,10,1024]{3,2,1,0:T(8,128)(2,1)} async-done(((bf16[8,10,10,256]{3,2,1,0:T(8,128)(2,1)}), bf16[8,10,10,1024]{3,2,1,0:T(8,128)(2,1)}) %all-gather.8.cloned.1.call-update) | async-done | bytes 1638416 | tf_op jit(solution)/shard_map/all_gather | solution.py:126
  41.4 31.5 %all-gather.6.cloned.1.call-done = bf16[8,14,14,1024]{3,2,1,0:T(8,128)(2,1)} async-done(((bf16[8,14,14,256]{3,2,1,0:T(8,128)(2,1)}), bf16[8,14,14,1024]{3,2,1,0:T(8,128)(2,1)}) %all-gather.6.cloned.1.call-update) | async-done | bytes 3211280 | tf_op jit(solution)/shard_map/all_gather | solution.py:125
  76.1 21.4 %psum.241 = f32[64]{0:T(128)S(1)} all-reduce(f32[64]{0:T(128)S(1)} %add.967), channel_id=1, replica_groups=mesh['img'=8,'ch'=4] {'img'}, use_global_device_ids=true, to_apply=%region_2.0 | all-reduce | flops 64 | bytes 512 | tf_op jit(solution)/shard_map/psum | solution.py:164
  98.1 17.1 psum.242
  122.7 32.3 %all_gather.39 = bf16[8,10,10,256]{2,0,1,3:T(8,128)(2,1)} all-gather(bf16[8,10,10,64]{2,0,1,3:T(8,128)(2,1)S(1)} %copy.169), channel_id=1, replica_groups=mesh['img'=8,'ch'=4] {'ch'}, dimensions={3}, use_global_device_ids=true | all-gather | bytes 512000 | tf_op jit(solution)/shard_map/all_gather | solution.py:126
  164.5 56.6 %all_gather.38 = bf16[8,14,14,256]{2,0,1,3:T(8,128)(2,1)} all-gather(bf16[8,14,14,64]{2,0,1,3:T(8,128)(2,1)S(1)} %copy-done.38), channel_id=1, replica_groups=mesh['img'=8,'ch'=4] {'ch'}, dimensions={3}, use_global_device_ids=true | all-gather | bytes 1003520 | tf_op jit(solution)/shard_map/all_gather | solution.py:125
  233.5 19.1 %psum.243 = f32[64]{0:T(128)S(1)} all-reduce(f32[64]{0:T(128)S(1)} %add.996), channel_id=1, replica_groups=mesh['img'=8,'ch'=4] {'img'}, use_global_device_ids=true, to_apply=%region_10.11 | all-reduce | flops 64 | bytes 512 | tf_op jit(solution)/shard_map/psum | solution.py:164
  253.3 17.1 psum.244
  276.9 36.7 %all_gather.41 = bf16[8,10,10,256]{2,0,1,3:T(8,128)(2,1)} all-gather(bf16[8,10,10,64]{2,0,1,3:T(8,128)(2,1)} %copy.174), channel_id=1, replica_groups=mesh['img'=8,'ch'=4] {'ch'}, dimensions={3}, use_global_device_ids=true | all-gather | bytes 512000 | tf_op jit(solution)/shard_map/all_gather | solution.py:126
  319.8 44.9 %all_gather.40 = bf16[8,14,14,256]{2,0,1,3:T(8,128)(2,1)} all-gather(bf16[8,14,14,64]{2,0,1,3:T(8,128)(2,1)S(1)} %copy.172), channel_id=1, replica_groups=mesh['img'=8,'ch'=4] {'ch'}, dimensions={3}, use_global_device_ids=true | all-gather | bytes 1003520 | tf_op jit(solution)/shard_map/all_gather | solution.py:125
  364.7 8.6 copy.173
  375.3 19.5 %psum.245 = f32[256]{0:T(256)} all-reduce(f32[256]{0:T(256)S(1)} %add.1008), channel_id=1, replica_groups=mesh['img'=8,'ch'=4] {'img'}, use_global_device_ids=true, to_apply=%region_16.17 | all-reduce | flops 256 | bytes 2048 | tf_op jit(solution)/shard_map/psum | solution.py:164
  398.1 18.0 psum.246
  427.4 16.5 all-gather.12.cloned.1.call-done
  449.8 28.2 %all-gather.10.cloned.1.call-done = bf16[8,14,14,1024]{3,2,1,0:T(8,128)(2,1)} async-done(((bf16[8,14,14,256]{3,2,1,0:T(8,128)(2,1)}), bf16[8,14,14,1024]{3,2,1,0:T(8,128)(2,1)}) %all-gather.10.cloned.1.call-update) | async-done | bytes 3211280 | tf_op jit(solution)/shard_map/all_gather | solution.py:125
  482.6 22.0 %psum.247 = f32[128]{0:T(128)} all-reduce(f32[128]{0:T(128)} %add.1022), channel_id=1, replica_groups=mesh['img'=8,'ch'=4] {'img'}, use_global_device_ids=true, to_apply=%region_22.23 | all-reduce | flops 128 | bytes 1024 | tf_op jit(solution)/shard_map/psum | solution.py:164
  508.6 17.7 psum.248
  532.2 15.3 all_gather.45
  564.2 8.6 fusion.449
  576.6 20.3 %psum.249 = f32[128]{0:T(128)} all-reduce(f32[128]{0:T(128)} %add.1050), channel_id=1, replica_groups=mesh['img'=8,'ch'=4] {'img'}, use_global_device_ids=true, to_apply=%region_28.29 | all-reduce | flops 128 | bytes 1024 | tf_op jit(solution)/shard_map/psum | solution.py:164
  600.2 17.7 psum.250
  637.1 19.7 %psum.251 = f32[512]{0:T(512)} all-reduce(f32[512]{0:T(512)S(1)} %add.1063), channel_id=1, replica_groups=mesh['img'=8,'ch'=4] {'img'}, use_global_device_ids=true, to_apply=%region_34.35 | all-reduce | flops 512 | bytes 4096 | tf_op jit(solution)/shard_map/psum | solution.py:164
  663.6 17.7 psum.253
  686.3 20.0 %all-reduce.14 = (f32[512]{0:T(512)}, f32[512]{0:T(512)}) all-reduce(f32[512]{0:T(512)} %add.1070, f32[512]{0:T(512)} %add.1064), channel_id=1, replica_groups=mesh['img'=8,'ch'=4] {'img'}, use_global_device_ids=true, to_apply=%region_43.44 | all-reduce | flops 1024 | bytes 8192 | tf_op jit(solution)/shard_map/psum | solution.py:167
  717.2 17.8 all-reduce.13
  776.0 17.6 reduce-scatter.37.cloned.1.call-done
  804.1 22.1 %all-reduce.12 = (f32[128]{0:T(128)}, f32[128]{0:T(128)}) all-reduce(f32[128]{0:T(128)} %add.1093, f32[128]{0:T(128)} %add.1091), channel_id=1, replica_groups=mesh['img'=8,'ch'=4] {'img'}, use_global_device_ids=true, to_apply=%region_57.58 | all-reduce | flops 256 | bytes 2048 | tf_op jit(solution)/shard_map/psum | solution.py:179
  838.3 26.2 %copy.298 = bf16[8,10,10,512]{2,1,0,3:T(8,128)(2,1)} copy(bf16[8,10,10,512]{3,0,2,1:T(8,128)(2,1)} %slice.1962) | data formatting | bytes 1638400
  864.5 18.6 %reshape.1890 = bf16[512,800]{1,0:T(8,128)(2,1)} reshape(bf16[512,8,10,10]{3,2,1,0:T(8,128)(2,1)} %bitcast.1073) | data formatting | bytes 1638400
  904.2 26.6 %copy.296 = bf16[8,14,14,512]{2,1,0,3:T(8,128)(2,1)} copy(bf16[8,14,14,512]{3,0,2,1:T(8,128)(2,1)} %slice.1954) | data formatting | bytes 3211264
  930.8 20.2 %reshape.1888 = bf16[512,1568]{1,0:T(8,128)(2,1)} reshape(bf16[512,8,14,14]{3,2,1,0:T(8,128)(2,1)} %bitcast.1074) | data formatting | bytes 3211264
  967.2 9.1 reduce-scatter.41.cloned.1.call-done
  995.4 22.2 %all-reduce.11 = (f32[128]{0:T(128)}, f32[128]{0:T(128)}, f32[512]{0:T(512)}) all-reduce(f32[128]{0:T(128)} %add.1115, f32[128]{0:T(128)} %add.1113, f32[512]{0:T(512)} %add.1117), channel_id=1, replica_groups=mesh['img'=8,'ch'=4] {'img'}, use_global_device_ids=true, to_apply=%region_65.66 | all-reduce | flops 768 | bytes 6144 | tf_op jit(solution)/shard_map/psum | solution.py:179
  1047.9 8.8 reduce-scatter.31.cloned.1.call-done
  1060.6 40.1 %reduce-scatter.29.cloned.1.call-done = bf16[8,14,14,256]{3,2,1,0:T(8,128)(2,1)} async-done(((bf16[8,14,14,1024]{3,2,1,0:T(8,128)(2,1)}), bf16[8,14,14,256]{3,2,1,0:T(8,128)(2,1)}) %reduce-scatter.29.cloned.1.call-update) | async-done | bytes 802832 | tf_op jit(solution)/shard_map/reduce_scatter | solution.py:132
  1105.2 21.5 %all-reduce.10 = (f32[256]{0:T(256)S(1)}, f32[256]{0:T(256)S(1)}) all-reduce(f32[256]{0:T(256)S(1)} %add.1126, f32[256]{0:T(256)S(1)} %add.1124), channel_id=1, replica_groups=mesh['img'=8,'ch'=4] {'img'}, use_global_device_ids=true, to_apply=%region_76.77 | all-reduce | flops 512 | bytes 4096 | tf_op jit(solution)/shard_map/psum | solution.py:179
  1130.9 13.0 copy.302
  1143.9 10.0 reshape.1894
  1158.0 12.7 copy.300
  1170.8 10.9 reshape.1892
  1211.4 21.7 %all-reduce.9 = (f32[64]{0:T(128)S(1)}, f32[64]{0:T(128)S(1)}) all-reduce(f32[64]{0:T(128)S(1)} %add.1132, f32[64]{0:T(128)S(1)} %add.1130), channel_id=1, replica_groups=mesh['img'=8,'ch'=4] {'img'}, use_global_device_ids=true, to_apply=%region_84.85 | all-reduce | flops 128 | bytes 1024 | tf_op jit(solution)/shard_map/psum | solution.py:179
  1360.6 13.1 copy.306
  1373.6 10.2 reshape.1898
  1408.5 13.5 copy.304
  1422.0 10.9 reshape.1896
  1462.6 21.4 %all-reduce.8 = (f32[64]{0:T(128)S(1)}, f32[64]{0:T(128)S(1)}) all-reduce(f32[64]{0:T(128)S(1)} %add.1154, f32[64]{0:T(128)S(1)} %add.1152), channel_id=1, replica_groups=mesh['img'=8,'ch'=4] {'img'}, use_global_device_ids=true, to_apply=%region_93.94 | all-reduce | flops 128 | bytes 1024 | tf_op jit(solution)/shard_map/psum | solution.py:179
  1526.1 35.5 %reduce-scatter.33.cloned.1.call-done = bf16[8,14,14,256]{3,2,1,0:T(8,128)(2,1)} async-done(((bf16[8,14,14,1024]{3,2,1,0:T(8,128)(2,1)}), bf16[8,14,14,256]{3,2,1,0:T(8,128)(2,1)}) %reduce-scatter.33.cloned.1.call-update) | async-done | bytes 802832 | tf_op jit(solution)/shard_map/reduce_scatter | solution.py:132
  1565.5 243.5 %all-reduce.18.cloned.1.call-done = (f32[1024,64]{0,1:T(8,128)}, f32[3,3,256,64]{2,3,1,0:T(8,128)}, f32[256,256]{1,0:T(8,128)}, f32[1024,128]{1,0:T(8,128)}, f32...) async-done(((f32[1024,64]{0,1:T(8,128)}, f32[3,3,256,64]{2,3,1,0:T(8,128)}, f32[256,256]{1,0:T(8,128)}, f32[1024,128]{1,0:T(8,128)}, ...) | async-done | bytes 7143440 | tf_op jit(solution)/shard_map/psum | solution.py:307
  (680 shorter events, 592.7 us)
Async XLA Ops:
  7.2 650.4 %copy-start = (bf16[1024,512]{1,0:T(8,128)(2,1)S(1)}, bf16[1024,512]{1,0:T(8,128)(2,1)}, u32[]{:S(2)}) copy-start(bf16[1024,512]{1,0:T(8,128)(2,1)} %param.107) | copy-start | bytes 3145732
  7.2 31.6 %all-gather.8.cloned.1.call-start = ((), (), s32[]{:S(2)}) async-start(), calls=%async_computation.13 | async-start | bytes 3276800 | tf_op jit(solution)/shard_map/all_gather | solution.py:126
  9.3 29.4 %copy-start.102 = (bf16[1024,64]{0,1:T(8,128)(2,1)S(1)}, bf16[1024,64]{0,1:T(8,128)(2,1)}, u32[]{:S(2)}) copy-start(bf16[1024,64]{0,1:T(8,128)(2,1)} %param.101) | copy-start | bytes 393220
  9.4 63.6 %all-gather.6.cloned.1.call-start = ((), (), s32[]{:S(2)}) async-start(), calls=%async_computation.12 | async-start | bytes 4587520 | tf_op jit(solution)/shard_map/all_gather | solution.py:125
  10.6 433.4 %all-gather.12.cloned.1.call-start = ((), (), s32[]{:S(2)}) async-start(), calls=%async_computation.15 | async-start | bytes 3276800 | tf_op jit(solution)/shard_map/all_gather | solution.py:126
  14.5 102.3 %copy-start.135 = (f32[64]{0:T(128)}, f32[64]{0:T(128)S(1)}, u32[]{:S(2)}) copy-start(f32[64]{0:T(128)S(1)} %get-tuple-element.645) | copy-start | bytes 772
  14.5 102.3 %copy-start.137 = (f32[64]{0:T(128)}, f32[64]{0:T(128)S(1)}, u32[]{:S(2)}) copy-start(f32[64]{0:T(128)S(1)} %get-tuple-element.678) | copy-start | bytes 772
  14.5 257.4 %copy-start.122 = (f32[64]{0:T(128)}, f32[64]{0:T(128)S(1)}, u32[]{:S(2)}) copy-start(f32[64]{0:T(128)S(1)} %get-tuple-element.644) | copy-start | bytes 772
  14.5 257.4 %copy-start.124 = (f32[64]{0:T(128)}, f32[64]{0:T(128)S(1)}, u32[]{:S(2)}) copy-start(f32[64]{0:T(128)S(1)} %get-tuple-element.679) | copy-start | bytes 772
  41.4 74.4 %copy-start.25 = (f32[8,10,10,64]{3,2,1,0:T(8,128)}, f32[8,10,10,64]{3,2,1,0:T(8,128)S(1)}, u32[]{:S(2)}) copy-start(f32[8,10,10,64]{3,2,1,0:T(8,128)S(1)} %get-tuple-element.655) | copy-start | bytes 614404
  76.1 41.9 %copy-start.21 = (f32[8,14,14,64]{3,2,1,0:T(8,128)}, f32[8,14,14,64]{3,2,1,0:T(8,128)S(1)}, u32[]{:S(2)}) copy-start(f32[8,14,14,64]{3,2,1,0:T(8,128)S(1)} %get-tuple-element.653) | copy-start | bytes 1204228
  97.5 19.3 %copy-start.126 = (f32[64]{0:T(128)}, f32[64]{0:T(128)S(1)}, u32[]{:S(2)}) copy-start(f32[64]{0:T(128)S(1)} %broadcast_divide_fusion.6) | copy-start | bytes 772
  164.5 1031.5 %copy-start.19 = (f32[8,10,10,64]{3,2,1,0:T(8,128)}, f32[8,10,10,64]{3,2,1,0:T(8,128)S(1)}, u32[]{:S(2)}) copy-start(f32[8,10,10,64]{3,2,1,0:T(8,128)S(1)} %get-tuple-element.659) | copy-start | bytes 614404
  233.5 39.6 %copy-start.11 = (f32[8,14,14,64]{3,2,1,0:T(8,128)}, f32[8,14,14,64]{3,2,1,0:T(8,128)S(1)}, u32[]{:S(2)}) copy-start(f32[8,14,14,64]{3,2,1,0:T(8,128)S(1)} %get-tuple-element.657) | copy-start | bytes 1204228
  252.7 20.5 %copy-start.114 = (f32[64]{0:T(128)}, f32[64]{0:T(128)S(1)}, u32[]{:S(2)}) copy-start(f32[64]{0:T(128)S(1)} %broadcast_divide_fusion.5) | copy-start | bytes 772
  420.3 57.7 %all-gather.10.cloned.1.call-start = ((), (), s32[]{:S(2)}) async-start(), calls=%async_computation.14 | async-start | bytes 4587520 | tf_op jit(solution)/shard_map/all_gather | solution.py:125
  423.3 133.2 %all-gather.14.cloned.1.call-start = ((), (), s32[]{:S(2)}) async-start(), calls=%async_computation.16 | async-start | bytes 2293760 | tf_op jit(solution)/shard_map/all_gather | solution.py:125
  505.2 26.9 %copy-start.116 = (f32[128]{0:T(128)}, f32[128]{0:T(128)S(1)}, u32[]{:S(2)}) copy-start(f32[128]{0:T(128)S(1)} %broadcast_divide_fusion.4) | copy-start | bytes 1540
  532.1 237.5 %reduce-scatter.39.cloned.1.call-start = ((), (), s32[]{:S(2)}) async-start(), calls=%async_computation.22 | async-start | bytes 327680
  597.6 39.5 %copy-start.113 = (f32[128]{0:T(128)}, f32[128]{0:T(128)S(1)}, u32[]{:S(2)}) copy-start(f32[128]{0:T(128)S(1)} %broadcast_divide_fusion.3) | copy-start | bytes 1540
  617.9 17.9 copy-start.30
  626.9 10.1 copy-start.101
  749.9 43.8 %reduce-scatter.37.cloned.1.call-start = ((), (), s32[]{:S(2)}) async-start(), calls=%async_computation.21 | async-start | bytes 655360
  769.6 182.7 %reduce-scatter.43.cloned.1.call-start = ((), (), s32[]{:S(2)}) async-start(), calls=%async_computation.24 | async-start | bytes 1146880
  883.1 93.3 %reduce-scatter.41.cloned.1.call-start = ((), (), s32[]{:S(2)}) async-start(), calls=%async_computation.23 | async-start | bytes 2129920
  951.0 105.7 %reduce-scatter.31.cloned.1.call-start = ((), (), s32[]{:S(2)}) async-start(), calls=%async_computation.18 | async-start | bytes 3276800 | tf_op jit(solution)/shard_map/reduce_scatter | solution.py:135
  1025.5 75.2 %reduce-scatter.29.cloned.1.call-start = ((), (), s32[]{:S(2)}) async-start(), calls=%async_computation.17 | async-start | bytes 4587520 | tf_op jit(solution)/shard_map/reduce_scatter | solution.py:132
  1035.3 153.4 %reduce-scatter.47.cloned.1.call-start = ((), (), s32[]{:S(2)}) async-start(), calls=%async_computation.26 | async-start | bytes 573440
  1046.8 9.9 copy-start.132
  1060.6 66.0 %copy-start.139 = (f32[256]{0:T(256)S(1)}, f32[256]{0:T(256)}, u32[]{:S(2)}) copy-start(f32[256]{0:T(256)} %get-tuple-element.609) | copy-start | bytes 3076
  1105.1 24.5 %copy-start.65 = (bf16[256,256]{1,0:T(8,128)(2,1)S(1)}, bf16[256,256]{1,0:T(8,128)(2,1)}, u32[]{:S(2)}) copy-start(bf16[256,256]{1,0:T(8,128)(2,1)} %param.103) | copy-start | bytes 393220
  1126.7 29.4 %copy-start.145 = (f32[256]{0:T(256)}, f32[256]{0:T(256)S(1)}, u32[]{:S(2)}) copy-start(f32[256]{0:T(256)S(1)} %get-tuple-element.695) | copy-start | bytes 3076
  1126.7 29.4 %copy-start.146 = (f32[256]{0:T(256)}, f32[256]{0:T(256)S(1)}, u32[]{:S(2)}) copy-start(f32[256]{0:T(256)S(1)} %get-tuple-element.696) | copy-start | bytes 3076
  1154.0 47.8 %reduce-scatter.45.cloned.1.call-start = ((), (), s32[]{:S(2)}) async-start(), calls=%async_computation.25 | async-start | bytes 1064960
  1181.7 261.9 %reduce-scatter.51.cloned.1.call-start = ((), (), s32[]{:S(2)}) async-start(), calls=%async_computation.28 | async-start | bytes 573440
  1196.0 14.3 copy-start.54
  1206.7 26.3 %copy-start.142 = (f32[64]{0:T(128)S(1)}, f32[64]{0:T(128)}, u32[]{:S(2)}) copy-start(f32[64]{0:T(128)} %get-tuple-element.607) | copy-start | bytes 772
  1210.4 23.6 %copy-start.20 = (f32[8,10,10,64]{3,2,1,0:T(8,128)S(1)}, f32[8,10,10,64]{3,2,1,0:T(8,128)}, u32[]{:S(2)}) copy-start(f32[8,10,10,64]{3,2,1,0:T(8,128)} %copy-done.19) | copy-start | bytes 614404
  1211.3 23.4 %copy-start.47 = (bf16[3,3,256,64]{2,3,1,0:T(8,128)(2,1)S(1)}, bf16[3,3,256,64]{2,3,1,0:T(8,128)(2,1)}, u32[]{:S(2)}) copy-start(bf16[3,3,256,64]{2,3,1,0:T(8,128)(2,1)} %param.102) | copy-start | bytes 884740
  1234.0 165.5 %copy-start.6 = (bf16[8,14,14,64]{3,2,1,0:T(8,128)(2,1)}, bf16[8,14,14,64]{3,2,1,0:T(8,128)(2,1)S(1)}, u32[]{:S(2)}) copy-start(bf16[8,14,14,64]{3,2,1,0:T(8,128)(2,1)S(1)} %multiply_convert_fusion.5) | copy-start | bytes 602116
  1383.9 69.2 %reduce-scatter.49.cloned.1.call-start = ((), (), s32[]{:S(2)}) async-start(), calls=%async_computation.27 | async-start | bytes 1064960
  1432.9 90.5 %reduce-scatter.35.cloned.1.call-start = ((), (), s32[]{:S(2)}) async-start(), calls=%async_computation.20 | async-start | bytes 3276800 | tf_op jit(solution)/shard_map/reduce_scatter | solution.py:135
  1451.3 32.6 %copy-start.92 = (bf16[8,10,10,64]{3,2,1,0:T(8,128)(2,1)}, bf16[8,10,10,64]{3,2,1,0:T(8,128)(2,1)S(1)}, u32[]{:S(2)}) copy-start(bf16[8,10,10,64]{3,2,1,0:T(8,128)(2,1)S(1)} %copy.307) | copy-start | bytes 307204
  1457.9 26.0 %copy-start.103 = (bf16[1024,64]{0,1:T(8,128)(2,1)S(1)}, bf16[1024,64]{0,1:T(8,128)(2,1)}, u32[]{:S(2)}) copy-start(bf16[1024,64]{0,1:T(8,128)(2,1)} %param.101) | copy-start | bytes 393220
  1457.9 26.0 %copy-start.151 = (f32[64]{0:T(128)S(1)}, f32[64]{0:T(128)}, u32[]{:S(2)}) copy-start(f32[64]{0:T(128)} %get-tuple-element.605) | copy-start | bytes 772
  1486.7 74.9 %reduce-scatter.33.cloned.1.call-start = ((), (), s32[]{:S(2)}) async-start(), calls=%async_computation.19 | async-start | bytes 4587520 | tf_op jit(solution)/shard_map/reduce_scatter | solution.py:132
  1499.9 309.2 %all-reduce.18.cloned.1.call-start = ((), (), s32[]{:S(2)}) async-start(), calls=%async_computation.29 | async-start | bytes 14286848 | tf_op jit(solution)/shard_map/psum | solution.py:307
  1524.7 37.0 %copy-start.18 = (f32[8,14,14,256]{3,2,1,0:T(8,128)S(1)}, f32[8,14,14,256]{3,2,1,0:T(8,128)}, u32[]{:S(2)}) copy-start(f32[8,14,14,256]{3,2,1,0:T(8,128)} %get-tuple-element.612) | copy-start | bytes 4816900
  (124 other events, 409.7 us)
Sparse Core Ops, SparseCore 0:
  10.2 28.5 all-gather.7
  40.9 31.9 all-gather.5
  420.4 23.5 all-gather.11
  445.9 31.9 all-gather.9
  532.3 21.6 all-gather.13
  750.0 18.7 reduce-scatter.38
  771.9 21.6 reduce-scatter.36
  883.2 20.3 reduce-scatter.42
  951.1 25.1 reduce-scatter.40
  1025.6 31.0 reduce-scatter.30
  1059.4 41.2 reduce-scatter.28
  1154.1 17.5 reduce-scatter.46
  1181.8 19.9 reduce-scatter.44
  1384.0 17.5 reduce-scatter.50
  1433.0 19.9 reduce-scatter.48
  1486.8 30.9 reduce-scatter.34
  1520.4 41.2 reduce-scatter.32
  1568.2 240.8 all-reduce.17
where the time goes:
time: 1840 us; the launch traced here: 1830 us
  blocking collectives  572 us (31%)
  local copies, waits for them, and re-layouts  504 us (27%)
  waiting for transfers between devices  462 us (25%)
  matrix products  163 us (9%)
  other arithmetic  108 us (6%)
    unnamed x353, local copies, waits for them, and re-layouts  316 us
    psum x1, waiting for transfers between devices, per_device(): lax.psum((grad_reduce, grad_mix, grad_expand, grad_narrow, grad_stride, g...  244 us
    psum x7, blocking collectives, norm_forward(): first = lax.psum(live_sum(pre, lives), 'img')  140 us
    psum x6, blocking collectives, norm_backward(): sum_grad, sum_hat = lax.psum((sum_grad, sum_hat), 'img')  127 us
    all_gather x3, blocking collectives, gather_pair(): lax.all_gather(pair[0], 'ch', axis=3, tiled=True)  108 us
    psum x6, blocking collectives, norm_forward(): lax.psum(live_sum([devs[0] * devs[0], devs[1] * devs[1]], lives), 'img')  108 us
    scatter-add x18, local copies, waits for them, and re-layouts, taps_input(): grad_pad = grad_pad.at[:, row_tap:row_tap + height, col_tap:col_tap + wid...  106 us
    all_gather x4, blocking collectives, gather_pair(): lax.all_gather(pair[1], 'ch', axis=3, tiled=True)  89.9 us
  transfers between devices with their start and end apart: 18, of which 12 were waited for; matrix products, arithmetic and copies ran while one was open for 17% of the time, Pallas kernels for 0%

commit v1 on v0

v1 whole, which is shorter than its diff:
```python
import functools

import jax
import jax.numpy as jnp
from jax import lax
from jax.experimental import pallas as pl
from jax.experimental.pallas import tpu as pltpu
from jax.sharding import PartitionSpec as P

EPS = 1e-05
G0 = 0.7978845608028654
G1 = G0 * 0.044715
F32 = jnp.float32
BF16 = jnp.bfloat16
VIEWS = 8

ANY = pl.BlockSpec(memory_space=pl.ANY)
VMEM = pl.BlockSpec(memory_space=pltpu.VMEM)
SMEM = pl.BlockSpec(memory_space=pltpu.SMEM)


def sds(shape, dtype=F32):
    return jax.ShapeDtypeStruct(tuple(shape), dtype)


def call(name, kernel, ins, outs, scratch=(), limit=48, cost=None):
    outs = [o if isinstance(o, tuple) else (o, VMEM) for o in outs]
    result = pl.pallas_call(
        kernel,
        out_shape=[o[0] for o in outs],
        in_specs=[spec for _, spec in ins],
        out_specs=[o[1] for o in outs],
        scratch_shapes=list(scratch),
        compiler_params=pltpu.CompilerParams(vmem_limit_bytes=limit << 20),
        cost_estimate=cost,
        name=name,
    )(*[array for array, _ in ins])
    return result


def vm(*arrays):
    return [(a, VMEM) for a in arrays]


def nn(a, b):
    return lax.dot_general(a, b, (((1,), (0,)), ((), ())), preferred_element_type=F32)


def nt(a, b):
    return lax.dot_general(a, b, (((1,), (1,)), ((), ())), preferred_element_type=F32)


def tn(a, b):
    return lax.dot_general(a, b, (((0,), (0,)), ((), ())), preferred_element_type=F32)


def gelu(t):
    half = 0.5 * t
    return half + half * jnp.tanh(t * (G0 + G1 * (t * t)))


def gelu_slope(t):
    sq = t * t
    th = jnp.tanh(t * (G0 + G1 * sq))
    return 0.5 * (1.0 + th) + (0.5 * t) * (1.0 - th * th) * (G0 + (3.0 * G1) * sq)


def live_rows(count, chans):
    return (lax.broadcasted_iota(jnp.int32, (VIEWS, chans), 0) < count).astype(F32)


def rows_sum(v):
    return jnp.sum(v, axis=0, keepdims=True)


def merged(sa, sb, na, nb):
    total = na + nb
    mean = (na * sa[0:1] + nb * sb[0:1]) / total
    diff = sb[0:1] - sa[0:1]
    square = sa[1:2] + sb[1:2] + diff * diff * (na * nb / total)
    return mean, lax.rsqrt(square / total + EPS)


def as_rows(v):
    return v.reshape(v.shape[0] * v.shape[1], v.shape[2])


def as_pix(v):
    return v.reshape(v.shape[0] // VIEWS, VIEWS, v.shape[1])


class Geo:
    def __init__(self, hb, hs):
        self.hb, self.hs = hb, hs
        self.pb, self.ps = hb * hb, hs * hs
        self.px = self.pb + self.ps
        self.rows = self.px * VIEWS
        self.qb, self.qs = self.pb // 4, self.ps // 4
        self.px4 = self.qb + self.qs
        self.rows4 = self.px4 * VIEWS
        self.parts = ((hb, 0), (hs, self.pb))

    def loop(self, body, carries):
        out = []
        for part, (side, start) in enumerate(self.parts):
            step = 2 * side

            def run(i, carry, part=part, start=start, step=step):
                pix = start + i * step
                row = pl.multiple_of(start * VIEWS + i * (step * VIEWS), 16)
                return body(part, i, pix, step, row, step * VIEWS, carry)

            out.append(lax.fori_loop(0, side // 2, run, carries[part]))
        return out


def finish_stats(geo, ref, sums, lives, count, out, quarter=None):
    mean = (rows_sum(sums[0] * lives[0]) + rows_sum(sums[1] * lives[1])) / count

    def body(part, i, pix, npx, row, nrows, carry):
        dev = ref[pl.ds(pix, npx)] - mean
        return carry + jnp.sum(dev * dev, axis=0)

    zero = jnp.zeros(sums[0].shape, F32)
    sq = geo.loop(body, [zero, zero])
    out[0:1] = mean
    out[1:2] = rows_sum(sq[0] * lives[0]) + rows_sum(sq[1] * lives[1])


def block_stats(geo, value, lives, count):
    big, small = value[: geo.qb], value[geo.qb :]
    mean = (
        rows_sum(jnp.sum(big, axis=0) * lives[0]) + rows_sum(jnp.sum(small, axis=0) * lives[1])
    ) / count
    db, ds = big - mean, small - mean
    square = rows_sum(jnp.sum(db * db, axis=0) * lives[0]) + rows_sum(
        jnp.sum(ds * ds, axis=0) * lives[1]
    )
    return mean, square


def k_assemble(plan, me, *refs):
    n = len(plan)
    pieces, outs, sem = refs[: 4 * n], refs[4 * n : 5 * n], refs[5 * n]
    copies = []
    for w, (kind, size) in enumerate(plan):
        for p in range(4):
            src = pieces[4 * w + p]
            at = pl.ds(pl.multiple_of((me[0] ^ p) * size, size), size)
            if kind == "cols":
                dsts = [(src, outs[w].at[:, at])]
            elif kind == "rows":
                dsts = [(src, outs[w].at[at, :])]
            elif kind == "taps_nt":
                dsts = [
                    (src.at[t], outs[w].at[t // 3, at, pl.ds((t % 3) * 256, 256)])
                    for t in range(9)
                ]
            else:
                dsts = [(src.at[t], outs[w].at[t, at, :]) for t in range(9)]
            for a, b in dsts:
                copies.append(pltpu.make_async_copy(a, b, sem.at[len(copies)]))
                copies[-1].start()
    for c in copies:
        c.wait()


def assemble(name, me, items):
    plan = [(kind, size) for _, kind, size, _ in items]
    ncopies = sum(36 if k.startswith("taps") else 4 for k, _ in plan)
    ins = [(me, SMEM)] + [(p, ANY) for pieces, _, _, _ in items for p in pieces]
    return call(
        name,
        functools.partial(k_assemble, plan),
        ins,
        [(sds(shape, BF16), ANY) for _, _, _, shape in items],
        [pltpu.SemaphoreType.DMA((ncopies,))],
        limit=4,
    )


def k_reduce(geo, me, nf, x0b, x1b, x2b, x3b, x0s, x1s, x2s, x3s, wt, pre, xs, stats, wx):
    xb, xsm = (x0b, x1b, x2b, x3b), (x0s, x1s, x2s, x3s)
    q = me[0]
    for p in range(4):
        wx[p] = wt[:, pl.ds(pl.multiple_of((q ^ p) * 256, 256), 256)]
    chans = wt.shape[0]
    lives = [live_rows(me[1], chans), live_rows(me[2], chans)]

    def body(part, i, pix, npx, row, nrows, carry):
        src = (xb, xsm)[part]
        local = pl.multiple_of(i * nrows, 16)
        acc = None
        for p in range(4):
            v = src[p][pl.ds(local, nrows), :]
            xs[q ^ p, pl.ds(row, nrows), :] = v
            d = nt(v, wx[p])
            acc = d if acc is None else acc + d
        z = as_pix(acc)
        pre[pl.ds(pix, npx)] = z
        return carry + jnp.sum(z, axis=0)

    zero = jnp.zeros((VIEWS, chans), F32)
    sums = geo.loop(body, [zero, zero])
    finish_stats(geo, pre, sums, lives, nf[0], stats)


def side_shift(v, by):
    zero = jnp.zeros((v.shape[0], 1) + v.shape[2:], v.dtype)
    if by > 0:
        return jnp.concatenate([zero, v[:, :-1]], axis=1)
    return jnp.concatenate([v[:, 1:], zero], axis=1)


def store_shifted(buf, row, nrows, side, v, order):
    img = v.reshape(2, side, VIEWS, v.shape[-1])
    chans = v.shape[-1]
    forms = [side_shift(img, 1), img, side_shift(img, -1)]
    for lane, k in enumerate(order):
        flat = forms[k].reshape(nrows, chans).astype(BF16)
        buf[pl.ds(row, nrows), lane * chans : (lane + 1) * chans] = flat


def put_phases(ref, i, v):
    for k in range(4):
        ref[k // 2, k % 2, i] = v[k // 2, :, k % 2]


def get_phases(ref, i):
    rows = [jnp.stack([ref[r, 0, i], ref[r, 1, i]], axis=1) for r in range(2)]
    return jnp.stack(rows)


def zero_edges(buf, edge):
    total = buf.shape[0]
    buf[0:edge, :] = jnp.zeros((edge, buf.shape[1]), BF16)
    buf[total - edge : total, :] = jnp.zeros((edge, buf.shape[1]), BF16)


def k_mix(geo, me, nf, pre1, sa, sb, gs, w, pre2, wb, ws, stats):
    chans = pre1.shape[-1]
    lives = [live_rows(me[1], chans), live_rows(me[2], chans)]
    mean, inv = merged(sa[...], sb[...], nf[1], nf[2])
    scale, shift = gs[0:1] * inv, gs[1:2]
    bufs = (wb, ws)
    for part, (side, _) in enumerate(geo.parts):
        zero_edges(bufs[part], side * VIEWS)

    def act(part, i, pix, npx, row, nrows, carry):
        a = gelu((pre1[pl.ds(pix, npx)] - mean) * scale + shift)
        side = geo.parts[part][0]
        at = pl.multiple_of(side * VIEWS + i * nrows, 16)
        store_shifted(bufs[part], at, nrows, side, a, (0, 1, 2))
        return carry

    geo.loop(act, [0, 0])

    def dots(part, i, pix, npx, row, nrows, carry):
        acc = None
        for r in range(3):
            at = pl.multiple_of(i * nrows + r * (nrows // 2), 16)
            d = nt(bufs[part][pl.ds(at, nrows), :], w[r])
            acc = d if acc is None else acc + d
        z = as_pix(acc)
        pre2[pl.ds(pix, npx)] = z
        return carry + jnp.sum(z, axis=0)

    zero = jnp.zeros((VIEWS, chans), F32)
    sums = geo.loop(dots, [zero, zero])
    finish_stats(geo, pre2, sums, lives, nf[0], stats)


def k_expand(geo, me, nf, pre2, sa, sb, gs, w, pre3, act2, stats):
    chans = w.shape[1]
    lives = [live_rows(me[1], chans), live_rows(me[2], chans)]
    mean, inv = merged(sa[...], sb[...], nf[1], nf[2])
    scale, shift = gs[0:1] * inv, gs[1:2]

    def body(part, i, pix, npx, row, nrows, carry):
        a = as_rows(gelu((pre2[pl.ds(pix, npx)] - mean) * scale + shift)).astype(BF16)
        act2[pl.ds(row, nrows), :] = a
        z = as_pix(nn(a, w[...]))
        pre3[pl.ds(pix, npx)] = z
        return carry + jnp.sum(z, axis=0)

    zero = jnp.zeros((VIEWS, chans), F32)
    sums = geo.loop(body, [zero, zero])
    finish_stats(geo, pre3, sums, lives, nf[0], stats)


def k_narrow(geo, me, nf, pre3, xs, sa, sb, gs, w, pre4b, pre4s, mid, mids, stats, mid_even):
    chans = w.shape[1]
    lives = [live_rows(me[1], chans), live_rows(me[2], chans)]
    mean, inv = merged(sa[...], sb[...], nf[1], nf[2])
    scale, shift = gs[0:1] * inv, gs[1:2]
    pre4 = (pre4b, pre4s)

    def body(part, i, pix, npx, row, nrows, carry):
        side = geo.parts[part][0]
        half = side // 2
        for j in range(4):
            at = slice(256 * j, 256 * j + 256)
            dev = pre3[pl.ds(pix, npx), :, at] - mean[:, at]
            x = as_pix(xs[j, pl.ds(row, nrows), :].astype(F32))
            a = gelu(dev * scale[:, at] + shift[:, at] + x)
            mid[pl.ds(row, nrows), at] = as_rows(a).astype(BF16)
            even = a.reshape(2, half, 2, VIEWS, 256)[0, :, 0]
            mid_even[pl.ds((0, geo.qb)[part] + half * i, half), :, at] = even
        z = nn(mid[pl.ds(row, nrows), :], w[...])
        put_phases(pre4[part], i, z.reshape(2, half, 2, VIEWS, chans))
        return carry + jnp.sum(as_pix(z), axis=0)

    zero = jnp.zeros((VIEWS, chans), F32)
    sums = geo.loop(body, [zero, zero])
    mean4 = (rows_sum(sums[0] * lives[0]) + rows_sum(sums[1] * lives[1])) / nf[0]
    mids[...] = as_rows(mid_even[...]).astype(BF16)
    sq = []
    for part in range(2):

        def dev2(i, carry, part=part):
            for k in range(4):
                d = pre4[part][k // 2, k % 2, i] - mean4
                carry = carry + jnp.sum(d * d, axis=0)
            return carry

        sq.append(lax.fori_loop(0, geo.parts[part][0] // 2, dev2, zero))
    stats[0:1] = mean4
    stats[1:2] = rows_sum(sq[0] * lives[0]) + rows_sum(sq[1] * lives[1])


def k_short(geo, me, nf, mids, w0, w1, w2, w3, side, stats):
    chans = w0.shape[1]
    lives = [live_rows(me[1], chans), live_rows(me[2], chans)]
    for p, w in enumerate((w0, w1, w2, w3)):
        j = me[0] ^ p
        z = as_pix(nn(mids[...], w[...]))
        side[j] = z
        mean, square = block_stats(geo, z, lives, nf[0])
        stats[j] = jnp.concatenate([mean, square], axis=0)


def k_stride(geo, me, nf, n4, pre4b, pre4s, sa, sb, gs, w, pre5, cols, stats, sb_act, ss_act):
    chans = pre4b.shape[-1]
    lives = [live_rows(me[1], chans), live_rows(me[2], chans)]
    mean, inv = merged(sa[...], sb[...], n4[1], n4[2])
    scale, shift = gs[0:1] * inv, gs[1:2]
    srcs, dsts = (pre4b, pre4s), (sb_act, ss_act)
    for part in range(2):

        def act(i, carry, part=part):
            for k in range(4):
                at = (k // 2, k % 2, i)
                dsts[part][at] = gelu((srcs[part][at] - mean) * scale + shift)
            return carry

        lax.fori_loop(0, geo.parts[part][0] // 2, act, 0)
    for r in range(3):
        for c in range(3):
            flats = []
            for part in range(2):
                half = geo.parts[part][0] // 2
                v = dsts[part][(r + 1) % 2, (c + 1) % 2]
                if c == 0:
                    v = side_shift(v, 1)
                if r == 0:
                    v = jnp.concatenate([jnp.zeros((1,) + v.shape[1:], F32), v[:-1]], axis=0)
                flats.append(v.reshape(half * half * VIEWS, chans))
            t = 3 * r + c
            cols[:, t * chans : (t + 1) * chans] = jnp.concatenate(flats, axis=0).astype(BF16)
    z = as_pix(nn(cols[...], w[...]))
    pre5[...] = z
    m5, s5 = block_stats(geo, z, lives, nf[0])
    stats[0:1] = m5
    stats[1:2] = s5


def k_widen(geo, me, nf, pre5, sa, sb, gs, w0, w1, w2, w3, pre6, act5, stats):
    chans = w0.shape[1]
    lives = [live_rows(me[1], chans), live_rows(me[2], chans)]
    mean, inv = merged(sa[...], sb[...], nf[1], nf[2])
    scale, shift = gs[0:1] * inv, gs[1:2]
    act5[...] = as_rows(gelu((pre5[...] - mean) * scale + shift)).astype(BF16)
    for p, w in enumerate((w0, w1, w2, w3)):
        j = me[0] ^ p
        z = as_pix(nn(act5[...], w[...]))
        pre6[j] = z
        m6, s6 = block_stats(geo, z, lives, nf[0])
        stats[j] = jnp.concatenate([m6, s6], axis=0)


def k_total(geo, me, nf, pre6, side, sa, sb, gs, cb0, cb1, cb2, cb3, cs0, cs1, cs2, cs3, out_b, out_s, dt, sums):
    chans = pre6.shape[-1]
    lives = [live_rows(me[1], chans), live_rows(me[2], chans)]
    cots = ((cb0, cb1, cb2, cb3), (cs0, cs1, cs2, cs3))
    spans = ((0, geo.qb), (geo.qb, geo.px4))
    outs = (out_b, out_s)
    for p in range(4):
        j = me[0] ^ p
        a, b, g = sa[j], sb[j], gs[j]
        m6, r6 = merged(a[0:2], b[0:2], nf[1], nf[2])
        ms, rs = merged(a[2:4], b[2:4], nf[1], nf[2])
        acc = [None, None, None]
        for part, (lo, hi) in enumerate(spans):
            d6 = pre6[j, lo:hi] - m6
            dd = side[j, lo:hi] - ms
            total = d6 * (g[0:1] * r6) + g[1:2] + (dd * (g[2:3] * rs) + g[3:4])
            live = lives[part]
            if p == 0:
                outs[part][...] = gelu(total) * live
            grad = gelu_slope(total) * (as_pix(cots[part][p][...].astype(F32)) * live)
            dt[j, lo:hi] = grad
            terms = [jnp.sum(v, axis=0) for v in (grad, grad * d6, grad * dd)]
            acc = [t if s is None else s + t for s, t in zip(acc, terms)]
        sums[j] = jnp.concatenate(
            [rows_sum(acc[0]), rows_sum(acc[1]) * r6, rows_sum(acc[2]) * rs], axis=0
        )


def back_coefs(lives, s1, s2, inv, gain, count):
    c1 = gain * inv
    c2 = [live * (c1 * s1 / count) for live in lives]
    c3 = [live * (c1 * inv * s2 / count) for live in lives]
    return c1, c2, c3


def k_back_wide(geo, me, nf, dt, pre6, side, sa, sb, gs, ga, gb, pre5, sa5, sb5, gs5, w0, w1, w2, w3, dt5, dz6, dzs, sums5):
    chans = pre6.shape[-1]
    lives = [live_rows(me[1], chans), live_rows(me[2], chans)]
    total = nf[1] + nf[2]
    spans = ((0, geo.qb), (geo.qb, geo.px4))
    acc = None
    for p, w in enumerate((w0, w1, w2, w3)):
        j = me[0] ^ p
        a, b, g = sa[j], sb[j], gs[j]
        s = ga[j] + gb[j]
        m6, r6 = merged(a[0:2], b[0:2], nf[1], nf[2])
        ms, rs = merged(a[2:4], b[2:4], nf[1], nf[2])
        k1, k2, k3 = back_coefs(lives, s[0:1], s[1:2], r6, g[0:1], total)
        h1, h2, h3 = back_coefs(lives, s[0:1], s[2:3], rs, g[2:3], total)
        main, short = [], []
        for part, (lo, hi) in enumerate(spans):
            grad = dt[j, lo:hi]
            main.append(grad * k1 - k2[part] - (pre6[j, lo:hi] - m6) * k3[part])
            short.append(grad * h1 - h2[part] - (side[j, lo:hi] - ms) * h3[part])
        z6 = as_rows(jnp.concatenate(main, axis=0)).astype(BF16)
        dzs[j] = as_rows(jnp.concatenate(short, axis=0)).astype(BF16)
        if p == 0:
            dz6[...] = z6
        d = nt(z6, w[...])
        acc = d if acc is None else acc + d
    m5, r5 = merged(sa5[...], sb5[...], nf[1], nf[2])
    dev = pre5[...] - m5
    grad = gelu_slope(dev * (gs5[0:1] * r5) + gs5[1:2]) * as_pix(acc)
    dt5[...] = grad
    sums5[0:1] = rows_sum(jnp.sum(grad, axis=0))
    sums5[1:2] = rows_sum(jnp.sum(grad * dev, axis=0)) * r5


def k_back_short(geo, me, dzs, w0, w1, w2, w3, dms):
    acc = None
    for p, w in enumerate((w0, w1, w2, w3)):
        d = nt(dzs[me[0] ^ p], w[...])
        acc = d if acc is None else acc + d
    dms[...] = as_pix(acc)


def k_back_stride(geo, me, nf, dt5, pre5, sa5, sb5, gs5, ga, gb, pre4b, pre4s, sa4, sb4, gs4, n4, w, dt4b, dt4s, dz5, sums4, shifts):
    chans = pre5.shape[-1]
    lives = [live_rows(me[1], chans), live_rows(me[2], chans)]
    s = ga[...] + gb[...]
    m5, r5 = merged(sa5[...], sb5[...], nf[1], nf[2])
    c1, c2, c3 = back_coefs(lives, s[0:1], s[1:2], r5, gs5[0:1], nf[1] + nf[2])
    spans = ((0, geo.qb), (geo.qb, geo.px4))
    imgs = []
    for part, (lo, hi) in enumerate(spans):
        half = geo.parts[part][0] // 2
        z = dt5[lo:hi] * c1 - c2[part] - (pre5[lo:hi] - m5) * c3[part]
        imgs.append(z.reshape(half, half, VIEWS, chans))

    def flat(moved):
        return jnp.concatenate([v.reshape(-1, chans) for v in moved], axis=0).astype(BF16)

    def up(v):
        return jnp.concatenate([v[1:], jnp.zeros((1,) + v.shape[1:], F32)], axis=0)

    shifts[0] = flat(imgs)
    dz5[...] = shifts[0]
    shifts[1] = flat([side_shift(v, -1) for v in imgs])
    shifts[2] = flat([up(v) for v in imgs])
    shifts[3] = flat([up(side_shift(v, -1)) for v in imgs])
    m4, r4 = merged(sa4[...], sb4[...], n4[1], n4[2])
    scale, off = gs4[0:1] * r4, gs4[1:2]
    plan = {
        (0, 0): ((0, 4),),
        (0, 1): ((0, 5), (1, 3)),
        (1, 0): ((0, 7), (2, 1)),
        (1, 1): ((0, 8), (1, 6), (2, 2), (3, 0)),
    }
    t1, t2 = jnp.zeros((VIEWS, chans), F32), jnp.zeros((VIEWS, chans), F32)
    for (rp, cp), terms in plan.items():
        acc = None
        for k, t in terms:
            d = nt(shifts[k], w[t * chans : (t + 1) * chans, :])
            acc = d if acc is None else acc + d
        for part, (lo, hi) in enumerate(spans):
            half = geo.parts[part][0] // 2
            d = acc[lo * VIEWS : hi * VIEWS].reshape(half, half, VIEWS, chans)
            dev = (pre4b, pre4s)[part][rp, cp] - m4
            grad = gelu_slope(dev * scale + off) * d
            (dt4b, dt4s)[part][rp, cp] = grad
            t1 = t1 + jnp.sum(grad, axis=(0, 1))
            t2 = t2 + jnp.sum(grad * dev, axis=(0, 1))
    sums4[0:1] = rows_sum(t1)
    sums4[1:2] = rows_sum(t2) * r4


def k_back_narrow(geo, me, nf, dt4b, dt4s, pre4b, pre4s, sa4, sb4, gs4, ga, gb, pre3, xs, sa3, sb3, gs3, dms, w, dt3, dz4, sums3, db, ds):
    chans = w.shape[1]
    wide = w.shape[0]
    lives = [live_rows(me[1], chans), live_rows(me[2], chans)]
    s = ga[...] + gb[...]
    m4, r4 = merged(sa4[...], sb4[...], nf[1], nf[2])
    c1, c2, c3 = back_coefs(lives, s[0:1], s[1:2], r4, gs4[0:1], nf[1] + nf[2])
    m3, r3 = merged(sa3[...], sb3[...], nf[1], nf[2])
    scale, off = gs3[0:1] * r3, gs3[1:2]
    dts, pres, bufs = (dt4b, dt4s), (pre4b, pre4s), (db, ds)

    def body(part, i, pix, npx, row, nrows, carry):
        half = geo.parts[part][0] // 2
        dev4 = get_phases(pres[part], i) - m4
        z = get_phases(dts[part], i) * c1 - c2[part] - dev4 * c3[part]
        z = z.reshape(nrows, chans).astype(BF16)
        dz4[pl.ds(row, nrows), :] = z
        buf = bufs[part]
        buf[...] = nt(z, w[...]).reshape(buf.shape)
        buf[0, :, 0] += dms[pl.ds((0, geo.qb)[part] + half * i, half)]
        t1, t2 = [], []
        for j in range(4):
            at = slice(256 * j, 256 * j + 256)
            dev = pre3[pl.ds(pix, npx), :, at] - m3[:, at]
            x = as_pix(xs[j, pl.ds(row, nrows), :].astype(F32))
            d = buf[:, :, :, :, at].reshape(npx, VIEWS, 256)
            grad = gelu_slope(dev * scale[:, at] + off[:, at] + x) * d
            dt3[pl.ds(pix, npx), :, at] = grad
            t1.append(jnp.sum(grad, axis=0))
            t2.append(jnp.sum(grad * dev, axis=0))
        return carry[0] + jnp.concatenate(t1, axis=1), carry[1] + jnp.concatenate(t2, axis=1)

    zero = jnp.zeros((VIEWS, wide), F32)
    (a1, a2), (b1, b2) = geo.loop(body, [(zero, zero), (zero, zero)])
    sums3[0:1] = rows_sum(a1 + b1)
    sums3[1:2] = rows_sum(a2 + b2) * r3


def k_back_expand(geo, me, nf, dt3, pre3, sa3, sb3, gs3, ga, gb, pre2, sa2, sb2, gs2, w, dt2, dz3, sums2, zbuf_b, zbuf_s):
    wide, chans = w.shape[1], w.shape[0]
    lives = [live_rows(me[1], wide), live_rows(me[2], wide)]
    s = ga[...] + gb[...]
    m3, r3 = merged(sa3[...], sb3[...], nf[1], nf[2])
    c1, c2, c3 = back_coefs(lives, s[0:1], s[1:2], r3, gs3[0:1], nf[1] + nf[2])
    m2, r2 = merged(sa2[...], sb2[...], nf[1], nf[2])
    scale, off = gs2[0:1] * r2, gs2[1:2]
    mine = pl.ds(pl.multiple_of(me[0] * 256, 256), 256)

    def body(part, i, pix, npx, row, nrows, carry):
        zbuf = (zbuf_b, zbuf_s)[part]
        for j in range(4):
            at = slice(256 * j, 256 * j + 256)
            z = (
                dt3[pl.ds(pix, npx), :, at] * c1[:, at]
                - c2[part][:, at]
                - (pre3[pl.ds(pix, npx), :, at] - m3[:, at]) * c3[part][:, at]
            )
            zbuf[:, at] = as_rows(z).astype(BF16)
        dz3[pl.ds(row, nrows), :] = zbuf[:, mine]
        d = as_pix(nt(zbuf[...], w[...]))
        dev = pre2[pl.ds(pix, npx)] - m2
        grad = gelu_slope(dev * scale + off) * d
        dt2[pl.ds(pix, npx)] = grad
        return carry[0] + jnp.sum(grad, axis=0), carry[1] + jnp.sum(grad * dev, axis=0)

    zero = jnp.zeros((VIEWS, chans), F32)
    (a1, a2), (b1, b2) = geo.loop(body, [(zero, zero), (zero, zero)])
    sums2[0:1] = rows_sum(a1 + b1)
    sums2[1:2] = rows_sum(a2 + b2) * r2


def k_back_mix(geo, me, nf, dt2, pre2, sa2, sb2, gs2, ga, gb, pre1, sa1, sb1, gs1, w, dt1, dz2, sums1, zb, zs):
    chans = pre2.shape[-1]
    lives = [live_rows(me[1], chans), live_rows(me[2], chans)]
    s = ga[...] + gb[...]
    m2, r2 = merged(sa2[...], sb2[...], nf[1], nf[2])
    c1, c2, c3 = back_coefs(lives, s[0:1], s[1:2], r2, gs2[0:1], nf[1] + nf[2])
    m1, r1 = merged(sa1[...], sb1[...], nf[1], nf[2])
    scale, off = gs1[0:1] * r1, gs1[1:2]
    bufs = (zb, zs)
    for part, (side, _) in enumerate(geo.parts):
        zero_edges(bufs[part], side * VIEWS)

    def back(part, i, pix, npx, row, nrows, carry):
        z = dt2[pl.ds(pix, npx)] * c1 - c2[part] - (pre2[pl.ds(pix, npx)] - m2) * c3[part]
        dz2[pl.ds(row, nrows), :] = as_rows(z).astype(BF16)
        side = geo.parts[part][0]
        at = pl.multiple_of(side * VIEWS + i * nrows, 16)
        store_shifted(bufs[part], at, nrows, side, z, (2, 1, 0))
        return carry

    geo.loop(back, [0, 0])

    def dots(part, i, pix, npx, row, nrows, carry):
        acc = None
        for r in range(3):
            at = pl.multiple_of(i * nrows + (2 - r) * (nrows // 2), 16)
            d = nn(bufs[part][pl.ds(at, nrows), :], w[r])
            acc = d if acc is None else acc + d
        dev = pre1[pl.ds(pix, npx)] - m1
        grad = gelu_slope(dev * scale + off) * as_pix(acc)
        dt1[pl.ds(pix, npx)] = grad
        return carry[0] + jnp.sum(grad, axis=0), carry[1] + jnp.sum(grad * dev, axis=0)

    zero = jnp.zeros((VIEWS, chans), F32)
    (a1, a2), (b1, b2) = geo.loop(dots, [(zero, zero), (zero, zero)])
    sums1[0:1] = rows_sum(a1 + b1)
    sums1[1:2] = rows_sum(a2 + b2) * r1


def k_back_reduce(geo, me, nf, dt1, pre1, sa1, sb1, gs1, ga, gb, dt3, wt, gxb, gxs, dz1, wq):
    chans = pre1.shape[-1]
    lives = [live_rows(me[1], chans), live_rows(me[2], chans)]
    s = ga[...] + gb[...]
    m1, r1 = merged(sa1[...], sb1[...], nf[1], nf[2])
    c1, c2, c3 = back_coefs(lives, s[0:1], s[1:2], r1, gs1[0:1], nf[1] + nf[2])
    mine = pl.ds(pl.multiple_of(me[0] * 256, 256), 256)
    wq[...] = wt[:, mine]

    def body(part, i, pix, npx, row, nrows, carry):
        z = dt1[pl.ds(pix, npx)] * c1 - c2[part] - (pre1[pl.ds(pix, npx)] - m1) * c3[part]
        z = as_rows(z).astype(BF16)
        dz1[pl.ds(row, nrows), :] = z
        g = as_pix(nn(z, wq[...])) + dt3[pl.ds(pix, npx), :, mine]
        (gxb, gxs)[part][pl.ds(pix - (0, geo.pb)[part], npx)] = g
        return carry

    geo.loop(body, [0, 0])


def k_dw_wide(act5, dz6, mids, me, dzs, dwide, dshort):
    dwide[...] = tn(act5[...], dz6[...])
    dshort[...] = tn(mids[...], dzs[me[0]])


def k_dw_stride(me, cols, dz5, dw):
    mine = pl.ds(pl.multiple_of(me[0] * 128, 128), 128)
    z = dz5[:, mine]
    for t in range(9):
        dw[t] = tn(cols[:, t * 512 : (t + 1) * 512], z)


def k_dw_cols(me, size, act, dz, dw):
    mine = pl.ds(pl.multiple_of(me[0] * size, size), size)
    dw[...] = tn(act[...], dz[:, mine])


def k_dw_narrow(me, mid, dz4, dw):
    k_dw_cols(me, 128, mid, dz4, dw)


def k_dw_expand(act2, dz3, dw):
    dw[...] = tn(act2[...], dz3[...])


def k_dw_mix(geo, me, wb, ws, dz2, dw, full):
    mine = pl.ds(pl.multiple_of(me[0] * 64, 64), 64)
    nb, ns = geo.pb * VIEWS, geo.ps * VIEWS
    for r in range(3):
        ob, os = r * geo.hb * VIEWS, r * geo.hs * VIEWS
        full[...] = tn(dz2[0:nb, :], wb[ob : ob + nb, :]) + tn(
            dz2[nb : nb + ns, :], ws[os : os + ns, :]
        )
        dw[r] = full[mine, :]


def k_dw_reduce(me, xs, dz1, dw, full):
    mine = pl.ds(pl.multiple_of(me[0] * 64, 64), 64)
    for j in range(4):
        full[...] = tn(dz1[...], xs[j])
        dw[:, 256 * j : 256 * j + 256] = full[mine, :]


def per_device(
    ni,
    nc,
    x_big,
    x_small,
    cot_big,
    cot_small,
    counts,
    w_reduce,
    w_mix,
    w_expand,
    w_narrow,
    w_stride,
    w_widen,
    w_short,
    gain_mid3,
    shift_mid3,
    gain_out3,
    shift_out3,
    gain_mid4,
    shift_mid4,
    gain_out4,
    shift_out4,
):
    assert nc == 4 and x_big.shape[0] == VIEWS and x_small.shape[0] == VIEWS
    geo = Geo(x_big.shape[1], x_small.shape[1])
    img = lax.axis_index("img")
    q = lax.axis_index("ch").astype(jnp.int32)
    levels = ni.bit_length() - 1
    mine = lax.dynamic_slice_in_dim(counts, img, 1, 0)[0]
    me = jnp.stack([q, mine[0], mine[1]]).astype(jnp.int32)
    per3 = counts[:, 0] * geo.pb + counts[:, 1] * geo.ps
    per4 = counts[:, 0] * geo.qb + counts[:, 1] * geo.qs

    def group_counts(per):
        at = jnp.arange(ni, dtype=jnp.int32)
        out = []
        for k in range(levels):
            own = jnp.sum(jnp.where((at >> k) == (img >> k), per, 0))
            other = jnp.sum(jnp.where((at >> k) == ((img >> k) ^ 1), per, 0))
            out.append((own.astype(F32), other.astype(F32)))
        return out

    cnt3, cnt4 = group_counts(per3), group_counts(per4)
    nf3 = jnp.stack([cnt3[0][0], cnt3[-1][0], cnt3[-1][1]])
    nf4 = jnp.stack([cnt4[0][0], cnt4[-1][0], cnt4[-1][1]])

    def over_img(v, k):
        return lax.ppermute(v, "img", [(i, i ^ (1 << k)) for i in range(ni)])

    def over_ch(v, k):
        return lax.ppermute(v, "ch", [(i, i ^ k) for i in range(nc)])

    def sync_stats(stats, cnt):
        for k in range(levels):
            other = over_img(stats, k)
            if k == levels - 1:
                return stats, other
            na, nb = cnt[k]
            shape = stats.shape
            a = stats.reshape(shape[:-2] + (shape[-2] // 2, 2, shape[-1]))
            b = other.reshape(a.shape)
            ma, mb = a[..., 0, :], b[..., 0, :]
            diff = mb - ma
            mean = (na * ma + nb * mb) / (na + nb)
            square = a[..., 1, :] + b[..., 1, :] + diff * diff * (na * nb / (na + nb))
            stats = jnp.stack([mean, square], axis=-2).reshape(shape)

    def sync_sums(sums):
        for k in range(levels):
            other = over_img(sums, k)
            if k == levels - 1:
                return sums, other
            sums = sums + other

    def quarters(v):
        p1 = over_ch(v, 1)
        p2 = over_ch(v, 2)
        return [v, p1, p2, over_ch(p2, 1)]

    def in_order(pieces):
        full = jnp.stack(pieces)
        return jnp.take(full, jnp.arange(4, dtype=jnp.int32) ^ q, axis=0)

    params = jnp.concatenate(
        [
            v.reshape(-1)
            for v in (
                gain_mid3,
                shift_mid3,
                gain_out3,
                shift_out3,
                gain_mid4,
                shift_mid4,
                gain_out4,
                shift_out4,
            )
        ]
    ).reshape(-1, 128)
    params = in_order(quarters(params)).reshape(4, -1)
    cuts, at = [], 0
    for v in (gain_mid3, shift_mid3, gain_out3, shift_out3, gain_mid4, shift_mid4, gain_out4, shift_out4):
        cuts.append(params[:, at : at + v.size].reshape((4,) + v.shape))
        at += v.size
    gm3, sm3, go3, so3, gm4, sm4, go4, so4 = cuts

    def pair(g, s):
        return jnp.stack([g.reshape(-1), s.reshape(-1)])

    gs1, gs2 = pair(gm3[:, 0], sm3[:, 0]), pair(gm3[:, 1], sm3[:, 1])
    gs3 = pair(go3, so3)
    gs4, gs5 = pair(gm4[:, 0], sm4[:, 0]), pair(gm4[:, 1], sm4[:, 1])
    gs6 = jnp.stack([go4[:, 0], so4[:, 0], go4[:, 1], so4[:, 1]], axis=1)

    def rows_of(v):
        return jnp.transpose(v, (1, 2, 0, 3)).reshape(-1, v.shape[3])

    wr = quarters(w_reduce.T)
    xb, xsm = quarters(rows_of(x_big)), quarters(rows_of(x_small))
    wm = quarters(jnp.transpose(w_mix, (0, 1, 3, 2)).reshape(9, w_mix.shape[3], w_mix.shape[2]))
    we = quarters(w_expand)
    wn = quarters(w_narrow)
    wst = quarters(w_stride.reshape(-1, w_stride.shape[3]))
    wsh = quarters(w_short)
    wwi = quarters(w_widen)
    cb, cs = quarters(rows_of(cot_big)), quarters(rows_of(cot_small))

    m3 = 4 * w_reduce.shape[1]
    c3 = w_reduce.shape[0]
    m4 = w_widen.shape[0]
    c4q = w_widen.shape[1]
    (wt,) = assemble("asm_reduce", me, [(wr, "rows", m3 // 4, (m3, c3))])
    wmix_f, wmix_b = assemble(
        "asm_mix",
        me,
        [
            (wm, "taps_nt", m3 // 4, (3, m3, 3 * m3)),
            (wm, "taps_nn", m3 // 4, (9, m3, m3)),
        ],
    )
    wexp, wnar = assemble(
        "asm_mid",
        me,
        [(we, "cols", c3 // 4, (m3, c3)), (wn, "cols", m4 // 4, (c3, m4))],
    )
    (wstr,) = assemble("asm_stride", me, [(wst, "cols", m4 // 4, (9 * m4, m4))])
    wmix_b = wmix_b.reshape(3, 3 * m3, m3)

    smem = [(me, SMEM)]
    n3, n4 = [(nf3, SMEM)], [(nf4, SMEM)]

    def k(fn):
        return functools.partial(fn, geo)

    hb, hs = geo.hb, geo.hs
    sb4, ss4 = (2, 2, hb // 2, hb // 2, VIEWS, m4), (2, 2, hs // 2, hs // 2, VIEWS, m4)
    wb_shape, ws_shape = ((hb + 2) * hb * VIEWS, 3 * m3), ((hs + 2) * hs * VIEWS, 3 * m3)

    pre1, xs, st = call(
        "reduce",
        k(k_reduce),
        smem + n3 + vm(*xb, *xsm, wt),
        [sds((geo.px, VIEWS, m3)), sds((4, geo.rows, c3 // 4), BF16), sds((2, m3))],
        [pltpu.VMEM((4, m3, c3 // 4), BF16)],
    )
    a1, b1 = sync_stats(st, cnt3)
    pre2, winb, wins, st = call(
        "mix",
        k(k_mix),
        smem + n3 + vm(pre1, a1, b1, gs1, wmix_f),
        [sds((geo.px, VIEWS, m3)), sds(wb_shape, BF16), sds(ws_shape, BF16), sds((2, m3))],
    )
    a2, b2 = sync_stats(st, cnt3)
    pre3, act2, st = call(
        "expand",
        k(k_expand),
        smem + n3 + vm(pre2, a2, b2, gs2, wexp),
        [sds((geo.px, VIEWS, c3)), sds((geo.rows, m3), BF16), sds((2, c3))],
    )
    a3, b3 = sync_stats(st, cnt3)
    pre4b, pre4s, mid, mids, st = call(
        "narrow",
        k(k_narrow),
        smem + n3 + vm(pre3, xs, a3, b3, gs3, wnar),
        [sds(sb4), sds(ss4), sds((geo.rows, c3), BF16), sds((geo.rows4, c3), BF16), sds((2, m4))],
        [pltpu.VMEM((geo.px4, VIEWS, c3), F32)],
    )
    a4, b4 = sync_stats(st, cnt3)
    side, st_side = call(
        "short",
        k(k_short),
        smem + n4 + vm(mids, *wsh),
        [sds((4, geo.px4, VIEWS, c4q)), sds((4, 2, c4q))],
    )
    pre5, cols, st = call(
        "stride",
        k(k_stride),
        smem + n4 + n3 + vm(pre4b, pre4s, a4, b4, gs4, wstr),
        [sds((geo.px4, VIEWS, m4)), sds((geo.rows4, 9 * m4), BF16), sds((2, m4))],
        [pltpu.VMEM(sb4, F32), pltpu.VMEM(ss4, F32)],
    )
    a5, b5 = sync_stats(st, cnt4)
    pre6, act5, st = call(
        "widen",
        k(k_widen),
        smem + n4 + vm(pre5, a5, b5, gs5, *wwi),
        [sds((4, geo.px4, VIEWS, c4q)), sds((geo.rows4, m4), BF16), sds((4, 2, c4q))],
    )
    a6, b6 = sync_stats(jnp.concatenate([st, st_side], axis=1), cnt4)
    out_b, out_s, dt6, sums = call(
        "total",
        k(k_total),
        smem + n4 + vm(pre6, side, a6, b6, gs6, *cb, *cs),
        [
            sds((geo.qb, VIEWS, c4q)),
            sds((geo.qs, VIEWS, c4q)),
            sds((4, geo.px4, VIEWS, c4q)),
            sds((4, 3, c4q)),
        ],
    )
    ga6, gb6 = sync_sums(sums)
    dt5, dz6, dzs, sums = call(
        "back_wide",
        k(k_back_wide),
        smem + n4 + vm(dt6, pre6, side, a6, b6, gs6, ga6, gb6, pre5, a5, b5, gs5, *wwi),
        [
            sds((geo.px4, VIEWS, m4)),
            sds((geo.rows4, c4q), BF16),
            sds((4, geo.rows4, c4q), BF16),
            sds((2, m4)),
        ],
    )
    ga5, gb5 = sync_sums(sums)
    (dms,) = call(
        "back_short", k(k_back_short), smem + vm(dzs, *wsh), [sds((geo.px4, VIEWS, c3))]
    )
    dwide, dshort = call(
        "dw_wide",
        k_dw_wide,
        vm(act5, dz6, mids) + smem + vm(dzs),
        [sds((m4, c4q)), sds((c3, c4q))],
    )
    dt4b, dt4s, dz5, sums = call(
        "back_stride",
        k(k_back_stride),
        smem
        + n4
        + vm(dt5, pre5, a5, b5, gs5, ga5, gb5, pre4b, pre4s, a4, b4, gs4)
        + n3
        + vm(wstr),
        [sds(sb4), sds(ss4), sds((geo.rows4, m4), BF16), sds((2, m4))],
        [pltpu.VMEM((4, geo.rows4, m4), BF16)],
    )
    ga4, gb4 = sync_sums(sums)
    (dstride,) = call("dw_stride", k_dw_stride, smem + vm(cols, dz5), [sds((9, m4, m4 // 4))])
    dt3, dz4, sums = call(
        "back_narrow",
        k(k_back_narrow),
        smem
        + n3
        + vm(dt4b, dt4s, pre4b, pre4s, a4, b4, gs4, ga4, gb4, pre3, xs, a3, b3, gs3, dms, wnar),
        [sds((geo.px, VIEWS, c3)), sds((geo.rows, m4), BF16), sds((2, c3))],
        [pltpu.VMEM((2, hb // 2, 2, VIEWS, c3), F32), pltpu.VMEM((2, hs // 2, 2, VIEWS, c3), F32)],
        limit=56,
    )
    ga3, gb3 = sync_sums(sums)
    (dnarrow,) = call("dw_narrow", k_dw_narrow, smem + vm(mid, dz4), [sds((c3, m4 // 4))])
    dt2, dz3, sums = call(
        "back_expand",
        k(k_back_expand),
        smem + n3 + vm(dt3, pre3, a3, b3, gs3, ga3, gb3, pre2, a2, b2, gs2, wexp),
        [sds((geo.px, VIEWS, m3)), sds((geo.rows, c3 // 4), BF16), sds((2, m3))],
        [
            pltpu.VMEM((2 * hb * VIEWS, c3), BF16),
            pltpu.VMEM((2 * hs * VIEWS, c3), BF16),
        ],
    )
    ga2, gb2 = sync_sums(sums)
    (dexpand,) = call("dw_expand", k_dw_expand, vm(act2, dz3), [sds((m3, c3 // 4))])
    dt1, dz2, sums = call(
        "back_mix",
        k(k_back_mix),
        smem + n3 + vm(dt2, pre2, a2, b2, gs2, ga2, gb2, pre1, a1, b1, gs1, wmix_b),
        [sds((geo.px, VIEWS, m3)), sds((geo.rows, m3), BF16), sds((2, m3))],
        [pltpu.VMEM(wb_shape, BF16), pltpu.VMEM(ws_shape, BF16)],
    )
    ga1, gb1 = sync_sums(sums)
    (dmix,) = call(
        "dw_mix",
        k(k_dw_mix),
        smem + vm(winb, wins, dz2),
        [sds((3, m3 // 4, 3 * m3))],
        [pltpu.VMEM((m3, 3 * m3), F32)],
    )
    gxb, gxs, dz1 = call(
        "back_reduce",
        k(k_back_reduce),
        smem + n3 + vm(dt1, pre1, a1, b1, gs1, ga1, gb1, dt3, wt),
        [
            sds((geo.pb, VIEWS, c3 // 4)),
            sds((geo.ps, VIEWS, c3 // 4)),
            sds((geo.rows, m3), BF16),
        ],
        [pltpu.VMEM((m3, c3 // 4), BF16)],
    )
    (dreduce,) = call(
        "dw_reduce",
        k_dw_reduce,
        smem + vm(xs, dz1),
        [sds((m3 // 4, c3))],
        [pltpu.VMEM((m3, c3 // 4), F32)],
    )
    dwide, dshort = lax.psum((dwide, dshort), "img")
    dstride = lax.psum(dstride, "img")
    dnarrow, dexpand, dmix, dreduce = lax.psum((dnarrow, dexpand, dmix, dreduce), "img")

    def views_first(v, side):
        return jnp.transpose(v.reshape(side, side, VIEWS, v.shape[2]), (2, 0, 1, 3))

    def own(v):
        n = v.shape[0] // 4
        return lax.dynamic_slice_in_dim(v, q * n, n, 0)

    t1, t2, t3 = ga1 + gb1, ga2 + gb2, ga3 + gb3
    t4, t5 = ga4 + gb4, ga5 + gb5
    t6 = lax.dynamic_index_in_dim(ga6 + gb6, q, 0, keepdims=False)
    return (
        views_first(out_b, hb // 2),
        views_first(out_s, hs // 2),
        views_first(gxb, hb),
        views_first(gxs, hs),
        dreduce.T,
        jnp.transpose(dmix.reshape(3, m3 // 4, 3, m3), (0, 2, 3, 1)),
        dexpand,
        dnarrow,
        dstride.reshape(3, 3, m4, m4 // 4),
        dwide,
        dshort,
        jnp.stack([own(t1[1]), own(t2[1])]),
        jnp.stack([own(t1[0]), own(t2[0])]),
        own(t3[1]),
        own(t3[0]),
        jnp.stack([own(t4[1]), own(t5[1])]),
        jnp.stack([own(t4[0]), own(t5[0])]),
        jnp.stack([t6[1], t6[2]]),
        jnp.stack([t6[0], t6[0]]),
    )


def solution(mesh):
    act = P("img", None, None, "ch")
    flat, taps, vec = P(None, "ch"), P(None, None, None, "ch"), P("ch")
    in_specs = (act,) * 4 + (P(), flat, taps, flat, flat, taps, flat, flat)
    in_specs += (flat, flat, vec, vec, flat, flat, flat, flat)
    out_specs = (act,) * 4 + (flat, taps, flat, flat, taps, flat, flat)
    out_specs += (flat, flat, vec, vec, flat, flat, flat, flat)
    return jax.shard_map(
        functools.partial(per_device, mesh.shape["img"], mesh.shape["ch"]),
        mesh=mesh,
        in_specs=in_specs,
        out_specs=out_specs,
        check_vma=False,
    )
```

time: 1840 us -> 690 us (0.38)
  blocking collectives: 572 us -> 0 us
  local copies, waits for them, and re-layouts: 504 us -> 49.7 us
  Pallas kernels: 0 us -> 198 us
  matrix products: 163 us -> 0 us
  waiting for transfers between devices: 462 us -> 327 us
  other arithmetic: 108 us -> 11 us
  starting transfers between devices: 1.94 us -> 71.1 us
    psum x19 -> x0, blocking collectives: 374 us -> none  [the longest x7 140 us: norm_forward(): first = lax.psum(live_sum(pre, lives), 'img')]
    unnamed x353 -> x222, local copies, waits for them, and re-layouts: 316 us -> 40 us
    pallas_call x0 -> x25, Pallas kernels: none -> 198 us  [call(): pl.pallas_call(kernel, out_shape=[o[0] for o in outs], in_specs=[spec for...]
    all_gather x7 -> x0, blocking collectives: 198 us -> none  [the longest x3 108 us: gather_pair(): lax.all_gather(pair[0], 'ch', axis=3, tiled=True)]
    dot_general x138 -> x0, matrix products: 163 us -> none  [the longest x36 62.6 us: taps_input(): jnp.einsum('bhwd,cd->bhwc', grad_out, weight[row_tap, col_tap], preferred...]
    scatter-add x20 -> x0, local copies, waits for them, and re-layouts: 109 us -> none  [the longest x18 106 us: taps_input(): grad_pad = grad_pad.at[:, row_tap:row_tap + height, col_tap:col_tap + wid...]
    all_gather x5 -> x0, waiting for transfers between devices: 100 us -> none  [the longest x3 59.7 us: gather_pair(): lax.all_gather(pair[0], 'ch', axis=3, tiled=True)]
    ppermute x0 -> x72, waiting for transfers between devices: none -> 87.3 us  [the longest x36 59 us: over_img(): return lax.ppermute(v, 'img', [(i, i ^ 1 << k) for i in range(ni)])]
  transfers between devices with their start and end apart: 18 -> 73, of which waited for: 12 -> 34; matrix products, arithmetic and copies ran while one was open for 17% -> 3% of each run, Pallas kernels for 0% -> 13%
where the time goes in v1:
time: 690 us; the launch traced here: 681 us
  waiting for transfers between devices  327 us (47%)
  Pallas kernels  198 us (29%)
  starting transfers between devices  71.1 us (10%)
  local copies, waits for them, and re-layouts  49.7 us (7%)
  between operations  23.7 us (3%)
  other arithmetic  11 us (2%)
    psum x1, waiting for transfers between devices, per_device(): lax.psum((dnarrow, dexpand, dmix, dreduce), 'img')  240 us
    pallas_call x25, Pallas kernels, call(): pl.pallas_call(kernel, out_shape=[o[0] for o in outs], in_specs=[spec for...  198 us
    ppermute x36, waiting for transfers between devices, over_img(): return lax.ppermute(v, 'img', [(i, i ^ 1 << k) for i in range(ni)])  59 us
    ppermute x36, starting transfers between devices, over_img(): return lax.ppermute(v, 'img', [(i, i ^ 1 << k) for i in range(ni)])  53.7 us
    unnamed x222, local copies, waits for them, and re-layouts  40 us
    ppermute x36, waiting for transfers between devices, over_ch(): return lax.ppermute(v, 'ch', [(i, i ^ k) for i in range(nc)])  28.3 us
    ppermute x36, starting transfers between devices, over_ch(): return lax.ppermute(v, 'ch', [(i, i ^ k) for i in range(nc)])  17.4 us
  transfers between devices with their start and end apart: 73, of which 34 were waited for; matrix products, arithmetic and copies ran while one was open for 3% of the time, Pallas kernels for 13%

profile of v1, /device:TPU:0, one launch (start us, length us, event | category | flops | bytes accessed | tf_op | source)
XLA Modules:
  0.0 681.5 jit_solution(2759765980431064023)
XLA Ops:
  12.9 3.0 collective-permute-start.13
  28.1 20.0 %collective-permute-done.7.refs_2_ = bf16[64,1024]{1,0:T(8,128)(2,1)S(1)} collective-permute-done((bf16[64,1024]{1,0:T(8,128)(2,1)}, bf16[64,1024]{1,0:T(8,128)(2,1)S(1)}, u32[]{:S(2)}, u32[]{:S(2)}) %collective-permute-start.7) | collective-permute-done | bytes 131104 | tf_op jit(solution)/shard_map/ppermute | solution.py:741
  54.4 8.0 %reduce.17 = (f32[296,8,256]{2,1,0:T(8,128)}, bf16[4,2368,256]{2,1,0:T(8,128)(2,1)}, f32[2,256]{1,0:T(2,128)S(1)}) custom-call(s32[3]{0:T(128)S(1)} %pad_add_fusion.me, f32[3]{0:T(128)S(1)} %pad_maximum_fusion.17.nf.n4, bf16[1568,256]{1,0:T(8,128)(2,1)S(1)} %bitcast.145, bf16[1568,256]{1,0:T(8,128)(2,1)S(1)} %collective-permute-done.x1b, ...), custom_call_target="tpu_custom_call" | custom-call | tf_op jit(solution)/shard_map/reduce/pallas_call | solution.py:28
  69.7 2.8 collective-permute-start.11
  72.5 3.1 asm_mix.1
  76.6 11.4 %mix.1 = (f32[296,8,256]{2,1,0:T(8,128)S(1)}, bf16[1792,768]{1,0:T(8,128)(2,1)}, bf16[960,768]{1,0:T(8,128)(2,1)S(1)}, f32[2,256]{1,0:T(2,128)S(1)}) custom-call(s32[3]{0:T(128)S(1)} %pad_add_fusion.me, f32[3]{0:T(128)S(1)} %pad_maximum_fusion.17.nf.n4, f32[296,8,256]{2,1,0:T(8,128)} %get-tuple-element.72.pre1, f32[2,256]{1,0:T(2,128)S(1)} %maximum_bitcast_fusion.7.sa.sa1, ...), custom_call_target="tpu_custom_call" | custom-call | tf_op jit(solution)/shard_map/mix/pallas_call | solution.py:28
  97.1 5.6 collective-permute-done.25.refs_6_
  113.3 9.3 %expand.1 = (f32[296,8,1024]{2,1,0:T(8,128)}, bf16[2368,256]{1,0:T(8,128)(2,1)S(1)}, f32[2,1024]{1,0:T(2,128)S(1)}) custom-call(s32[3]{0:T(128)S(1)} %pad_add_fusion.me, f32[3]{0:T(128)S(1)} %pad_maximum_fusion.17.nf.n4, f32[296,8,256]{2,1,0:T(8,128)S(1)} %get-tuple-element.75.pre2, f32[2,256]{1,0:T(2,128)S(1)} %maximum_bitcast_fusion.9.sa.sa2, ...), custom_call_target="tpu_custom_call" | custom-call | tf_op jit(solution)/shard_map/expand/pallas_call | solution.py:28
  132.6 2.6 collective-permute-start.29
  137.2 15.4 %narrow.1 = (f32[2,2,7,7,8,512]{5,4,3,2,1,0:T(8,128)}, f32[2,2,5,5,8,512]{5,4,3,2,1,0:T(8,128)S(1)}, bf16[2368,1024]{1,0:T(8,128)(2,1)}, bf16[592,1024]{1,0:T(8,128)(2,1)S(1)}, f32[2,512]{1,0:T(2,128)S(1)}) custom-call(s32[3]{0:T(128)S(1)} %pad_add_fusion.me, f32[3]{0:T(128)S(1)} %pad_maximum_fusion.17.nf.n4, f32[296,8,1024]{2,1,0:T(8,128)} %get-tuple-element.78.pre3, ...), custom_call_target="tpu_custom_call" | custom-call | tf_op jit(solution)/shard_map/narrow/pallas_call | solution.py:28
  153.8 2.5 collective-permute-done.30
  160.1 2.6 collective-permute-start.32
  162.8 2.8 asm_stride.1.w
  167.8 10.3 %stride.1 = (f32[74,8,512]{2,1,0:T(8,128)S(1)}, bf16[592,4608]{1,0:T(8,128)(2,1)}, f32[2,512]{1,0:T(2,128)S(1)}) custom-call(s32[3]{0:T(128)S(1)} %pad_add_fusion.me, f32[3]{0:T(128)S(1)} %pad_maximum_fusion.16.nf, f32[3]{0:T(128)S(1)} %pad_maximum_fusion.17.nf.n4, f32[2,2,7,7,8,512]{5,4,3,2,1,0:T(8,128)S(1)} %copy-done.1, ...), custom_call_target="tpu_custom_call" | custom-call | tf_op jit(solution)/shard_map/stride/pallas_call | solution.py:28
  189.9 7.5 %short.1 = (f32[4,74,8,512]{3,2,1,0:T(8,128)}, f32[4,2,512]{2,1,0:T(2,128)S(1)}) custom-call(s32[3]{0:T(128)S(1)} %pad_add_fusion.me, f32[3]{0:T(128)S(1)} %pad_maximum_fusion.16.nf, bf16[592,1024]{1,0:T(8,128)(2,1)S(1)} %copy-done.7, bf16[1024,512]{1,0:T(8,128)(2,1)} %w0.7, bf16[1024,512]{1,0:T(8,128)(2,1)} %collective-permute-done.42.w1, ...), custom_call_target="tpu_custom_call" | custom-call | tf_op jit(solution)/shard_map/short/pallas_call | solution.py:28
  199.5 5.4 widen.1
  214.6 2.6 collective-permute-start.47
  217.3 2.2 collective-permute-done.47.sb
  219.5 15.9 %total.1 = (f32[49,8,512]{2,1,0:T(8,128)}, f32[25,8,512]{2,1,0:T(8,128)}, f32[4,74,8,512]{3,2,1,0:T(8,128)}, f32[4,3,512]{2,1,0:T(4,128)S(1)}) custom-call(s32[3]{0:T(128)S(1)} %copy-done.30, f32[3]{0:T(128)S(1)} %copy-done.80, f32[4,74,8,512]{3,2,1,0:T(8,128)} %get-tuple-element.87.pre6, f32[4,74,8,512]{3,2,1,0:T(8,128)} %get-tuple-element.89.side, ...), custom_call_target="tpu_custom_call" | custom-call | tf_op jit(solution)/shard_map/total/pallas_call | solution.py:28
  236.4 2.9 collective-permute-done.54
  241.0 2.7 collective-permute-done.55
  243.7 2.3 collective-permute-start.56
  246.0 2.6 collective-permute-done.56.gb
  248.6 9.6 %back_wide.1 = (f32[74,8,512]{2,1,0:T(8,128)S(1)}, bf16[592,512]{1,0:T(8,128)(2,1)S(1)}, bf16[4,592,512]{2,1,0:T(8,128)(2,1)}, f32[2,512]{1,0:T(2,128)S(1)}) custom-call(s32[3]{0:T(128)S(1)} %copy-done.30, f32[3]{0:T(128)S(1)} %copy-done.81, f32[4,74,8,512]{3,2,1,0:T(8,128)} %get-tuple-element.94.dt, f32[4,74,8,512]{3,2,1,0:T(8,128)} %get-tuple-element.87.pre6, ...), custom_call_target="tpu_custom_call" | custom-call | tf_op jit(solution)/shard_map/back_wide/pallas_call | solution.py:28
  259.3 2.6 collective-permute-done.57
  265.5 2.2 collective-permute-start.59
  267.7 2.3 collective-permute-done.59.gb
  270.0 11.1 %back_stride.1 = (f32[2,2,7,7,8,512]{5,4,3,2,1,0:T(8,128)}, f32[2,2,5,5,8,512]{5,4,3,2,1,0:T(8,128)S(1)}, bf16[592,512]{1,0:T(8,128)(2,1)S(1)}, f32[2,512]{1,0:T(2,128)S(1)}) custom-call(s32[3]{0:T(128)S(1)} %copy-done.30, f32[3]{0:T(128)S(1)} %copy-done.81, f32[74,8,512]{2,1,0:T(8,128)S(1)} %get-tuple-element.96.dt5, f32[74,8,512]{2,1,0:T(8,128)S(1)} %copy-done.5, ...), custom_call_target="tpu_custom_call" | custom-call | tf_op jit(solution)/shard_map/back_stride/pallas_call | solution.py:28
  283.3 2.6 collective-permute-done.60
  287.3 2.1 collective-permute-done.61
  289.5 2.2 collective-permute-start.62
  291.7 7.1 %back_short.1.dms = f32[74,8,1024]{2,1,0:T(8,128)} custom-call(s32[3]{0:T(128)S(1)} %copy-done.30, bf16[4,592,512]{2,1,0:T(8,128)(2,1)} %get-tuple-element.101.dzs, bf16[1024,512]{1,0:T(8,128)(2,1)} %w0.7, bf16[1024,512]{1,0:T(8,128)(2,1)} %collective-permute-done.42.w1, bf16[1024,512]{1,0:T(8,128)(2,1)} %collective-permute-done.43.w2, ...), custom_call_target="tpu_custom_call" | custom-call | tf_op jit(solution)/shard_map/back_short/pallas_call | solution.py:28
  299.4 23.8 %back_narrow.1 = (f32[296,8,1024]{2,1,0:T(8,128)}, bf16[2368,512]{1,0:T(8,128)(2,1)}, f32[2,1024]{1,0:T(2,128)}) custom-call(s32[3]{0:T(128)} %copy-done.28, f32[3]{0:T(128)} %copy-done.58, f32[2,2,7,7,8,512]{5,4,3,2,1,0:T(8,128)} %get-tuple-element.98.dt4b, f32[2,2,5,5,8,512]{5,4,3,2,1,0:T(8,128)} %copy-done.17, ...), custom_call_target="tpu_custom_call" | custom-call | tf_op jit(solution)/shard_map/back_narrow/pallas_call | solution.py:28
  324.3 2.8 collective-permute-done.63
  332.3 3.8 collective-permute-done.65.gb
  336.2 12.4 %back_expand.1 = (f32[296,8,256]{2,1,0:T(8,128)S(1)}, bf16[2368,256]{1,0:T(8,128)(2,1)S(1)}, f32[2,256]{1,0:T(2,128)S(1)}) custom-call(s32[3]{0:T(128)S(1)} %copy-done.31, f32[3]{0:T(128)S(1)} %copy-done.60, f32[296,8,1024]{2,1,0:T(8,128)} %get-tuple-element.102.dt3, f32[296,8,1024]{2,1,0:T(8,128)} %get-tuple-element.78.pre3, f32[2,1024]{1,0:T(2,128)S(1)} %copy-done.40, ...), custom_call_target="tpu_custom_call" | custom-call | tf_op jit(solution)/shard_map/back_expand/pallas_call | solution.py:28
  351.1 2.5 collective-permute-done.66
  358.0 3.7 collective-permute-done.68.gb
  361.7 9.8 %back_mix.1 = (f32[296,8,256]{2,1,0:T(8,128)S(1)}, bf16[2368,256]{1,0:T(8,128)(2,1)S(1)}, f32[2,256]{1,0:T(2,128)S(1)}) custom-call(s32[3]{0:T(128)S(1)} %copy-done.31, f32[3]{0:T(128)S(1)} %copy-done.60, f32[296,8,256]{2,1,0:T(8,128)} %copy-done.14, f32[296,8,256]{2,1,0:T(8,128)} %copy-done.2, f32[2,256]{1,0:T(2,128)S(1)} %copy-done.68, ...), custom_call_target="tpu_custom_call" | custom-call | tf_op jit(solution)/shard_map/back_mix/pallas_call | solution.py:28
  372.7 2.5 collective-permute-done.69
  380.2 4.4 dw_wide.1
  384.6 5.9 dw_stride.1
  390.5 4.9 dw_narrow.1
  396.8 4.2 dw_mix.1
  403.0 8.0 %back_reduce.1 = (f32[196,8,256]{2,1,0:T(8,128)}, f32[100,8,256]{2,1,0:T(8,128)}, bf16[2368,256]{1,0:T(8,128)(2,1)S(1)}) custom-call(s32[3]{0:T(128)S(1)} %copy-done.32, f32[3]{0:T(128)S(1)} %copy-done.61, f32[296,8,256]{2,1,0:T(8,128)S(1)} %get-tuple-element.107.dt1, f32[296,8,256]{2,1,0:T(8,128)} %get-tuple-element.72.pre1, f32[2,256]{1,0:T(2,128)S(1)} %copy-done.75, ...), custom_call_target="tpu_custom_call" | custom-call | tf_op jit(solution)/shard_map/back_reduce/pallas_call | solution.py:28
  411.0 4.7 dw_reduce.1
  422.3 240.2 %all-reduce.3.cloned.1.call-done = (f32[1024,64]{0,1:T(8,128)}, f32[3,3,256,64]{2,1,3,0:T(4,128)}, f32[256,256]{1,0:T(8,128)}, f32[1024,128]{1,0:T(8,128)}, f32[...) async-done(((f32[1024,64]{0,1:T(8,128)}, f32[3,3,256,64]{2,1,3,0:T(4,128)}, f32[256,256]{1,0:T(8,128)}, f32[1024,128]{1,0:T(8,128)}, ...) | async-done | bytes 7143440 | tf_op jit(solution)/shard_map/psum | solution.py:1004
  662.5 2.2 copy.58
  (453 shorter events, 136.6 us)
Async XLA Ops:
  7.2 655.3 %all-reduce.3.cloned.1.call-start = ((), (), s32[]{:S(2)}) async-start(), calls=%async_computation | async-start | bytes 14680064 | tf_op jit(solution)/shard_map/psum | solution.py:1004
  12.9 11.1 %collective-permute-start.13 = (f32[26,128]{1,0:T(8,128)S(1)}, f32[26,128]{1,0:T(8,128)S(1)}, u32[]{:S(2)}, u32[]{:S(2)}) collective-permute-start(f32[26,128]{1,0:T(8,128)S(1)} %bitcast.177), channel_id=1, source_target_pairs={{0,2},{1,3},{2,0},{3,1},{4,6},{5,7},{6,4},{7,5},{8,10},{9,11},{10,... | collective-permute-start | bytes 39944 | tf_op jit(solution)/shard_map/ppermute | solution.py:741
  15.9 8.5 %collective-permute-start.12 = (f32[26,128]{1,0:T(8,128)S(1)}, f32[26,128]{1,0:T(8,128)S(1)}, u32[]{:S(2)}, u32[]{:S(2)}) collective-permute-start(f32[26,128]{1,0:T(8,128)S(1)} %bitcast.178), channel_id=1, source_target_pairs={{0,1},{1,0},{2,3},{3,2},{4,5},{5,4},{6,7},{7,6},{8,9},{9,8},{10,11... | collective-permute-start | bytes 39944 | tf_op jit(solution)/shard_map/ppermute | solution.py:741
  15.9 32.6 %collective-permute-start.1 = (bf16[1568,256]{1,0:T(8,128)(2,1)}, bf16[1568,256]{1,0:T(8,128)(2,1)S(1)}, u32[]{:S(2)}, u32[]{:S(2)}) collective-permute-start(bf16[1568,256]{1,0:T(8,128)(2,1)} %bitcast.143), channel_id=1, source_target_pairs={{0,2},{1,3},{2,0},{3,1},{4,6},{5,7},{6,4},{7,5},{8,10},{9,11},{10,... | collective-permute-start | bytes 2408456 | tf_op jit(solution)/shard_map/ppermute | solution.py:741
  16.1 32.0 %collective-permute-start.4 = (bf16[800,256]{1,0:T(8,128)(2,1)}, bf16[800,256]{1,0:T(8,128)(2,1)S(1)}, u32[]{:S(2)}, u32[]{:S(2)}) collective-permute-start(bf16[800,256]{1,0:T(8,128)(2,1)} %bitcast.146), channel_id=1, source_target_pairs={{0,2},{1,3},{2,0},{3,1},{4,6},{5,7},{6,4},{7,5},{8,10},{9,11},{10,... | collective-permute-start | bytes 1228808 | tf_op jit(solution)/shard_map/ppermute | solution.py:741
  17.9 9.7 %collective-permute-start.6 = (bf16[64,1024]{1,0:T(8,128)(2,1)}, bf16[64,1024]{1,0:T(8,128)(2,1)S(1)}, u32[]{:S(2)}, u32[]{:S(2)}) collective-permute-start(bf16[64,1024]{1,0:T(8,128)(2,1)} %bitcast.155), channel_id=1, source_target_pairs={{0,1},{1,0},{2,3},{3,2},{4,5},{5,4},{6,7},{7,6},{8,9},{9,8},{10,11... | collective-permute-start | bytes 393224 | tf_op jit(solution)/shard_map/ppermute | solution.py:741
  24.0 24.0 %collective-permute-start.7 = (bf16[64,1024]{1,0:T(8,128)(2,1)}, bf16[64,1024]{1,0:T(8,128)(2,1)S(1)}, u32[]{:S(2)}, u32[]{:S(2)}) collective-permute-start(bf16[64,1024]{1,0:T(8,128)(2,1)} %bitcast.156), channel_id=1, source_target_pairs={{0,2},{1,3},{2,0},{3,1},{4,6},{5,7},{6,4},{7,5},{8,10},{9,11},{10,... | collective-permute-start | bytes 393224 | tf_op jit(solution)/shard_map/ppermute | solution.py:741
  26.8 25.4 %collective-permute-start = (bf16[1568,256]{1,0:T(8,128)(2,1)}, bf16[1568,256]{1,0:T(8,128)(2,1)S(1)}, u32[]{:S(2)}, u32[]{:S(2)}) collective-permute-start(bf16[1568,256]{1,0:T(8,128)(2,1)} %bitcast.144), channel_id=1, source_target_pairs={{0,1},{1,0},{2,3},{3,2},{4,5},{5,4},{6,7},{7,6},{8,9},{9,8},{10,11... | collective-permute-start | bytes 2408456 | tf_op jit(solution)/shard_map/ppermute | solution.py:741
  27.7 24.1 %collective-permute-start.3 = (bf16[800,256]{1,0:T(8,128)(2,1)}, bf16[800,256]{1,0:T(8,128)(2,1)S(1)}, u32[]{:S(2)}, u32[]{:S(2)}) collective-permute-start(bf16[800,256]{1,0:T(8,128)(2,1)} %bitcast.147), channel_id=1, source_target_pairs={{0,1},{1,0},{2,3},{3,2},{4,5},{5,4},{6,7},{7,6},{8,9},{9,8},{10,11... | collective-permute-start | bytes 1228808 | tf_op jit(solution)/shard_map/ppermute | solution.py:741
  48.0 4.2 collective-permute-start.5
  49.4 23.1 %collective-permute-start.15 = (bf16[9,64,256]{2,1,0:T(8,128)(2,1)}, bf16[9,64,256]{2,1,0:T(8,128)(2,1)S(1)}, u32[]{:S(2)}, u32[]{:S(2)}) collective-permute-start(bf16[9,64,256]{2,1,0:T(8,128)(2,1)} %bitcast.139), channel_id=1, source_target_pairs={{0,1},{1,0},{2,3},{3,2},{4,5},{5,4},{6,7},{7,6},{8,9},{9,8},{10,11... | collective-permute-start | bytes 884744 | tf_op jit(solution)/shard_map/ppermute | solution.py:741
  51.7 16.2 %collective-permute-start.16 = (bf16[9,64,256]{2,1,0:T(8,128)(2,1)}, bf16[9,64,256]{2,1,0:T(8,128)(2,1)S(1)}, u32[]{:S(2)}, u32[]{:S(2)}) collective-permute-start(bf16[9,64,256]{2,1,0:T(8,128)(2,1)} %bitcast.140), channel_id=1, source_target_pairs={{0,2},{1,3},{2,0},{3,1},{4,6},{5,7},{6,4},{7,5},{8,10},{9,11},{10,... | collective-permute-start | bytes 884744 | tf_op jit(solution)/shard_map/ppermute | solution.py:741
  68.0 4.5 collective-permute-start.17
  69.7 6.9 %collective-permute-start.11 = (f32[2,256]{1,0:T(2,128)S(1)}, f32[2,256]{1,0:T(2,128)S(1)}, u32[]{:S(2)}, u32[]{:S(2)}) collective-permute-start(f32[2,256]{1,0:T(2,128)S(1)} %maximum_bitcast_fusion.7.sa.sa1), channel_id=1, source_target_pairs={{0,16},{4,20},{8,24},{12,28},{16,0},{20,4},{24,8},{28,12},{1,17},{... | collective-permute-start | bytes 6152 | tf_op jit(solution)/shard_map/ppermute | solution.py:738
  89.1 5.1 collective-permute-start.18
  90.6 6.4 collective-permute-start.22
  92.1 10.6 %collective-permute-start.25 = (bf16[1024,128]{1,0:T(8,128)(2,1)S(1)}, bf16[1024,128]{1,0:T(8,128)(2,1)S(1)}, u32[]{:S(2)}, u32[]{:S(2)}) collective-permute-start(bf16[1024,128]{1,0:T(8,128)(2,1)S(1)} %copy-done.33), channel_id=1, source_target_pairs={{0,2},{1,3},{2,0},{3,1},{4,6},{5,7},{6,4},{7,5},{8,10},{9,11},{10,... | collective-permute-start | bytes 786440 | tf_op jit(solution)/shard_map/ppermute | solution.py:741
  92.7 37.8 %collective-permute-start.34 = (bf16[4608,128]{1,0:T(8,128)(2,1)}, bf16[4608,128]{1,0:T(8,128)(2,1)}, u32[]{:S(2)}, u32[]{:S(2)}) collective-permute-start(bf16[4608,128]{1,0:T(8,128)(2,1)} %bitcast.53.refs_0_), channel_id=1, source_target_pairs={{0,2},{1,3},{2,0},{3,1},{4,6},{5,7},{6,4},{7,5},{8,10},{9,11},{10,... | collective-permute-start | bytes 3538952 | tf_op jit(solution)/shard_map/ppermute | solution.py:741
  94.2 9.2 %collective-permute-start.19 = (f32[2,256]{1,0:T(2,128)S(1)}, f32[2,256]{1,0:T(2,128)S(1)}, u32[]{:S(2)}, u32[]{:S(2)}) collective-permute-start(f32[2,256]{1,0:T(2,128)S(1)} %maximum_bitcast_fusion.8), channel_id=1, source_target_pairs={{0,8},{4,12},{8,0},{12,4},{16,24},{20,28},{24,16},{28,20},{1,9},{5... | collective-permute-start | bytes 6152 | tf_op jit(solution)/shard_map/ppermute | solution.py:738
  95.8 8.8 %collective-permute-start.21 = (bf16[256,256]{1,0:T(8,128)(2,1)S(1)}, bf16[256,256]{1,0:T(8,128)(2,1)S(1)}, u32[]{:S(2)}, u32[]{:S(2)}) collective-permute-start(bf16[256,256]{1,0:T(8,128)(2,1)S(1)} %copy-done.43), channel_id=1, source_target_pairs={{0,1},{1,0},{2,3},{3,2},{4,5},{5,4},{6,7},{7,6},{8,9},{9,8},{10,11... | collective-permute-start | bytes 393224 | tf_op jit(solution)/shard_map/ppermute | solution.py:741
  97.1 8.6 %collective-permute-start.24 = (bf16[1024,128]{1,0:T(8,128)(2,1)S(1)}, bf16[1024,128]{1,0:T(8,128)(2,1)S(1)}, u32[]{:S(2)}, u32[]{:S(2)}) collective-permute-start(bf16[1024,128]{1,0:T(8,128)(2,1)S(1)} %copy-done.33), channel_id=1, source_target_pairs={{0,1},{1,0},{2,3},{3,2},{4,5},{5,4},{6,7},{7,6},{8,9},{9,8},{10,11... | collective-permute-start | bytes 786440 | tf_op jit(solution)/shard_map/ppermute | solution.py:741
  105.3 8.1 %collective-permute-start.20 = (f32[2,256]{1,0:T(2,128)S(1)}, f32[2,256]{1,0:T(2,128)S(1)}, u32[]{:S(2)}, u32[]{:S(2)}) collective-permute-start(f32[2,256]{1,0:T(2,128)S(1)} %maximum_bitcast_fusion.9.sa.sa2), channel_id=1, source_target_pairs={{0,16},{4,20},{8,24},{12,28},{16,0},{20,4},{24,8},{28,12},{1,17},{... | collective-permute-start | bytes 6152 | tf_op jit(solution)/shard_map/ppermute | solution.py:738
  105.6 54.5 %collective-permute-start.33 = (bf16[4608,128]{1,0:T(8,128)(2,1)}, bf16[4608,128]{1,0:T(8,128)(2,1)}, u32[]{:S(2)}, u32[]{:S(2)}) collective-permute-start(bf16[4608,128]{1,0:T(8,128)(2,1)} %bitcast.53.refs_0_), channel_id=1, source_target_pairs={{0,1},{1,0},{2,3},{3,2},{4,5},{5,4},{6,7},{7,6},{8,9},{9,8},{10,11... | collective-permute-start | bytes 3538952 | tf_op jit(solution)/shard_map/ppermute | solution.py:741
  105.7 75.2 %collective-permute-start.40 = (bf16[512,512]{1,0:T(8,128)(2,1)}, bf16[512,512]{1,0:T(8,128)(2,1)}, u32[]{:S(2)}, u32[]{:S(2)}) collective-permute-start(bf16[512,512]{1,0:T(8,128)(2,1)} %w0.6), channel_id=1, source_target_pairs={{0,2},{1,3},{2,0},{3,1},{4,6},{5,7},{6,4},{7,5},{8,10},{9,11},{10,... | collective-permute-start | bytes 1572872 | tf_op jit(solution)/shard_map/ppermute | solution.py:741
  107.3 51.6 %collective-permute-start.43 = (bf16[1024,512]{1,0:T(8,128)(2,1)}, bf16[1024,512]{1,0:T(8,128)(2,1)}, u32[]{:S(2)}, u32[]{:S(2)}) collective-permute-start(bf16[1024,512]{1,0:T(8,128)(2,1)} %w0.7), channel_id=1, source_target_pairs={{0,2},{1,3},{2,0},{3,1},{4,6},{5,7},{6,4},{7,5},{8,10},{9,11},{10,... | collective-permute-start | bytes 3145736 | tf_op jit(solution)/shard_map/ppermute | solution.py:741
  130.4 32.3 %collective-permute-start.35 = (bf16[4608,128]{1,0:T(8,128)(2,1)}, bf16[4608,128]{1,0:T(8,128)(2,1)S(1)}, u32[]{:S(2)}, u32[]{:S(2)}) collective-permute-start(bf16[4608,128]{1,0:T(8,128)(2,1)} %collective-permute-done.34.refs_2_), channel_id=1, source_target_pairs={{0,1},{1,0},{2,3},{3,2},{4,5},{5,4},{6,7},{7,6},{8,9},{9,8},{10,11... | collective-permute-start | bytes 3538952 | tf_op jit(solution)/shard_map/ppermute | solution.py:741
  132.6 4.6 collective-permute-start.29
  158.9 28.0 %collective-permute-start.42 = (bf16[1024,512]{1,0:T(8,128)(2,1)}, bf16[1024,512]{1,0:T(8,128)(2,1)}, u32[]{:S(2)}, u32[]{:S(2)}) collective-permute-start(bf16[1024,512]{1,0:T(8,128)(2,1)} %w0.7), channel_id=1, source_target_pairs={{0,1},{1,0},{2,3},{3,2},{4,5},{5,4},{6,7},{7,6},{8,9},{9,8},{10,11... | collective-permute-start | bytes 3145736 | tf_op jit(solution)/shard_map/ppermute | solution.py:741
  160.0 27.0 %collective-permute-start.44 = (bf16[1024,512]{1,0:T(8,128)(2,1)}, bf16[1024,512]{1,0:T(8,128)(2,1)}, u32[]{:S(2)}, u32[]{:S(2)}) collective-permute-start(bf16[1024,512]{1,0:T(8,128)(2,1)} %collective-permute-done.43.w2), channel_id=1, source_target_pairs={{0,1},{1,0},{2,3},{3,2},{4,5},{5,4},{6,7},{7,6},{8,9},{9,8},{10,11... | collective-permute-start | bytes 3145736 | tf_op jit(solution)/shard_map/ppermute | solution.py:741
  160.1 7.7 %collective-permute-start.32 = (f32[2,512]{1,0:T(2,128)S(1)}, f32[2,512]{1,0:T(2,128)S(1)}, u32[]{:S(2)}, u32[]{:S(2)}) collective-permute-start(f32[2,512]{1,0:T(2,128)S(1)} %maximum_bitcast_fusion.3.sa.sa4), channel_id=1, source_target_pairs={{0,16},{4,20},{8,24},{12,28},{16,0},{20,4},{24,8},{28,12},{1,17},{... | collective-permute-start | bytes 12296 | tf_op jit(solution)/shard_map/ppermute | solution.py:738
  180.2 17.2 %collective-permute-start.39 = (bf16[512,512]{1,0:T(8,128)(2,1)}, bf16[512,512]{1,0:T(8,128)(2,1)S(1)}, u32[]{:S(2)}, u32[]{:S(2)}) collective-permute-start(bf16[512,512]{1,0:T(8,128)(2,1)} %w0.6), channel_id=1, source_target_pairs={{0,1},{1,0},{2,3},{3,2},{4,5},{5,4},{6,7},{7,6},{8,9},{9,8},{10,11... | collective-permute-start | bytes 1572872 | tf_op jit(solution)/shard_map/ppermute | solution.py:741
  180.9 16.7 %collective-permute-start.41 = (bf16[512,512]{1,0:T(8,128)(2,1)}, bf16[512,512]{1,0:T(8,128)(2,1)S(1)}, u32[]{:S(2)}, u32[]{:S(2)}) collective-permute-start(bf16[512,512]{1,0:T(8,128)(2,1)} %collective-permute-done.40.w2), channel_id=1, source_target_pairs={{0,1},{1,0},{2,3},{3,2},{4,5},{5,4},{6,7},{7,6},{8,9},{9,8},{10,11... | collective-permute-start | bytes 1572872 | tf_op jit(solution)/shard_map/ppermute | solution.py:741
  186.5 11.7 %collective-permute-start.38 = (f32[2,512]{1,0:T(2,128)S(1)}, f32[2,512]{1,0:T(2,128)S(1)}, u32[]{:S(2)}, u32[]{:S(2)}) collective-permute-start(f32[2,512]{1,0:T(2,128)S(1)} %maximum_bitcast_fusion.5.sa.sa5), channel_id=1, source_target_pairs={{0,16},{4,20},{8,24},{12,28},{16,0},{20,4},{24,8},{28,12},{1,17},{... | collective-permute-start | bytes 12296 | tf_op jit(solution)/shard_map/ppermute | solution.py:738
  186.9 30.4 %collective-permute-start.48 = (bf16[392,512]{1,0:T(8,128)(2,1)}, bf16[392,512]{1,0:T(8,128)(2,1)}, u32[]{:S(2)}, u32[]{:S(2)}) collective-permute-start(bf16[392,512]{1,0:T(8,128)(2,1)} %bitcast.149), channel_id=1, source_target_pairs={{0,1},{1,0},{2,3},{3,2},{4,5},{5,4},{6,7},{7,6},{8,9},{9,8},{10,11... | collective-permute-start | bytes 1204232 | tf_op jit(solution)/shard_map/ppermute | solution.py:741
  187.0 26.1 %collective-permute-start.49 = (bf16[392,512]{1,0:T(8,128)(2,1)}, bf16[392,512]{1,0:T(8,128)(2,1)}, u32[]{:S(2)}, u32[]{:S(2)}) collective-permute-start(bf16[392,512]{1,0:T(8,128)(2,1)} %bitcast.150), channel_id=1, source_target_pairs={{0,2},{1,3},{2,0},{3,1},{4,6},{5,7},{6,4},{7,5},{8,10},{9,11},{10,... | collective-permute-start | bytes 1204232 | tf_op jit(solution)/shard_map/ppermute | solution.py:741
  197.4 19.9 %collective-permute-start.51 = (bf16[200,512]{1,0:T(8,128)(2,1)S(1)}, bf16[200,512]{1,0:T(8,128)(2,1)}, u32[]{:S(2)}, u32[]{:S(2)}) collective-permute-start(bf16[200,512]{1,0:T(8,128)(2,1)S(1)} %bitcast.152), channel_id=1, source_target_pairs={{0,1},{1,0},{2,3},{3,2},{4,5},{5,4},{6,7},{7,6},{8,9},{9,8},{10,11... | collective-permute-start | bytes 614408 | tf_op jit(solution)/shard_map/ppermute | solution.py:741
  197.6 15.4 %collective-permute-start.52 = (bf16[200,512]{1,0:T(8,128)(2,1)S(1)}, bf16[200,512]{1,0:T(8,128)(2,1)}, u32[]{:S(2)}, u32[]{:S(2)}) collective-permute-start(bf16[200,512]{1,0:T(8,128)(2,1)S(1)} %bitcast.153), channel_id=1, source_target_pairs={{0,2},{1,3},{2,0},{3,1},{4,6},{5,7},{6,4},{7,5},{8,10},{9,11},{10,... | collective-permute-start | bytes 614408 | tf_op jit(solution)/shard_map/ppermute | solution.py:741
  205.5 4.2 collective-permute-start.45
  213.0 4.3 collective-permute-start.53
  213.1 4.2 collective-permute-start.50
  214.6 4.9 collective-permute-start.47
  239.3 4.3 collective-permute-start.55
  243.7 4.9 collective-permute-start.56
  265.5 4.5 collective-permute-start.59
  289.5 9.3 %collective-permute-start.62 = (f32[2,512]{1,0:T(2,128)S(1)}, f32[2,512]{1,0:T(2,128)S(1)}, u32[]{:S(2)}, u32[]{:S(2)}) collective-permute-start(f32[2,512]{1,0:T(2,128)S(1)} %add.450.ga), channel_id=1, source_target_pairs={{0,16},{4,20},{8,24},{12,28},{16,0},{20,4},{24,8},{28,12},{1,17},{... | collective-permute-start | bytes 12296 | tf_op jit(solution)/shard_map/ppermute | solution.py:738
  331.5 4.6 collective-permute-start.65
  357.2 4.5 collective-permute-start.68
  379.4 22.9 %collective-permute-start.71 = (f32[2,256]{1,0:T(2,128)}, f32[2,256]{1,0:T(2,128)}, u32[]{:S(2)}, u32[]{:S(2)}) collective-permute-start(f32[2,256]{1,0:T(2,128)} %add.456.ga), channel_id=1, source_target_pairs={{0,16},{4,20},{8,24},{12,28},{16,0},{20,4},{24,8},{28,12},{1,17},{... | collective-permute-start | bytes 6152 | tf_op jit(solution)/shard_map/ppermute | solution.py:738
  (127 other events, 1708.7 us)
Sparse Core Ops, SparseCore 0:
  415.9 246.5 all-reduce.2

commit v2 on v1

v2 whole, which is shorter than its diff:
```python
import functools
import math

import jax
import jax.numpy as jnp
from jax import lax
from jax.experimental import pallas as pl
from jax.experimental.pallas import tpu as pltpu
from jax.sharding import PartitionSpec as P

EPS = 1e-05
G0 = 0.7978845608028654
G1 = G0 * 0.044715
F32 = jnp.float32
BF16 = jnp.bfloat16
VIEWS = 8
AHEAD = 3

ANY = pl.BlockSpec(memory_space=pl.ANY)
HBM = pl.BlockSpec(memory_space=pltpu.HBM)
VMEM = pl.BlockSpec(memory_space=pltpu.VMEM)
SMEM = pl.BlockSpec(memory_space=pltpu.SMEM)


def sds(shape, dtype=F32):
    return jax.ShapeDtypeStruct(tuple(shape), dtype)


class Flow:
    WHOLE = ("w", "all", "part", "w_in", "w_ahead", "w_back")

    def __init__(self, kind, base=0, shape=None):
        self.kind, self.base, self.shape = kind, base, shape

    def keys(self, geo, shape):
        parts = (0, 1)
        if self.kind in ("big", "big_px"):
            parts = (0,)
        if self.kind in ("small", "small_px"):
            parts = (1,)
        if self.kind not in ("lead",) + self.WHOLE:
            return [(part, n) for part in parts for n in range(len(geo.groups[part]))]
        if self.kind == "lead":
            return list(range(shape[0]))
        return [None]

    def buffer(self, geo, shapes, dtype):
        if self.kind == "x":
            return pltpu.VMEM((4, geo.rows, shapes[0][1]), dtype)
        if self.kind == "w":
            return pltpu.VMEM(self.shape, dtype)
        if self.kind == "part":
            return pltpu.VMEM(self.shape, dtype)
        c = shapes[0][-1]
        if self.kind.startswith("w_"):
            return pltpu.VMEM({"w_in": (4, c, c), "w_ahead": (3, c, 3 * c), "w_back": (9, c, c)}[self.kind], dtype)
        return pltpu.VMEM(tuple(shapes[0]), dtype)

    def pairs(self, geo, q, hbm, buf, key):
        if self.kind == "w":
            rows, n = buf.shape[0], buf.shape[1] // 4
            found = []
            for p in range(4):
                for b in range(n // 128):
                    at = pl.ds(pl.multiple_of((q ^ p) * n + 128 * b, 128), 128)
                    found.append((hbm[p].at[pl.ds(self.base + rows * b, rows)], buf.at[:, at]))
            return found
        if self.kind.startswith("w_"):
            c = buf.shape[1]
            n = c // 4
            found = []
            for p in range(4):
                at = pl.ds(pl.multiple_of((q ^ p) * n, n), n)
                for t in range(4 if self.kind == "w_in" else 9):
                    src = hbm[p].at[pl.ds(self.base + n * t, n)]
                    if self.kind == "w_ahead":
                        found.append((src, buf.at[t // 3, at, pl.ds(t % 3 * c, c)]))
                    else:
                        found.append((src, buf.at[t, at]))
            return found
        if self.kind == "part":
            return [(hbm[0].at[pl.ds(self.base, buf.shape[0])], buf)]
        if key is None:
            return [(hbm[0], buf)]
        if self.kind == "lead":
            return [(hbm[0].at[key], buf.at[key])]
        part, group = key
        i, end = geo.groups[part][group]
        pix, npx, row, nrows = geo.step(part, i)
        npx, nrows, first = npx * (end - i), nrows * (end - i), pix - geo.parts[part][1]
        if self.kind == "px":
            at = pl.ds(pix, npx)
        elif self.kind == "rows":
            at = pl.ds(row, nrows)
        elif self.kind in ("big_px", "small_px"):
            at = pl.ds(first, npx)
        elif self.kind == "x":
            local = pl.ds(first * VIEWS, nrows)
            return [
                (hbm[4 * part + p].at[local], buf.at[q ^ p, pl.ds(row, nrows)]) for p in range(4)
            ]
        else:
            at = pl.ds(i, end - i)
            return [(hbm[0].at[:, :, at], buf.at[:, :, at])]
        return [(hbm[0].at[at], buf.at[at])]


class Moves:
    def __init__(self, geo, q):
        self.geo, self.q, self.flows, self.kept = geo, q, [], []

    def add(self, flow, hbm, buf, sem, inward):
        self.flows.append((flow, hbm, buf, sem, inward))

    def copies(self, entry, key):
        flow, hbm, buf, sem, inward = entry
        if flow.kind in flow.WHOLE:
            at = 0
        elif flow.kind == "lead":
            at = key
        elif flow.kind in ("px", "rows", "x"):
            at = (0, len(self.geo.groups[0]))[key[0]] + key[1]
        else:
            at = key[1]
        pairs = flow.pairs(self.geo, self.q, hbm, buf, key)
        return [
            pltpu.make_async_copy(*((a, b) if inward else (b, a)), sem.at[n, at])
            for n, (a, b) in enumerate(pairs)
        ]

    def entries(self, inward, key):
        for entry in self.flows:
            flow = entry[0]
            if entry[4] != inward:
                continue
            if key is None:
                fits = flow.kind in flow.WHOLE
            elif isinstance(key, int):
                fits = flow.kind == "lead"
            else:
                kinds = ("px", "rows", "x") + (("big", "big_px"), ("small", "small_px"))[key[0]]
                fits = flow.kind in kinds
            if fits:
                yield entry

    def start(self, inward, key):
        for entry in self.entries(inward, key):
            for c in self.copies(entry, key):
                c.start()

    def wait(self, inward, key):
        for entry in self.entries(inward, key):
            for c in self.copies(entry, key):
                c.wait()

    def begin(self):
        self.order = [(part, n) for part in range(2) for n in range(len(self.geo.groups[part]))]
        self.start(True, self.order[0])
        self.start(True, None)
        for key in self.order[1:AHEAD]:
            self.start(True, key)
        leads = [e[1][0].shape[0] for e in self.flows if e[4] and e[0].kind == "lead"]
        for n in range(max(leads, default=0)):
            self.start(True, n)
        streams = any(e[4] and e[0].kind not in ("lead",) + Flow.WHOLE for e in self.flows)
        if not streams:
            for c in self.kept:
                c.start()

    def ready(self):
        self.wait(True, None)

    def arrive(self, *key):
        if len(key) == 1:
            self.wait(True, key[0])
            return
        self.wait(True, key)
        at = self.order.index(key)
        if at + AHEAD < len(self.order):
            self.start(True, self.order[at + AHEAD])
        streams = any(e[4] and e[0].kind not in ("lead",) + Flow.WHOLE for e in self.flows)
        if at == 0 and streams:
            for c in self.kept:
                c.start()

    def leave(self, *key):
        self.start(False, key if len(key) > 1 else key[0])

    def send(self, *refs):
        for entry in self.entries(False, None):
            if any(entry[2] is r for r in refs):
                for c in self.copies(entry, None):
                    c.start()

    def finish(self):
        for entry in self.flows:
            if not entry[4]:
                shape = entry[1][0].shape
                for key in entry[0].keys(self.geo, shape):
                    for c in self.copies(entry, key):
                        c.wait()
        for c in self.kept:
            c.wait()


class Keep:
    kind = "keep"

    def __init__(self, source):
        self.source = source


def fast(shape, dtype=F32):
    return pltpu.VMEM(tuple(shape), dtype)


def scoped_bytes(v):
    return math.prod(v.shape) * jnp.dtype(v.dtype).itemsize


def in_hbm(v):
    return pltpu.with_memory_space_constraint(v, pltpu.HBM)


def call(name, kernel, ins, outs, scratch=(), cost=None, order=False, geo=None, slack=14):
    if order:
        inner, n_in, n_out = kernel, len(ins), len(outs)

        def kernel(*refs):
            rest = refs[n_in:]
            return inner(*refs[:n_in], *rest[n_out:], *rest[:n_out])

    outs = [o if isinstance(o, tuple) else (o, VMEM) for o in outs]
    arrays, specs, moved = [], [], []
    for a, spec in ins:
        group = a if isinstance(a, list) else [a]
        flow = isinstance(spec, Flow)
        arrays += [in_hbm(v) for v in group] if flow else group
        specs += [HBM if flow else spec] * len(group)
        moved.append((spec if flow else None, len(group), [v.shape for v in group], group[0].dtype))
    out_shapes, out_specs = [], []
    for shape, spec in outs:
        flow = isinstance(spec, (Flow, Keep))
        out_shapes.append(pltpu.HBM(shape.shape, shape.dtype) if flow else shape)
        out_specs.append(HBM if flow else spec)
        moved.append((spec if flow else None, 1, [shape.shape], shape.dtype))
    extra = []
    for flow, _, shapes, dtype in moved:
        if isinstance(flow, Keep):
            extra += [pltpu.SemaphoreType.DMA((1,))]
        elif flow:
            keys = len(flow.keys(geo, shapes[0]))
            copies = {"x": 4, "w": 4, "w_in": 16, "w_ahead": 36, "w_back": 36}.get(flow.kind, 1)
            if flow.kind == "w":
                copies = flow.shape[1] // 128
            extra += [flow.buffer(geo, shapes, dtype), pltpu.SemaphoreType.DMA((copies, keys))]
    body = kernel
    if extra:

        def body(*refs):
            n_io = sum(n for _, n, _, _ in moved)
            given, own, rest = list(refs[:n_io]), refs[n_io : n_io + len(scratch)], refs[n_io + len(scratch) :]
            rest = list(rest)
            moves = Moves(geo, given[0][0])
            args = []
            for n, (flow, count, _, _) in enumerate(moved):
                group, given = given[:count], given[count:]
                if not flow:
                    args += group
                    continue
                if isinstance(flow, Keep):
                    moves.kept.append(pltpu.make_async_copy(args[flow.source], group[0], rest[0].at[0]))
                    rest = rest[1:]
                    continue
                buf, sem = rest[:2]
                rest = rest[2:]
                moves.add(flow, group, buf, sem, n < len(ins))
                args.append(buf)
            moves.begin()
            kernel(moves, *args, *own)
            moves.finish()

    scratch = list(scratch)
    def held(v):
        pinned = "vmem" in str(getattr(v, "memory_space", "")).lower()
        return 0 if pinned else scoped_bytes(v)

    need = sum(held(jax.typeof(a)) for a, spec in zip(arrays, specs) if spec is VMEM)
    need += sum(held(o) for o, spec in zip(out_shapes, out_specs) if spec is VMEM)
    need += sum(
        scoped_bytes(v)
        for v in scratch + extra
        if getattr(v, "memory_space", None) == pltpu.VMEM
    )
    result = pl.pallas_call(
        body,
        out_shape=out_shapes,
        in_specs=specs,
        out_specs=out_specs,
        scratch_shapes=scratch + extra,
        compiler_params=pltpu.CompilerParams(vmem_limit_bytes=need + need // 16 + (slack << 20)),
        cost_estimate=cost,
        name=name,
    )(*arrays)
    return list(result)


def vm(*arrays):
    return [(a, VMEM) for a in arrays]


def nn(a, b):
    return lax.dot_general(a, b, (((1,), (0,)), ((), ())), preferred_element_type=F32)


def nt(a, b):
    return lax.dot_general(a, b, (((1,), (1,)), ((), ())), preferred_element_type=F32)


def tn(a, b):
    return lax.dot_general(a, b, (((0,), (0,)), ((), ())), preferred_element_type=F32)


def gelu(t):
    half = 0.5 * t
    return half + half * jnp.tanh(t * (G0 + G1 * (t * t)))


def gelu_slope(t):
    sq = t * t
    th = jnp.tanh(t * (G0 + G1 * sq))
    return 0.5 * (1.0 + th) + (0.5 * t) * (1.0 - th * th) * (G0 + (3.0 * G1) * sq)


def live_rows(count, chans):
    return (lax.broadcasted_iota(jnp.int32, (VIEWS, chans), 0) < count).astype(F32)


def rows_sum(v):
    return jnp.sum(v, axis=0, keepdims=True)


def merged(sa, sb, na, nb):
    total = na + nb
    mean = (na * sa[0:1] + nb * sb[0:1]) / total
    diff = sb[0:1] - sa[0:1]
    square = sa[1:2] + sb[1:2] + diff * diff * (na * nb / total)
    return mean, lax.rsqrt(square / total + EPS)


def as_rows(v):
    return v.reshape(v.shape[0] * v.shape[1], v.shape[2])


def as_pix_rows(v):
    return v.reshape(v.shape[0] * v.shape[1], VIEWS, v.shape[3])


def as_pix(v):
    return v.reshape(v.shape[0] // VIEWS, VIEWS, v.shape[1])


class Geo:
    def __init__(self, hb, hs):
        self.hb, self.hs = hb, hs
        self.pb, self.ps = hb * hb, hs * hs
        self.px = self.pb + self.ps
        self.rows = self.px * VIEWS
        self.qb, self.qs = self.pb // 4, self.ps // 4
        self.px4 = self.qb + self.qs
        self.rows4 = self.px4 * VIEWS
        self.parts = ((hb, 0), (hs, self.pb))
        self.groups = [self.cuts(hb // 2, 1), self.cuts(hs // 2, 2)]

    @staticmethod
    def cuts(steps, first):
        at = sorted({0, steps} | set(range(first, steps, 2)))
        return list(zip(at[:-1], at[1:]))

    @staticmethod
    def aligned(n):
        return n if isinstance(n, int) else pl.multiple_of(n, 16)

    def step(self, part, i):
        side, start = self.parts[part]
        npx = 2 * side
        return start + i * npx, npx, self.aligned((start + i * npx) * VIEWS), npx * VIEWS

    def loop(self, body, carries, arrive=None, leave=None):
        out = []
        for part in range(2):

            def run(i, carry, part=part):
                for n, (lo, hi) in enumerate(self.groups[part]):
                    if arrive:
                        pl.when(i == lo)(functools.partial(arrive.arrive, part, n))
                carry = body(part, i, *self.step(part, i), carry)
                for n, (lo, hi) in enumerate(self.groups[part]):
                    if leave:
                        pl.when(i == hi - 1)(functools.partial(leave.leave, part, n))
                return carry

            out.append(lax.fori_loop(0, self.groups[part][-1][1], run, carries[part]))
        return out


def finish_stats(geo, ref, sums, lives, count, out, quarter=None):
    mean = (rows_sum(sums[0] * lives[0]) + rows_sum(sums[1] * lives[1])) / count

    def body(part, i, pix, npx, row, nrows, carry):
        dev = ref[pl.ds(pix, npx)] - mean
        return carry + jnp.sum(dev * dev, axis=0)

    zero = jnp.zeros(sums[0].shape, F32)
    sq = geo.loop(body, [zero, zero])
    out[0:1] = mean
    out[1:2] = rows_sum(sq[0] * lives[0]) + rows_sum(sq[1] * lives[1])


def block_stats(geo, value, lives, count):
    big, small = value[: geo.qb], value[geo.qb :]
    mean = (
        rows_sum(jnp.sum(big, axis=0) * lives[0]) + rows_sum(jnp.sum(small, axis=0) * lives[1])
    ) / count
    db, ds = big - mean, small - mean
    square = rows_sum(jnp.sum(db * db, axis=0) * lives[0]) + rows_sum(
        jnp.sum(ds * ds, axis=0) * lives[1]
    )
    return mean, square


def k_reduce(geo, io, me, nf, xs, wt, pre, stats):
    io.ready()
    chans = wt.shape[1]
    lives = [live_rows(me[1], chans), live_rows(me[2], chans)]

    def body(part, i, pix, npx, row, nrows, carry):
        acc = None
        for j in range(4):
            d = nt(xs[j, pl.ds(row, nrows), :], wt[j])
            acc = d if acc is None else acc + d
        z = as_pix(acc)
        pre[pl.ds(pix, npx)] = z
        return carry + jnp.sum(z, axis=0)

    zero = jnp.zeros((VIEWS, chans), F32)
    sums = geo.loop(body, [zero, zero], io, io)
    finish_stats(geo, pre, sums, lives, nf[0], stats)


def k_counts(ni, sizes, counts, me, nf3, cnt3, nf4, cnt4):
    img = lax.axis_index("img")
    levels = ni.bit_length() - 1
    me[0] = lax.axis_index("ch").astype(jnp.int32)
    me[1] = counts[img, 0]
    me[2] = counts[img, 1]
    me[3] = img
    for (big, small), nf, cnt in zip(sizes, (nf3, nf4), (cnt3, cnt4)):

        def group(shift, index):
            def add(i, total):
                at = index * (1 << shift) + i
                return total + counts[at, 0] * big + counts[at, 1] * small

            return lax.fori_loop(0, 1 << shift, add, jnp.int32(0)).astype(F32)

        nf[0] = group(0, img)
        for m in range(2):
            nf[1 + m] = group(levels - 1, (img >> (levels - 1)) ^ m)
        row, k = 0, 0
        while k < levels - 1:
            bits = 2 if k == 0 else 1
            for m in range(8):
                cnt[row + m] = group(k, (img >> k) ^ m) if m < 1 << bits else jnp.float32(0.0)
            row, k = row + 8, k + bits


def k_merge(first, n, cnt, *refs):
    arrays, out = refs[:n], refs[n]
    for at in range(0, out.shape[-2], 2):
        mean_at, sq_at = (..., slice(at, at + 1), slice(None)), (..., slice(at + 1, at + 2), slice(None))
        groups = [(cnt[first + m], a[mean_at], a[sq_at]) for m, a in enumerate(arrays)]
        while len(groups) > 1:
            pairs = []
            for (na, ma, qa), (nb, mb, qb) in zip(groups[::2], groups[1::2]):
                total = na + nb
                diff = mb - ma
                pairs.append(
                    (total, (na * ma + nb * mb) / total, qa + qb + diff * diff * (na * nb / total))
                )
            groups = pairs
        out[mean_at], out[sq_at] = groups[0][1], groups[0][2]


def k_add(n, *refs):
    values = [r[...] for r in refs[:n]]
    while len(values) > 1:
        values = [a + b for a, b in zip(values[::2], values[1::2])]
    refs[n][...] = values[0]


def side_shift(v, by):
    zero = jnp.zeros((v.shape[0], 1) + v.shape[2:], v.dtype)
    if by > 0:
        return jnp.concatenate([zero, v[:, :-1]], axis=1)
    return jnp.concatenate([v[:, 1:], zero], axis=1)


def store_shifted(buf, row, nrows, side, v, order):
    img = v.reshape(2, side, VIEWS, v.shape[-1])
    chans = v.shape[-1]
    forms = [side_shift(img, 1), img, side_shift(img, -1)]
    for lane, k in enumerate(order):
        flat = forms[k].reshape(nrows, chans).astype(BF16)
        buf[pl.ds(row, nrows), lane * chans : (lane + 1) * chans] = flat


def put_phases(ref, i, v):
    for k in range(4):
        ref[k // 2, k % 2, i] = v[k // 2, :, k % 2]


def get_phases(ref, i):
    rows = [jnp.stack([ref[r, 0, i], ref[r, 1, i]], axis=1) for r in range(2)]
    return jnp.stack(rows)


def zero_edges(buf, edge):
    total = buf.shape[0]
    buf[0:edge, :] = jnp.zeros((edge, buf.shape[1]), BF16)
    buf[total - edge : total, :] = jnp.zeros((edge, buf.shape[1]), BF16)


def k_mix(geo, io, me, nf, pre1, sa, sb, gs, w, pre2, wb, ws, stats):
    chans = pre1.shape[-1]
    lives = [live_rows(me[1], chans), live_rows(me[2], chans)]
    mean, inv = merged(sa[...], sb[...], nf[1], nf[2])
    scale, shift = gs[0:1] * inv, gs[1:2]
    bufs = (wb, ws)
    for part, (side, _) in enumerate(geo.parts):
        zero_edges(bufs[part], side * VIEWS)

    def act(part, i, pix, npx, row, nrows, carry):
        a = gelu((pre1[pl.ds(pix, npx)] - mean) * scale + shift)
        side = geo.parts[part][0]
        at = pl.multiple_of(side * VIEWS + i * nrows, 16)
        store_shifted(bufs[part], at, nrows, side, a, (0, 1, 2))
        return carry

    geo.loop(act, [0, 0], io)
    io.send(wb, ws)
    io.ready()

    def dots(part, i, pix, npx, row, nrows, carry):
        acc = None
        for r in range(3):
            at = pl.multiple_of(i * nrows + r * (nrows // 2), 16)
            d = nt(bufs[part][pl.ds(at, nrows), :], w[r])
            acc = d if acc is None else acc + d
        z = as_pix(acc)
        pre2[pl.ds(pix, npx)] = z
        return carry + jnp.sum(z, axis=0)

    zero = jnp.zeros((VIEWS, chans), F32)
    sums = geo.loop(dots, [zero, zero], None, io)
    finish_stats(geo, pre2, sums, lives, nf[0], stats)


def k_expand(geo, io, me, nf, pre2, sa, sb, gs, w, pre3, act2, stats):
    chans = w.shape[1]
    lives = [live_rows(me[1], chans), live_rows(me[2], chans)]
    mean, inv = merged(sa[...], sb[...], nf[1], nf[2])
    scale, shift = gs[0:1] * inv, gs[1:2]

    def body(part, i, pix, npx, row, nrows, carry):
        a = as_rows(gelu((pre2[pl.ds(pix, npx)] - mean) * scale + shift)).astype(BF16)
        act2[pl.ds(row, nrows), :] = a
        z = as_pix(nn(a, w[...]))
        pre3[pl.ds(pix, npx)] = z
        return carry + jnp.sum(z, axis=0)

    io.ready()
    zero = jnp.zeros((VIEWS, chans), F32)
    sums = geo.loop(body, [zero, zero], io, io)
    finish_stats(geo, pre3, sums, lives, nf[0], stats)


def k_narrow(geo, io, me, nf, pre3, xs, sa, sb, gs, w, pre4b, pre4s, mid, mids, stats, mid_even):
    chans = w.shape[1]
    lives = [live_rows(me[1], chans), live_rows(me[2], chans)]
    mean, inv = merged(sa[...], sb[...], nf[1], nf[2])
    scale, shift = gs[0:1] * inv, gs[1:2]
    pre4 = (pre4b, pre4s)

    def body(part, i, pix, npx, row, nrows, carry):
        side = geo.parts[part][0]
        half = side // 2
        for j in range(4):
            at = slice(256 * j, 256 * j + 256)
            dev = pre3[pl.ds(pix, npx), :, at] - mean[:, at]
            x = as_pix(xs[j, pl.ds(row, nrows), :].astype(F32))
            a = gelu(dev * scale[:, at] + shift[:, at] + x)
            mid[pl.ds(row, nrows), at] = as_rows(a).astype(BF16)
            even = a.reshape(2, half, 2, VIEWS, 256)[0, :, 0]
            mid_even[pl.ds((0, geo.qb)[part] + half * i, half), :, at] = even
        z = nn(mid[pl.ds(row, nrows), :], w[...])
        put_phases(pre4[part], i, z.reshape(2, half, 2, VIEWS, chans))
        return carry + jnp.sum(as_pix(z), axis=0)

    io.ready()
    zero = jnp.zeros((VIEWS, chans), F32)
    sums = geo.loop(body, [zero, zero], io, io)
    mean4 = (rows_sum(sums[0] * lives[0]) + rows_sum(sums[1] * lives[1])) / nf[0]
    mids[...] = as_rows(mid_even[...]).astype(BF16)
    io.send(mids)
    sq = []
    for part in range(2):

        def dev2(i, carry, part=part):
            for k in range(4):
                d = pre4[part][k // 2, k % 2, i] - mean4
                carry = carry + jnp.sum(d * d, axis=0)
            return carry

        sq.append(lax.fori_loop(0, geo.parts[part][0] // 2, dev2, zero))
    stats[0:1] = mean4
    stats[1:2] = rows_sum(sq[0] * lives[0]) + rows_sum(sq[1] * lives[1])


def k_short(geo, io, me, nf, mids, w0, w1, side, stats):
    io.ready()
    chans = w0.shape[1]
    lives = [live_rows(me[1], chans), live_rows(me[2], chans)]
    for j, w in enumerate((w0, w1)):
        z = as_pix(nn(mids[...], w[...]))
        side[j] = z
        io.leave(j)
        mean, square = block_stats(geo, z, lives, nf[0])
        stats[j] = jnp.concatenate([mean, square], axis=0)


def k_stride(geo, io, me, nf, n4, pre4b, pre4s, sa, sb, gs, w, pre5, cols, stats, sb_act, ss_act):
    chans = pre4b.shape[-1]
    lives = [live_rows(me[1], chans), live_rows(me[2], chans)]
    mean, inv = merged(sa[...], sb[...], n4[1], n4[2])
    scale, shift = gs[0:1] * inv, gs[1:2]
    srcs, dsts = (pre4b, pre4s), (sb_act, ss_act)
    for part in range(2):

        def act(i, carry, part=part):
            for k in range(4):
                at = (k // 2, k % 2, i)
                dsts[part][at] = gelu((srcs[part][at] - mean) * scale + shift)
            return carry

        lax.fori_loop(0, geo.parts[part][0] // 2, act, 0)
    for r in range(3):
        for c in range(3):
            flats = []
            for part in range(2):
                half = geo.parts[part][0] // 2
                v = dsts[part][(r + 1) % 2, (c + 1) % 2]
                if c == 0:
                    v = side_shift(v, 1)
                if r == 0:
                    v = jnp.concatenate([jnp.zeros((1,) + v.shape[1:], F32), v[:-1]], axis=0)
                flats.append(v.reshape(half * half * VIEWS, chans))
            t = 3 * r + c
            cols[:, t * chans : (t + 1) * chans] = jnp.concatenate(flats, axis=0).astype(BF16)
    io.send(cols)
    io.ready()
    z = as_pix(nn(cols[...], w[...]))
    pre5[...] = z
    m5, s5 = block_stats(geo, z, lives, nf[0])
    stats[0:1] = m5
    stats[1:2] = s5


def k_widen(geo, io, me, nf, pre5, sa, sb, gs, w0, w1, st_side, pre6, act5, stats):
    chans = w0.shape[1]
    lives = [live_rows(me[1], chans), live_rows(me[2], chans)]
    mean, inv = merged(sa[...], sb[...], nf[1], nf[2])
    scale, shift = gs[0:1] * inv, gs[1:2]
    act5[...] = as_rows(gelu((pre5[...] - mean) * scale + shift)).astype(BF16)
    io.ready()
    for j, w in enumerate((w0, w1)):
        z = as_pix(nn(act5[...], w[...]))
        pre6[j] = z
        io.leave(j)
        m6, s6 = block_stats(geo, z, lives, nf[0])
        stats[j] = jnp.concatenate([m6, s6, st_side[j]], axis=0)


def k_total(geo, io, me, nf, pre6, side, sa, sb, gs, cb0, cb1, cs0, cs1, out_b, out_s, dt, sums):
    chans = pre6.shape[-1]
    lives = [live_rows(me[1], chans), live_rows(me[2], chans)]
    cots = ((cb0, cb1), (cs0, cs1))
    spans = ((0, geo.qb), (geo.qb, geo.px4))
    outs = (out_b, out_s)
    io.ready()
    for j in range(2):
        io.arrive(j)
        a, b, g = sa[j], sb[j], gs[j]
        m6, r6 = merged(a[0:2], b[0:2], nf[1], nf[2])
        ms, rs = merged(a[2:4], b[2:4], nf[1], nf[2])
        acc = [None, None, None]
        for part, (lo, hi) in enumerate(spans):
            d6 = pre6[j, lo:hi] - m6
            dd = side[j, lo:hi] - ms
            total = d6 * (g[0:1] * r6) + g[1:2] + (dd * (g[2:3] * rs) + g[3:4])
            live = lives[part]
            if j == 0:
                outs[part][...] = gelu(total) * live
            grad = gelu_slope(total) * (as_pix(cots[part][j][...].astype(F32)) * live)
            dt[j, lo:hi] = grad
            terms = [jnp.sum(v, axis=0) for v in (grad, grad * d6, grad * dd)]
            acc = [t if s is None else s + t for s, t in zip(acc, terms)]
        io.leave(j)
        if j == 0:
            io.send(out_b, out_s)
        sums[j] = jnp.concatenate(
            [rows_sum(acc[0]), rows_sum(acc[1]) * r6, rows_sum(acc[2]) * rs], axis=0
        )


def back_coefs(lives, s1, s2, inv, gain, count):
    c1 = gain * inv
    c2 = [live * (c1 * s1 / count) for live in lives]
    c3 = [live * (c1 * inv * s2 / count) for live in lives]
    return c1, c2, c3


def k_back_wide(geo, io, me, nf, dt, pre6, side, sa, sb, gs, ga, gb, w0, w1, part5, dz6, dzs, tot):
    chans = pre6.shape[-1]
    lives = [live_rows(me[1], chans), live_rows(me[2], chans)]
    total = nf[1] + nf[2]
    spans = ((0, geo.qb), (geo.qb, geo.px4))
    acc = None
    io.ready()
    for j, w in enumerate((w0, w1)):
        io.arrive(j)
        a, b, g = sa[j], sb[j], gs[j]
        s = ga[j] + gb[j]
        tot[j] = s
        m6, r6 = merged(a[0:2], b[0:2], nf[1], nf[2])
        ms, rs = merged(a[2:4], b[2:4], nf[1], nf[2])
        k1, k2, k3 = back_coefs(lives, s[0:1], s[1:2], r6, g[0:1], total)
        h1, h2, h3 = back_coefs(lives, s[0:1], s[2:3], rs, g[2:3], total)
        main, short = [], []
        for part, (lo, hi) in enumerate(spans):
            grad = dt[j, lo:hi]
            main.append(grad * k1 - k2[part] - (pre6[j, lo:hi] - m6) * k3[part])
            short.append(grad * h1 - h2[part] - (side[j, lo:hi] - ms) * h3[part])
        z6 = as_rows(jnp.concatenate(main, axis=0)).astype(BF16)
        dzs[j] = as_rows(jnp.concatenate(short, axis=0)).astype(BF16)
        io.leave(j)
        if j == 0:
            dz6[...] = z6
        d = nt(z6, w[...])
        acc = d if acc is None else acc + d
    part5[...] = as_pix(acc)


def k_back_act5(nf, mine, other, pre5, sa5, sb5, gs5, dt5, sums5):
    m5, r5 = merged(sa5[...], sb5[...], nf[1], nf[2])
    dev = pre5[...] - m5
    grad = gelu_slope(dev * (gs5[0:1] * r5) + gs5[1:2]) * (mine[...] + other[...])
    dt5[...] = grad
    sums5[0:1] = rows_sum(jnp.sum(grad, axis=0))
    sums5[1:2] = rows_sum(jnp.sum(grad * dev, axis=0)) * r5


def k_back_short(io, me, dzs, w0, w1, dms):
    io.ready()
    acc = None
    for j, w in enumerate((w0, w1)):
        d = nt(dzs[j], w[...])
        acc = d if acc is None else acc + d
    dms[...] = as_pix(acc).astype(BF16)


def k_back_stride(geo, io, me, nf, dt5, pre5, sa5, sb5, gs5, ga, gb, pre4b, pre4s, sa4, sb4, gs4, n4, w, dt4b, dt4s, dz5, sums4, tot, shifts):
    chans = pre5.shape[-1]
    lives = [live_rows(me[1], chans), live_rows(me[2], chans)]
    s = ga[...] + gb[...]
    tot[...] = s
    m5, r5 = merged(sa5[...], sb5[...], nf[1], nf[2])
    c1, c2, c3 = back_coefs(lives, s[0:1], s[1:2], r5, gs5[0:1], nf[1] + nf[2])
    spans = ((0, geo.qb), (geo.qb, geo.px4))
    imgs = []
    for part, (lo, hi) in enumerate(spans):
        half = geo.parts[part][0] // 2
        z = dt5[lo:hi] * c1 - c2[part] - (pre5[lo:hi] - m5) * c3[part]
        imgs.append(z.reshape(half, half, VIEWS, chans))

    def flat(moved):
        return jnp.concatenate([v.reshape(-1, chans) for v in moved], axis=0).astype(BF16)

    def up(v):
        return jnp.concatenate([v[1:], jnp.zeros((1,) + v.shape[1:], F32)], axis=0)

    shifts[0] = flat(imgs)
    dz5[...] = shifts[0]
    shifts[1] = flat([side_shift(v, -1) for v in imgs])
    shifts[2] = flat([up(v) for v in imgs])
    shifts[3] = flat([up(side_shift(v, -1)) for v in imgs])
    m4, r4 = merged(sa4[...], sb4[...], n4[1], n4[2])
    scale, off = gs4[0:1] * r4, gs4[1:2]
    io.ready()
    plan = {
        (0, 0): ((0, 4),),
        (0, 1): ((0, 5), (1, 3)),
        (1, 0): ((0, 7), (2, 1)),
        (1, 1): ((0, 8), (1, 6), (2, 2), (3, 0)),
    }
    t1, t2 = jnp.zeros((VIEWS, chans), F32), jnp.zeros((VIEWS, chans), F32)
    for (rp, cp), terms in plan.items():
        acc = None
        for k, t in terms:
            d = nt(shifts[k], w[t * chans : (t + 1) * chans, :])
            acc = d if acc is None else acc + d
        for part, (lo, hi) in enumerate(spans):
            half = geo.parts[part][0] // 2
            d = acc[lo * VIEWS : hi * VIEWS].reshape(half, half, VIEWS, chans)
            dev = (pre4b, pre4s)[part][rp, cp] - m4
            grad = gelu_slope(dev * scale + off) * d
            (dt4b, dt4s)[part][rp, cp] = grad
            t1 = t1 + jnp.sum(grad, axis=(0, 1))
            t2 = t2 + jnp.sum(grad * dev, axis=(0, 1))
    io.send(dt4b, dt4s)
    sums4[0:1] = rows_sum(t1)
    sums4[1:2] = rows_sum(t2) * r4


def k_back_narrow(geo, io, me, nf, dt4b, dt4s, pre4b, pre4s, sa4, sb4, gs4, ga, gb, pre3, xs, sa3, sb3, gs3, dms, dmo, w, dt3, dz4, sums3, tot):
    chans = w.shape[1]
    wide = w.shape[0]
    lives = [live_rows(me[1], chans), live_rows(me[2], chans)]
    s = ga[...] + gb[...]
    tot[...] = s
    m4, r4 = merged(sa4[...], sb4[...], nf[1], nf[2])
    c1, c2, c3 = back_coefs(lives, s[0:1], s[1:2], r4, gs4[0:1], nf[1] + nf[2])
    m3, r3 = merged(sa3[...], sb3[...], nf[1], nf[2])
    scale, off = gs3[0:1] * r3, gs3[1:2]
    dts, pres = (dt4b, dt4s), (pre4b, pre4s)

    def body(part, i, pix, npx, row, nrows, carry):
        half = geo.parts[part][0] // 2
        dev4 = get_phases(pres[part], i) - m4
        z = get_phases(dts[part], i) * c1 - c2[part] - dev4 * c3[part]
        z = z.reshape(nrows, chans).astype(BF16)
        dz4[pl.ds(row, nrows), :] = z
        at = pl.ds((0, geo.qb)[part] + half * i, half)
        t1, t2 = [], []
        for j in range(4):
            at_j = slice(256 * j, 256 * j + 256)
            d = nt(z, w[at_j, :]).reshape(2, half, 2, VIEWS, 256)
            even = d[0, :, 0] + (dms[at, :, at_j].astype(F32) + dmo[at, :, at_j].astype(F32))
            top = jnp.stack([even, d[0, :, 1]], axis=1)
            d = jnp.concatenate([as_pix_rows(top), as_pix_rows(d[1])], axis=0)
            dev = pre3[pl.ds(pix, npx), :, at_j] - m3[:, at_j]
            x = as_pix(xs[j, pl.ds(row, nrows), :].astype(F32))
            grad = gelu_slope(dev * scale[:, at_j] + off[:, at_j] + x) * d
            dt3[pl.ds(row, nrows), at_j] = as_rows(grad).astype(BF16)
            t1.append(jnp.sum(grad, axis=0))
            t2.append(jnp.sum(grad * dev, axis=0))
        return carry[0] + jnp.concatenate(t1, axis=1), carry[1] + jnp.concatenate(t2, axis=1)

    io.ready()
    zero = jnp.zeros((VIEWS, wide), F32)
    (a1, a2), (b1, b2) = geo.loop(body, [(zero, zero), (zero, zero)], io, io)
    sums3[0:1] = rows_sum(a1 + b1)
    sums3[1:2] = rows_sum(a2 + b2) * r3


def k_back_expand(geo, io, me, nf, dt3, pre3, sa3, sb3, gs3, ga, gb, pre2, sa2, sb2, gs2, w, dt2, dz3, dt3q, sums2, tot, zbuf_b, zbuf_s):
    wide, chans = w.shape[1], w.shape[0]
    lives = [live_rows(me[1], wide), live_rows(me[2], wide)]
    s = ga[...] + gb[...]
    tot[...] = s
    m3, r3 = merged(sa3[...], sb3[...], nf[1], nf[2])
    c1, c2, c3 = back_coefs(lives, s[0:1], s[1:2], r3, gs3[0:1], nf[1] + nf[2])
    m2, r2 = merged(sa2[...], sb2[...], nf[1], nf[2])
    scale, off = gs2[0:1] * r2, gs2[1:2]
    mine = pl.ds(pl.multiple_of(me[0] * 256, 256), 256)

    def body(part, i, pix, npx, row, nrows, carry):
        zbuf = (zbuf_b, zbuf_s)[part]
        dt3q[pl.ds(row, nrows), :] = dt3[pl.ds(row, nrows), mine]
        for j in range(4):
            at = slice(256 * j, 256 * j + 256)
            z = (
                as_pix(dt3[pl.ds(row, nrows), at].astype(F32)) * c1[:, at]
                - c2[part][:, at]
                - (pre3[pl.ds(pix, npx), :, at] - m3[:, at]) * c3[part][:, at]
            )
            zbuf[:, at] = as_rows(z).astype(BF16)
        dz3[pl.ds(row, nrows), :] = zbuf[:, mine]
        d = as_pix(nt(zbuf[...], w[...]))
        dev = pre2[pl.ds(pix, npx)] - m2
        grad = gelu_slope(dev * scale + off) * d
        dt2[pl.ds(pix, npx)] = grad
        return carry[0] + jnp.sum(grad, axis=0), carry[1] + jnp.sum(grad * dev, axis=0)

    io.ready()
    zero = jnp.zeros((VIEWS, chans), F32)
    (a1, a2), (b1, b2) = geo.loop(body, [(zero, zero), (zero, zero)], io, io)
    sums2[0:1] = rows_sum(a1 + b1)
    sums2[1:2] = rows_sum(a2 + b2) * r2


def k_back_mix(geo, io, me, nf, dt2, pre2, sa2, sb2, gs2, ga, gb, pre1, sa1, sb1, gs1, w, dt1, dz2, sums1, tot, zb, zs):
    chans = pre2.shape[-1]
    lives = [live_rows(me[1], chans), live_rows(me[2], chans)]
    s = ga[...] + gb[...]
    tot[...] = s
    m2, r2 = merged(sa2[...], sb2[...], nf[1], nf[2])
    c1, c2, c3 = back_coefs(lives, s[0:1], s[1:2], r2, gs2[0:1], nf[1] + nf[2])
    m1, r1 = merged(sa1[...], sb1[...], nf[1], nf[2])
    scale, off = gs1[0:1] * r1, gs1[1:2]
    bufs = (zb, zs)
    for part, (side, _) in enumerate(geo.parts):
        zero_edges(bufs[part], side * VIEWS)

    def back(part, i, pix, npx, row, nrows, carry):
        z = dt2[pl.ds(pix, npx)] * c1 - c2[part] - (pre2[pl.ds(pix, npx)] - m2) * c3[part]
        dz2[pl.ds(row, nrows), :] = as_rows(z).astype(BF16)
        side = geo.parts[part][0]
        at = pl.multiple_of(side * VIEWS + i * nrows, 16)
        store_shifted(bufs[part], at, nrows, side, z, (2, 1, 0))
        return carry

    geo.loop(back, [0, 0], io)
    io.send(dz2)
    io.ready()

    def dots(part, i, pix, npx, row, nrows, carry):
        acc = None
        for r in range(3):
            at = pl.multiple_of(i * nrows + (2 - r) * (nrows // 2), 16)
            taps = w[3 * r : 3 * r + 3].reshape(3 * chans, chans)
            d = nn(bufs[part][pl.ds(at, nrows), :], taps)
            acc = d if acc is None else acc + d
        dev = pre1[pl.ds(pix, npx)] - m1
        grad = gelu_slope(dev * scale + off) * as_pix(acc)
        dt1[pl.ds(pix, npx)] = grad
        return carry[0] + jnp.sum(grad, axis=0), carry[1] + jnp.sum(grad * dev, axis=0)

    zero = jnp.zeros((VIEWS, chans), F32)
    (a1, a2), (b1, b2) = geo.loop(dots, [(zero, zero), (zero, zero)], None, io)
    sums1[0:1] = rows_sum(a1 + b1)
    sums1[1:2] = rows_sum(a2 + b2) * r1


def k_back_reduce(geo, io, me, nf, dt1, pre1, sa1, sb1, gs1, ga, gb, dt3q, wt, gxb, gxs, dz1, tot):
    chans = pre1.shape[-1]
    lives = [live_rows(me[1], chans), live_rows(me[2], chans)]
    s = ga[...] + gb[...]
    tot[...] = s
    m1, r1 = merged(sa1[...], sb1[...], nf[1], nf[2])
    c1, c2, c3 = back_coefs(lives, s[0:1], s[1:2], r1, gs1[0:1], nf[1] + nf[2])
    io.ready()

    def body(part, i, pix, npx, row, nrows, carry):
        z = dt1[pl.ds(pix, npx)] * c1 - c2[part] - (pre1[pl.ds(pix, npx)] - m1) * c3[part]
        z = as_rows(z).astype(BF16)
        dz1[pl.ds(row, nrows), :] = z
        g = as_pix(nn(z, wt[me[0]])) + as_pix(dt3q[pl.ds(row, nrows), :].astype(F32))
        (gxb, gxs)[part][pl.ds(pix - (0, geo.pb)[part], npx)] = g
        return carry

    geo.loop(body, [0, 0], io, io)


def k_dw_wide(act5, dz6, mids, dzs, dwide, dshort):
    dwide[...] = tn(act5[...], dz6[...]).astype(BF16)
    dshort[...] = tn(mids[...], dzs[0]).astype(BF16)


def lane_blocks(v):
    return [v[:, 128 * b : 128 * b + 128] for b in range(v.shape[1] // 128)]


def put_halves(me, full, keep, send):
    bit = me[3] & 1
    keep[...] = full[bit].astype(BF16)
    send[...] = full[1 - bit].astype(BF16)


def k_dw_stride(me, cols, dz5, keep, send, full):
    mine = pl.ds(pl.multiple_of(me[0] * 128, 128), 128)
    z = dz5[:, mine]
    rows = full.shape[1]
    for t in range(9):
        dw = tn(cols[:, t * 512 : (t + 1) * 512], z)
        lo = 0
        while lo < 512:
            half, at = divmod(t * 512 + lo, rows)
            n = min(512 - lo, rows - at)
            full[half, at : at + n] = dw[lo : lo + n]
            lo += n
    put_halves(me, full, keep, send)


def k_dw_mid(me, mid, dz4, act2, dz3, keep, send, full):
    mine = pl.ds(pl.multiple_of(me[0] * 128, 128), 128)
    blocks = [tn(mid[...], dz4[:, mine])] + lane_blocks(tn(act2[...], dz3[...]))
    flat = jnp.concatenate(blocks, axis=0)
    full[...] = flat.reshape(full.shape)
    put_halves(me, full, keep, send)


def k_dw_mix(geo, me, wb, ws, dz2, out, full):
    mine = pl.ds(pl.multiple_of(me[0] * 64, 64), 64)
    nb, ns = geo.pb * VIEWS, geo.ps * VIEWS
    at = 0
    for r in range(3):
        ob, os = r * geo.hb * VIEWS, r * geo.hs * VIEWS
        full[...] = tn(dz2[0:nb, :], wb[ob : ob + nb, :]) + tn(
            dz2[nb : nb + ns, :], ws[os : os + ns, :]
        )
        for block in lane_blocks(full[mine, :]):
            out[at : at + 64] = block
            at += 64


def k_dw_reduce(geo, me, x0b, x1b, x2b, x3b, x0s, x1s, x2s, x3s, dz1, dmix, keep, send, part, flat):
    mine = pl.ds(pl.multiple_of(me[0] * 64, 64), 64)
    nb = geo.pb * VIEWS
    base = dmix.shape[0]
    flat[0:base] = dmix[...]
    for p, (b, s) in enumerate(((x0b, x0s), (x1b, x1s), (x2b, x2s), (x3b, x3s))):
        part[...] = tn(dz1[0:nb, :], b[...]) + tn(dz1[nb:, :], s[0 : geo.ps * VIEWS, :])
        for n, block in enumerate(lane_blocks(part[mine, :])):
            flat[pl.ds(pl.multiple_of(base + (me[0] ^ p) * 128 + 64 * n, 64), 64)] = block
    half = keep.shape[0]
    bit = me[3] & 1
    keep[...] = flat[pl.ds(pl.multiple_of(bit * half, 8), half)].astype(BF16)
    send[...] = flat[pl.ds(pl.multiple_of((1 - bit) * half, 8), half)].astype(BF16)


def k_sum_split(shift, size, n_in, me, *refs):
    total = refs[n_in]
    acc = refs[0][...].astype(F32)
    for r in refs[1:n_in]:
        acc = acc + r[...].astype(F32)
    total[...] = acc
    where = (me[3] >> shift) & (size - 1)
    for m, out in enumerate(refs[n_in + 1 :]):
        out[...] = total[where ^ m].astype(BF16)


def k_sum(n_in, *refs):
    acc = refs[0][...].astype(F32)
    for r in refs[1:n_in]:
        acc = acc + r[...].astype(F32)
    refs[n_in][...] = acc.astype(BF16)


def k_join(shift, size, me, *refs):
    where = (me[3] >> shift) & (size - 1)
    for m in range(size):
        refs[size][where ^ m] = refs[m][...]


def k_unpack(plan, me, a, b, *refs):
    full = refs[-1]
    bit = me[3] & 1
    full[bit] = a[...].reshape(full.shape[1:]).astype(F32)
    full[1 - bit] = b[...].reshape(full.shape[1:]).astype(F32)
    flat = full[...].reshape(2 * full.shape[1], 128)
    at = 0
    for out, (lead, rows, cols) in zip(refs, plan):
        for t in range(lead):
            for block in range(cols // 128):
                v = flat[at : at + rows]
                lanes = slice(128 * block, 128 * block + 128)
                if lead > 1:
                    out[t, :, lanes] = v
                else:
                    out[:, lanes] = v
                at += rows


def per_device(
    ni,
    nc,
    x_big,
    x_small,
    cot_big,
    cot_small,
    counts,
    w_reduce,
    w_mix,
    w_expand,
    w_narrow,
    w_stride,
    w_widen,
    w_short,
    gain_mid3,
    shift_mid3,
    gain_out3,
    shift_out3,
    gain_mid4,
    shift_mid4,
    gain_out4,
    shift_out4,
):
    assert nc == 4 and ni >= 8 and x_big.shape[0] == VIEWS and x_small.shape[0] == VIEWS
    geo = Geo(x_big.shape[1], x_small.shape[1])
    img = lax.axis_index("img")
    q = lax.axis_index("ch").astype(jnp.int32)
    levels = ni.bit_length() - 1
    me, nf3, cnt3, nf4, cnt4 = call(
        "counts",
        functools.partial(k_counts, ni, ((geo.pb, geo.ps), (geo.qb, geo.qs))),
        [(counts, SMEM)],
        [(sds((4,), jnp.int32), SMEM)]
        + [(sds((n,)), SMEM) for n in (3, 8 * (levels - 2)) * 2],
        slack=1,
    )

    smem = [(me, SMEM)]

    def over_img(v, k):
        return lax.ppermute(v, "img", [(i, i ^ (1 << k)) for i in range(ni)])

    def over_ch(v, k):
        return lax.ppermute(v, "ch", [(i, i ^ k) for i in range(nc)])

    rounds, at = [], 0
    while at < levels:
        rounds.append((at, min(2, levels - at) if at == 0 else 1))
        at += rounds[-1][1]

    def peers(v, shift, bits):
        out = []
        for m in range(1, 1 << bits):
            out.append(lax.ppermute(v, "img", [(i, i ^ (m << shift)) for i in range(ni)]))
        return out

    def sync(v, combine, wait=(), free=()):
        wait, free = dict(wait), dict(free)
        freed = []
        for k, (shift, bits) in enumerate(rounds):
            if k in wait:
                v = lax.optimization_barrier((v,) + tuple(wait[k]))[0]
            others = peers(v, shift, bits)
            if k in free:
                held = lax.optimization_barrier(tuple(others) + tuple(free[k]))
                others = list(held[: len(others)])
                freed += held[len(others) :]
            if k == len(rounds) - 1:
                return (v, others[0]) + ((freed,) if free else ())
            v = combine(k, [v] + others)

    def sync_stats(stats, cnt):
        def combine(k, arrays):
            (v,) = call(
                "merge",
                functools.partial(k_merge, 8 * k, len(arrays)),
                [(cnt, SMEM)] + vm(*arrays),
                [sds(stats.shape)],
                slack=1,
            )
            return v

        return sync(stats, combine)

    def sync_sums(sums, wait=(), free=()):
        def combine(k, arrays):
            (v,) = call("add", functools.partial(k_add, len(arrays)), vm(*arrays), [sds(sums.shape)], slack=1)
            return v

        return sync(sums, combine, wait, free)

    groups = [(0, 1)]
    while groups[-1][0] + groups[-1][1] < levels:
        done = groups[-1][0] + groups[-1][1]
        groups.append((done, min(2, levels - done)))

    def to_peers(parts, group):
        shift, bits = group
        out = []
        for m in range(1, 1 << bits):
            perm = [(i, i ^ (m << shift)) for i in range(ni)]
            out.append(lax.ppermute(parts[m if len(parts) > 1 else 0], "img", perm))
        return out

    def sum_split(name, arrays, group):
        shift, bits = group
        size = 1 << bits
        shape = arrays[0].shape
        view = (size, shape[0] // size) + shape[1:]
        return call(
            name,
            functools.partial(k_sum_split, shift, size, len(arrays)),
            smem + vm(*[a.reshape(view) for a in arrays]),
            [sds(view[1:], BF16)] * size,
            [pltpu.VMEM(view, F32)],
            order=True,
        )

    def join(name, parts, group):
        shift, bits = group
        size = 1 << bits
        (full,) = call(
            name,
            functools.partial(k_join, shift, size),
            smem + vm(*parts),
            [sds((size,) + parts[0].shape, BF16)],
        )
        return full.reshape((-1,) + parts[0].shape[1:])

    def reduce_parts(name, parts):
        arrays = [parts[0]] + to_peers(parts, groups[1])
        for at, group in enumerate(groups[2:]):
            parts = sum_split(name + "_split%d" % at, arrays, group)
            arrays = [parts[0]] + to_peers(parts, group)
        return arrays

    def sum_parts(name, arrays):
        (part,) = call(
            name + "_sum",
            functools.partial(k_sum, len(arrays)),
            vm(*arrays),
            [sds(arrays[0].shape, BF16)],
        )
        return part

    def gather_parts(name, part, received):
        full = join(name + "_join", [part] + received, groups[-1])
        for at, group in reversed(list(enumerate(groups[1:-1]))):
            full = join(name + "_join%d" % at, [full] + to_peers([full], group), group)
        return full

    def quarters(v):
        p1 = over_ch(v, 1)
        p2 = over_ch(v, 2)
        return [v, p1, p2, over_ch(p2, 1)]

    def after(marker, *arrays):
        return list(lax.optimization_barrier((marker,) + arrays))

    def sent(v):
        return [v, over_ch(v, 1), over_ch(v, 2)]

    def passed_on(g):
        return g + [over_ch(g[2], 1)]

    def in_order(pieces):
        full = jnp.stack(pieces)
        return jnp.take(full, jnp.arange(4, dtype=jnp.int32) ^ q, axis=0)

    def rows_of(v):
        return jnp.transpose(v, (1, 2, 0, 3)).reshape(-1, v.shape[3])

    def chips(v):
        return [v, over_ch(v, 2)]

    def tie(first, *later):
        return list(lax.optimization_barrier(tuple(first) + tuple(later))[len(first) :])

    m3, c3 = 4 * w_reduce.shape[1], w_reduce.shape[0]
    m4, c4q = w_widen.shape
    first = [rows_of(x_small)]
    first.append(jnp.transpose(w_mix, (0, 1, 3, 2)).reshape(-1, m3))
    first += [w_reduce.T[:, j * m3 : (j + 1) * m3] for j in range(c3 // m3)]
    mix_at, reduce_at = first[0].shape[0], first[0].shape[0] + first[1].shape[0]
    xb, xsm = quarters(rows_of(x_big)), quarters(jnp.concatenate(first))
    held = (gain_mid3, shift_mid3, gain_out3, shift_out3, gain_mid4, shift_mid4, gain_out4, shift_out4)
    params = quarters(jnp.concatenate([v.reshape(-1) for v in held]).reshape(-1, 128))

    def split(flat):
        cuts, at = [], 0
        for v in held:
            cuts.append(flat[..., at : at + v.size].reshape(flat.shape[:-1] + v.shape))
            at += v.size
        return cuts

    gm3, sm3, go3, so3, gm4, sm4, _, _ = split(in_order(params).reshape(4, -1))

    def pair(g, s):
        return jnp.stack([g.reshape(-1), s.reshape(-1)])

    gs1, gs2 = pair(gm3[:, 0], sm3[:, 0]), pair(gm3[:, 1], sm3[:, 1])
    gs3 = pair(go3, so3)
    gs4, gs5 = pair(gm4[:, 0], sm4[:, 0]), pair(gm4[:, 1], sm4[:, 1])
    wide = [split(v.reshape(-1))[6:] for v in (params[0], params[2])]
    gs6 = jnp.stack([jnp.stack([g[0], h[0], g[1], h[1]]) for g, h in wide])

    n3, n4 = [(nf3, SMEM)], [(nf4, SMEM)]

    def k(fn):
        return functools.partial(fn, geo)

    hb, hs = geo.hb, geo.hs
    sb4, ss4 = (2, 2, hb // 2, hb // 2, VIEWS, m4), (2, 2, hs // 2, hs // 2, VIEWS, m4)
    wb_shape, ws_shape = ((hb + 2) * hb * VIEWS, 3 * m3), ((hs + 2) * hs * VIEWS, 3 * m3)

    def flow(kind, *arrays):
        return [(a, Flow(kind)) for a in arrays]

    def out(kind, shape, dtype=F32):
        return (sds(shape, dtype), Flow(kind))

    x_all = [(xb + xsm, Flow("x"))]
    w_in, w_ahead, w_back = [
        [(xsm, Flow(kind, base))]
        for kind, base in (("w_in", reduce_at), ("w_ahead", mix_at), ("w_back", mix_at))
    ]
    run = functools.partial(call, geo=geo)
    px1, px3, px4 = (geo.px, VIEWS, m3), (geo.px, VIEWS, c3), (geo.px4, VIEWS, m4)

    pre1, st = run(
        "reduce",
        k(k_reduce),
        smem + n3 + x_all + w_in,
        [fast(px1), sds((2, m3))],
    )
    def blocks128(v):
        return [v[:, 128 * b : 128 * b + 128] for b in range(v.shape[1] // 128)]

    st, w_mid = after(st, jnp.concatenate(blocks128(w_expand) + blocks128(w_narrow)))
    w_mid = sent(w_mid)
    a1, b1 = sync_stats(st, cnt3)
    pre2, winb, wins, st, keep1 = run(
        "mix",
        k(k_mix),
        smem + n3 + vm(pre1, a1, b1, gs1) + w_ahead,
        [
            fast(px1),
            out("all", wb_shape, BF16),
            out("all", ws_shape, BF16),
            sds((2, m3)),
            (sds(px1), Keep(2)),
        ],
    )
    st, w_mid[2], wst = after(st, w_mid[2], w_stride.reshape(-1, w_stride.shape[3]))
    w_mid, wst = passed_on(w_mid), sent(wst)
    w_expand_all = [(w_mid, Flow("w", 0, (m3, c3)))]
    w_narrow_all = [(w_mid, Flow("w", m3 * (c3 // 4 // 128), (c3, m4)))]
    a2, b2 = sync_stats(st, cnt3)
    pre3, act2, st, keep2 = run(
        "expand",
        k(k_expand),
        smem + n3 + vm(pre2, a2, b2, gs2) + w_expand_all,
        [
            fast(px3),
            out("rows", (geo.rows, m3), BF16),
            sds((2, c3)),
            (sds(px1), Keep(2)),
        ],
    )
    last_in = jnp.concatenate([w_short, w_widen, rows_of(cot_big), rows_of(cot_small)])
    st, wst[2], last_in = after(st, wst[2], last_in)
    wst, last_in = passed_on(wst), chips(last_in)
    a3, b3 = sync_stats(st, cnt3)
    pre4b, pre4s, mid, mids, st, keep3 = run(
        "narrow",
        k(k_narrow),
        smem + n3 + vm(pre3) + x_all + vm(a3, b3, gs3) + w_narrow_all,
        [
            fast(sb4),
            fast(ss4),
            out("rows", (geo.rows, c3), BF16),
            fast((geo.rows4, c3), BF16),
            sds((2, m4)),
            (sds(px3), Keep(2)),
        ],
        [pltpu.VMEM((geo.px4, VIEWS, c3), F32)],
    )
    a4, b4 = sync_stats(st, cnt3)
    w_stride_all = [(wst, Flow("w", 0, (9 * m4, m4)))]
    pre5, cols, st, keep4b, keep4s = run(
        "stride",
        k(k_stride),
        smem + n4 + n3 + vm(pre4b, pre4s, a4, b4, gs4) + w_stride_all,
        [
            sds(px4),
            out("all", (geo.rows4, 9 * m4), BF16),
            sds((2, m4)),
            (sds(sb4), Keep(3)),
            (sds(ss4), Keep(4)),
        ],
        [pltpu.VMEM(sb4, F32), pltpu.VMEM(ss4, F32)],
    )
    st, last_in[1], mids = after(st, last_in[1], mids)
    at_w, at_b, at_s = c3, c3 + m4, c3 + m4 + geo.qb * VIEWS
    wsh = [(v, Flow("part", 0, (c3, c4q))) for v in last_in]
    wwi = [(v, Flow("part", at_w, (m4, c4q))) for v in last_in]
    cots = [(v, Flow("part", at_b, (geo.qb * VIEWS, c4q))) for v in last_in]
    cots += [(v, Flow("part", at_s, (geo.qs * VIEWS, c4q))) for v in last_in]
    a5, b5 = sync_stats(st, cnt4)
    side, st_side = run(
        "short",
        k(k_short),
        smem + n4 + vm(mids) + wsh,
        [fast((2, geo.px4, VIEWS, c4q)), sds((2, 2, c4q))],
    )
    pre6, act5, st = run(
        "widen",
        k(k_widen),
        smem + n4 + vm(pre5, a5, b5, gs5) + wwi + vm(st_side),
        [
            fast((2, geo.px4, VIEWS, c4q)),
            sds((geo.rows4, m4), BF16),
            sds((2, 4, c4q)),
        ],
    )
    a6, b6 = sync_stats(st, cnt4)
    out_b, out_s, dt6, sums = run(
        "total",
        k(k_total),
        smem + n4 + vm(pre6, side, a6, b6, gs6) + cots,
        [
            out("all", (geo.qb, VIEWS, c4q)),
            out("all", (geo.qs, VIEWS, c4q)),
            fast((2, geo.px4, VIEWS, c4q)),
            sds((2, 3, c4q)),
        ],
    )
    ga6, gb6 = sync_sums(sums)
    part5, dz6, dzs, t6 = run(
        "back_wide",
        k(k_back_wide),
        smem
        + n4
        + vm(dt6, pre6, side, a6, b6, gs6, ga6, gb6)
        + wwi,
        [
            sds(px4),
            sds((geo.rows4, c4q), BF16),
            sds((2, geo.rows4, c4q), BF16),
            sds((2, 3, c4q)),
        ],
    )
    other5 = over_ch(part5, 1)
    dt5, sums = call(
        "back_act5",
        k_back_act5,
        n4 + vm(part5, other5, pre5, a5, b5, gs5),
        [sds(px4), sds((2, m4))],
    )
    (dms,) = run(
        "back_short", k_back_short, smem + vm(dzs) + wsh, [sds((geo.px4, VIEWS, c3), BF16)]
    )
    dmo = over_ch(dms, 1)
    dwide, dshort = call(
        "dw_wide",
        k_dw_wide,
        vm(act5, dz6, mids, dzs),
        [sds((m4, c4q), BF16), sds((c3, c4q), BF16)],
    )
    ga5, gb5, (dwide, dshort) = sync_sums(sums, free={0: [dwide, dshort]})
    dt4b, dt4s, dz5, sums, t5 = run(
        "back_stride",
        k(k_back_stride),
        smem
        + n4
        + vm(dt5, pre5, a5, b5, gs5, ga5, gb5)
        + flow("all", keep4b, keep4s)
        + vm(a4, b4, gs4)
        + n3
        + w_stride_all,
        [fast(sb4), fast(ss4), sds((geo.rows4, m4), BF16), sds((2, m4)), sds((2, m4))],
        [pltpu.VMEM((4, geo.rows4, m4), BF16)],
    )
    last = len(rounds) - 1

    def halves(rows):
        return [sds((rows // 2, 128), BF16)] * 2, pltpu.VMEM((2, rows // 2, 128), F32)

    outs, full = halves(9 * m4)
    own2, send2 = call("dw_stride", k_dw_stride, smem + vm(cols, dz5), outs, [full])
    ga4, gb4, (send2,) = sync_sums(sums, free={0: [send2]})
    recv2 = over_img(send2, 0)
    dt3, dz4, sums, t4 = run(
        "back_narrow",
        k(k_back_narrow),
        smem
        + n3
        + vm(dt4b, dt4s)
        + flow("big", keep4b)
        + flow("small", keep4s)
        + vm(a4, b4, gs4, ga4, gb4)
        + flow("px", keep3)
        + x_all
        + vm(a3, b3, gs3, dms, dmo)
        + w_narrow_all,
        [
            fast((geo.rows, c3), BF16),
            out("rows", (geo.rows, m4), BF16),
            sds((2, c3)),
            sds((2, m4)),
        ],
    )
    parts2 = sum_split("stride_split", [own2, recv2], groups[1])
    ga3, gb3, parts = sync_sums(sums, wait={0: [recv2]}, free={last: parts2[1:]})
    arrays2 = reduce_parts("stride", parts2[:1] + parts)
    dt2, dz3, dt3q, sums, t3 = run(
        "back_expand",
        k(k_back_expand),
        smem
        + n3
        + vm(dt3)
        + flow("px", keep3)
        + vm(a3, b3, gs3, ga3, gb3)
        + flow("px", keep2)
        + vm(a2, b2, gs2)
        + w_expand_all,
        [
            fast(px1),
            out("rows", (geo.rows, c3 // 4), BF16),
            out("rows", (geo.rows, c3 // 4), BF16),
            sds((2, m3)),
            sds((2, c3)),
        ],
        [
            pltpu.VMEM((2 * hb * VIEWS, c3), BF16),
            pltpu.VMEM((2 * hs * VIEWS, c3), BF16),
        ],
    )
    part2 = sum_parts("stride", arrays2)
    rows_mid = c3 + (c3 // 4 // 128) * m3
    outs, full = halves(rows_mid)
    own3, send3 = call("dw_mid", k_dw_mid, smem + vm(mid, dz4, act2, dz3), outs, [full])
    ga2, gb2, (send3, part2) = sync_sums(
        sums, wait={0: arrays2[1:]}, free={0: [send3], last: [part2]}
    )
    recv3 = over_img(send3, 0)
    back2 = to_peers([part2], groups[-1])
    dt1, dz2, sums, t2 = run(
        "back_mix",
        k(k_back_mix),
        smem
        + n3
        + vm(dt2)
        + flow("px", keep2)
        + vm(a2, b2, gs2, ga2, gb2)
        + flow("px", keep1)
        + vm(a1, b1, gs1)
        + w_back,
        [fast(px1), out("all", (geo.rows, m3), BF16), sds((2, m3)), sds((2, m3))],
        [pltpu.VMEM(wb_shape, BF16), pltpu.VMEM(ws_shape, BF16)],
    )
    join2 = gather_parts("stride", part2, back2)
    parts3 = sum_split("mid_split", [own3, recv3], groups[1])
    mix_rows = 9 * m3 // 128 * (m3 // 4)
    (dmix,) = call(
        "dw_mix",
        k(k_dw_mix),
        smem + vm(winb, wins, dz2),
        [sds((mix_rows, 128))],
        [pltpu.VMEM((m3, 3 * m3), F32)],
    )
    ga1, gb1, (join2, *parts) = sync_sums(
        sums, wait={0: back2 + [recv3]}, free={0: [join2], last: parts3[1:]}
    )
    other2 = over_img(join2, 0)
    arrays3 = reduce_parts("mid", parts3[:1] + parts)
    gxb, gxs, dz1, t1 = run(
        "back_reduce",
        k(k_back_reduce),
        smem
        + n3
        + vm(dt1)
        + flow("px", keep1)
        + vm(a1, b1, gs1, ga1, gb1)
        + flow("rows", dt3q)
        + w_in,
        [
            out("big_px", (geo.pb, VIEWS, c3 // 4)),
            out("small_px", (geo.ps, VIEWS, c3 // 4)),
            sds((geo.rows, m3), BF16),
            sds((2, m3)),
        ],
    )
    rows_last = mix_rows + c3 // 128 * (m3 // 4)
    outs, _ = halves(rows_last)
    dmix_late, *arrays3[1:] = after(dmix, *arrays3[1:])
    own4, send4 = call(
        "dw_reduce",
        k(k_dw_reduce),
        smem + vm(*xb, *xsm, dz1, dmix_late),
        outs,
        [pltpu.VMEM((m3, c3 // 4), F32), pltpu.VMEM((rows_last, 128), F32)],
    )
    recv4 = over_img(send4, 0)
    part3 = sum_parts("mid", arrays3)
    parts4 = sum_split("last_split", [own4, recv4], groups[1])
    join3 = gather_parts("mid", part3, to_peers([part3], groups[-1]))
    other3 = over_img(join3, 0)
    arrays4 = reduce_parts("last", parts4)
    part4 = sum_parts("last", arrays4)
    join4 = gather_parts("last", part4, to_peers([part4], groups[-1]))
    other4 = over_img(join4, 0)

    def unpack(name, a, b, plan):
        shapes = [((lead,) if lead > 1 else ()) + (rows, cols) for lead, rows, cols in plan]
        return call(
            name,
            functools.partial(k_unpack, plan),
            smem + vm(a, b),
            [sds(shape) for shape in shapes],
            [pltpu.VMEM((2,) + a.shape, F32)],
        )

    (dstride,) = unpack("out_stride", join2, other2, [(1, 9 * m4, 128)])
    dnarrow, dexpand = unpack("out_mid", join3, other3, [(1, c3, m4 // 4), (1, m3, c3 // 4)])
    dmix, dreduce = unpack(
        "out_last", join4, other4, [(3, m3 // 4, 3 * m3), (1, m3 // 4, c3)]
    )
    dwide, dshort = [v.astype(F32) for v in lax.psum((dwide, dshort), "img")]

    def views_first(v, side):
        return jnp.transpose(v.reshape(side, side, VIEWS, v.shape[2]), (2, 0, 1, 3))

    def own(v):
        n = v.shape[0] // 4
        return lax.dynamic_slice_in_dim(v, q * n, n, 0)

    t6 = t6[0]
    return (
        views_first(out_b, hb // 2),
        views_first(out_s, hs // 2),
        views_first(gxb, hb),
        views_first(gxs, hs),
        dreduce.T,
        jnp.transpose(dmix.reshape(3, m3 // 4, 3, m3), (0, 2, 3, 1)),
        dexpand,
        dnarrow,
        dstride.reshape(3, 3, m4, m4 // 4),
        dwide,
        dshort,
        jnp.stack([own(t1[1]), own(t2[1])]),
        jnp.stack([own(t1[0]), own(t2[0])]),
        own(t3[1]),
        own(t3[0]),
        jnp.stack([own(t4[1]), own(t5[1])]),
        jnp.stack([own(t4[0]), own(t5[0])]),
        jnp.stack([t6[1], t6[2]]),
        jnp.stack([t6[0], t6[0]]),
    )


def solution(mesh):
    act = P("img", None, None, "ch")
    flat, taps, vec = P(None, "ch"), P(None, None, None, "ch"), P("ch")
    in_specs = (act,) * 4 + (P(), flat, taps, flat, flat, taps, flat, flat)
    in_specs += (flat, flat, vec, vec, flat, flat, flat, flat)
    out_specs = (act,) * 4 + (flat, taps, flat, flat, taps, flat, flat)
    out_specs += (flat, flat, vec, vec, flat, flat, flat, flat)
    return jax.shard_map(
        functools.partial(per_device, mesh.shape["img"], mesh.shape["ch"]),
        mesh=mesh,
        in_specs=in_specs,
        out_specs=out_specs,
        check_vma=False,
    )
```

time: 690 us -> 421 us (0.61)
  waiting for transfers between devices: 327 us -> 103 us
  Pallas kernels: 198 us -> 150 us
  starting transfers between devices: 71.1 us -> 102 us
  local copies, waits for them, and re-layouts: 49.7 us -> 32.5 us
  between operations: 23.7 us -> 15.4 us
    psum x1, waiting for transfers between devices: 240 us -> 0.01 us  [per_device(): dwide, dshort = [v.astype(F32) for v in lax.psum((dwide, dshort), 'img')]]
    ppermute x0 -> x66, starting transfers between devices: none -> 85.2 us  [the longest x48 59.5 us: peers(): out.append(lax.ppermute(v, 'img', [(i, i ^ m << shift) for i in range(ni)]))]
    ppermute x0 -> x66, waiting for transfers between devices: none -> 67.1 us  [the longest x48 61.4 us: peers(): out.append(lax.ppermute(v, 'img', [(i, i ^ m << shift) for i in range(ni)]))]
    ppermute x36 -> x6, waiting for transfers between devices: 59 us -> 5.52 us  [over_img(): return lax.ppermute(v, 'img', [(i, i ^ 1 << k) for i in range(ni)])]
    pallas_call x25 -> x46, Pallas kernels: 198 us -> 150 us  [call(): pl.pallas_call(body, out_shape=out_shapes, in_specs=specs, out_specs=out_...]
    ppermute x36 -> x6, starting transfers between devices: 53.7 us -> 7.45 us  [over_img(): return lax.ppermute(v, 'img', [(i, i ^ 1 << k) for i in range(ni)])]
    unnamed x222 -> x100, local copies, waits for them, and re-layouts: 40 us -> 26.5 us
    ppermute x36 -> x18, starting transfers between devices: 17.4 us -> 9.85 us  [over_ch(): return lax.ppermute(v, 'ch', [(i, i ^ k) for i in range(nc)])]
  transfers between devices with their start and end apart: 73 -> 91, of which waited for: 34 -> 43; matrix products, arithmetic and copies ran while one was open for 3% -> 5% of each run, Pallas kernels for 13% -> 31%
where the time goes in v2:
time: 421 us; the launch traced here: 413 us
  Pallas kernels  150 us (36%)
  waiting for transfers between devices  103 us (24%)
  starting transfers between devices  102 us (24%)
  local copies, waits for them, and re-layouts  32.5 us (8%)
  between operations  15.4 us (4%)
  other arithmetic  9.77 us (2%)
    pallas_call x46, Pallas kernels, call(): pl.pallas_call(body, out_shape=out_shapes, in_specs=specs, out_specs=out_...  150 us
    ppermute x48, waiting for transfers between devices, peers(): out.append(lax.ppermute(v, 'img', [(i, i ^ m << shift) for i in range(ni)]))  61.4 us
    ppermute x48, starting transfers between devices, peers(): out.append(lax.ppermute(v, 'img', [(i, i ^ m << shift) for i in range(ni)]))  59.5 us
    ppermute x18, waiting for transfers between devices, over_ch(): return lax.ppermute(v, 'ch', [(i, i ^ k) for i in range(nc)])  30 us
    unnamed x100, local copies, waits for them, and re-layouts  26.5 us
    ppermute x18, starting transfers between devices, to_peers(): out.append(lax.ppermute(parts[m if len(parts) > 1 else 0], 'img', perm))  25.6 us
    ppermute x18, starting transfers between devices, over_ch(): return lax.ppermute(v, 'ch', [(i, i ^ k) for i in range(nc)])  9.85 us
  transfers between devices with their start and end apart: 91, of which 43 were waited for; matrix products, arithmetic and copies ran while one was open for 5% of the time, Pallas kernels for 31%

profile of v2, /device:TPU:0, one launch (start us, length us, event | category | flops | bytes accessed | tf_op | source)
XLA Modules:
  0.0 413.2 jit_solution(4074130474129525688)
XLA Ops:
  7.8 2.6 collective-permute-start.1
  24.8 4.8 %collective-permute-done.11 = f32[26,128]{1,0:T(8,128)S(1)} collective-permute-done((f32[26,128]{1,0:T(8,128)S(1)}, f32[26,128]{1,0:T(8,128)S(1)}, u32[]{:S(2)}, u32[]{:S(2)}) %collective-permute-start.11) | collective-permute-done | bytes 13344 | tf_op jit(solution)/shard_map/ppermute | solution.py:1129
  32.4 14.9 %collective-permute-done.4.refs_8_.refs_12_.refs_9_.refs_18_.refs_15_.x2s = bf16[1632,256]{1,0:T(8,128)(2,1)S(1)} collective-permute-done((bf16[1632,256]{1,0:T(8,128)(2,1)S(1)}, bf16[1632,256]{1,0:T(8,128)(2,1)S(1)}, u32[]{:S(2)}, u32[]{:S(2)}) %collective-permute-start.4) | collective-permute-done | bytes 835616 | tf_op jit(solution)/shard_map/ppermute | solution.py:1129
  50.6 7.1 %reduce.17 = (f32[296,8,256]{2,1,0:T(8,128)S(1)}, f32[2,256]{1,0:T(2,128)S(1)}) custom-call(s32[4]{0:T(128)S(1)} %get-tuple-element.152.refs_0_.me, f32[3]{0:T(128)S(1)} %get-tuple-element.154.refs_1_.refs_2_.refs_14_, bf16[1568,256]{1,0:T(8,128)(2,1)} %bitcast.93, bf16[1568,256]{1,0:T(8,128)(2,1)} %collective-permute-done.refs_3_.refs_4_.refs_13_.x1b, ...), custom_call_target="tpu_custom_call" | custom-call | tf_op jit(solution)/shard_map/reduce/pallas_call | solution.py:295
  69.3 2.6 collective-permute-start.9
  75.6 10.3 %mix.1 = (f32[296,8,256]{2,1,0:T(8,128)S(1)}, bf16[1792,768]{1,0:T(8,128)(2,1)}, bf16[960,768]{1,0:T(8,128)(2,1)}, f32[2,256]{1,0:T(2,128)S(1)}, f32[296,8,256]{2,1,0:T(8,128)}) custom-call(s32[4]{0:T(128)S(1)} %get-tuple-element.152.refs_0_.me, f32[3]{0:T(128)S(1)} %get-tuple-element.154.refs_1_.refs_2_.refs_14_, f32[296,8,256]{2,1,0:T(8,128)S(1)} %copy-done.15, ...), custom_call_target="tpu_custom_call" | custom-call | tf_op jit(solution)/shard_map/mix/pallas_call | solution.py:295
  87.2 2.8 collective-permute-start.16
  92.4 2.8 collective-permute-start.17
  96.9 7.3 %expand.1 = (f32[296,8,1024]{2,1,0:T(8,128)S(1)}, bf16[2368,256]{1,0:T(8,128)(2,1)}, f32[2,1024]{1,0:T(2,128)S(1)}, f32[296,8,256]{2,1,0:T(8,128)}) custom-call(s32[4]{0:T(128)S(1)} %get-tuple-element.152.refs_0_.me, f32[3]{0:T(128)S(1)} %get-tuple-element.154.refs_1_.refs_2_.refs_14_, f32[296,8,256]{2,1,0:T(8,128)S(1)} %get-tuple-element.159.refs_2_, ...), custom_call_target="tpu_custom_call" | custom-call | tf_op jit(solution)/shard_map/expand/pallas_call | solution.py:295
  104.2 8.1 %collective-permute-done.20.refs_10_.refs_17_ = bf16[4608,128]{1,0:T(8,128)(2,1)} collective-permute-done((bf16[4608,128]{1,0:T(8,128)(2,1)}, bf16[4608,128]{1,0:T(8,128)(2,1)}, u32[]{:S(2)}, u32[]{:S(2)}) %collective-permute-start.20) | collective-permute-done | bytes 1179680 | tf_op jit(solution)/shard_map/ppermute | solution.py:1129
  114.1 2.9 collective-permute-done.21.refs_1_
  117.6 4.0 collective-permute-done.23.refs_3_
  122.1 2.7 collective-permute-start.24
  126.7 10.3 %narrow.1 = (f32[2,2,7,7,8,512]{5,4,3,2,1,0:T(8,128)S(1)}, f32[2,2,5,5,8,512]{5,4,3,2,1,0:T(8,128)S(1)}, bf16[2368,1024]{1,0:T(8,128)(2,1)}, bf16[592,1024]{1,0:...) custom-call(s32[4]{0:T(128)S(1)} %get-tuple-element.152.refs_0_.me, ...), custom_call_target="tpu_custom_call" | custom-call | tf_op jit(solution)/shard_map/narrow/pallas_call | solution.py:295
  137.9 2.8 collective-permute-done.25.refs_1_
  141.4 3.9 collective-permute-done.27.refs_3_
  145.9 2.7 collective-permute-start.28
  151.5 8.7 %stride.1 = (f32[74,8,512]{2,1,0:T(8,128)S(1)}, bf16[592,4608]{1,0:T(8,128)(2,1)}, f32[2,512]{1,0:T(2,128)S(1)}, f32[2,2,7,7,8,512]{5,4,3,2,1,0:T(8,128)}, f32[2,2,5,5,8,512]{5,4,3,2,1,0:T(8,128)}) custom-call(s32[4]{0:T(128)S(1)} %get-tuple-element.152.refs_0_.me, f32[3]{0:T(128)S(1)} %get-tuple-element.153.refs_1_.nf, ...), custom_call_target="tpu_custom_call" | custom-call | tf_op jit(solution)/shard_map/stride/pallas_call | solution.py:295
  160.9 2.8 collective-permute-start.34
  166.1 2.9 collective-permute-start.35
  169.0 3.8 short.1
  172.8 2.8 widen.1
  181.0 2.6 collective-permute-done.38.refs_3_
  184.9 4.0 collective-permute-done.39.refs_5_.refs_6_
  188.8 6.7 %total.1 = (f32[49,8,512]{2,1,0:T(8,128)}, f32[25,8,512]{2,1,0:T(8,128)}, f32[2,74,8,512]{3,2,1,0:T(8,128)S(1)}, f32[2,3,512]{2,1,0:T(4,128)S(1)}) custom-call(s32[4]{0:T(128)S(1)} %get-tuple-element.152.refs_0_.me, f32[3]{0:T(128)S(1)} %get-tuple-element.153.refs_1_.nf, f32[2,74,8,512]{3,2,1,0:T(8,128)S(1)} %get-tuple-element.181.refs_2_.refs_3_, ...), custom_call_target="tpu_custom_call" | custom-call | tf_op jit(solution)/shard_map/total/pallas_call | solution.py:295
  196.5 2.6 collective-permute-start.42
  201.8 4.0 collective-permute-done.43.refs_9_
  205.8 3.2 back_wide.1
  209.1 3.6 back_short.1.refs_23_
  225.0 3.9 collective-permute-done.48.refs_8_
  230.1 10.3 %back_stride.1 = (f32[2,2,7,7,8,512]{5,4,3,2,1,0:T(8,128)S(1)}, f32[2,2,5,5,8,512]{5,4,3,2,1,0:T(8,128)S(1)}, bf16[592,512]{1,0:T(8,128)(2,1)S(1)}, f32[2,512]{1,0:T(2,128)S(1)}, f32[2,512]{1,0:T(2,128)S(1)}) custom-call(s32[4]{0:T(128)S(1)} %get-tuple-element.152.refs_0_.me, f32[3]{0:T(128)S(1)} %get-tuple-element.153.refs_1_.nf, ...), custom_call_target="tpu_custom_call" | custom-call | tf_op jit(solution)/shard_map/back_stride/pallas_call | solution.py:295
  249.4 3.8 dw_stride.1
  255.7 3.9 collective-permute-done.52.refs_10_
  261.0 17.5 %back_narrow.1 = (bf16[2368,1024]{1,0:T(8,128)(2,1)S(1)}, bf16[2368,512]{1,0:T(8,128)(2,1)}, f32[2,1024]{1,0:T(2,128)S(1)}, f32[2,512]{1,0:T(2,128)S(1)}) custom-call(s32[4]{0:T(128)S(1)} %get-tuple-element.152.refs_0_.me, f32[3]{0:T(128)S(1)} %get-tuple-element.154.refs_1_.refs_2_.refs_14_, f32[2,2,7,7,8,512]{5,4,3,2,1,0:T(8,128)} %copy-done.12, ...), custom_call_target="tpu_custom_call" | custom-call | tf_op jit(solution)/shard_map/back_narrow/pallas_call | solution.py:295
  286.9 3.7 collective-permute-done.58.refs_8_
  291.5 4.2 %collective-permute-start.60 = (bf16[576,128]{1,0:T(8,128)(2,1)S(1)}, bf16[576,128]{1,0:T(8,128)(2,1)S(1)}, u32[]{:S(2)}, u32[]{:S(2)}) collective-permute-start(bf16[576,128]{1,0:T(8,128)(2,1)S(1)} %get-tuple-element.224), channel_id=1, source_target_pairs={{0,16},{4,20},{8,24},{12,28},{16,0},{20,4},{24,8},{28,12},{1,17},{... | collective-permute-start | bytes 442376 | tf_op jit(solution)/shard_map/ppermute | solution.py:1187
  296.3 9.5 %back_expand.1 = (f32[296,8,256]{2,1,0:T(8,128)S(1)}, bf16[2368,256]{1,0:T(8,128)(2,1)}, bf16[2368,256]{1,0:T(8,128)(2,1)}, f32[2,256]{1,0:T(2,128)S(1)}, f32[2,1024]{1,0:T(2,128)S(1)}) custom-call(s32[4]{0:T(128)S(1)} %get-tuple-element.152.refs_0_.me, f32[3]{0:T(128)S(1)} %get-tuple-element.154.refs_1_.refs_2_.refs_14_, ...), custom_call_target="tpu_custom_call" | custom-call | tf_op jit(solution)/shard_map/back_expand/pallas_call | solution.py:295
  306.6 2.8 collective-permute-start.64
  319.3 2.9 collective-permute-start.67
  322.3 10.8 %back_mix.1 = (f32[296,8,256]{2,1,0:T(8,128)S(1)}, bf16[2368,256]{1,0:T(8,128)(2,1)}, f32[2,256]{1,0:T(2,128)S(1)}, f32[2,256]{1,0:T(2,128)S(1)}) custom-call(s32[4]{0:T(128)S(1)} %get-tuple-element.152.refs_0_.me, f32[3]{0:T(128)S(1)} %get-tuple-element.154.refs_1_.refs_2_.refs_14_, f32[296,8,256]{2,1,0:T(8,128)S(1)} %get-tuple-element.221.refs_2_, ...), custom_call_target="tpu_custom_call" | custom-call | tf_op jit(solution)/shard_map/back_mix/pallas_call | solution.py:295
  339.7 2.6 collective-permute-start.73
  350.3 4.2 %dw_mix.1.dmix = f32[1152,128]{1,0:T(8,128)S(1)} custom-call(s32[4]{0:T(128)S(1)} %get-tuple-element.152.refs_0_.me, bf16[1792,768]{1,0:T(8,128)(2,1)S(1)} %copy-done.13, bf16[960,768]{1,0:T(8,128)(2,1)S(1)} %copy-done.19, bf16[2368,256]{1,0:T(8,128)(2,1)S(1)} %copy-done.22), custom_call_target="tpu_custom_call" | custom-call | tf_op jit(solution)/shard_map/dw_mix/pallas_call | solution.py:295
  354.5 5.9 %back_reduce.1 = (f32[196,8,256]{2,1,0:T(8,128)}, f32[100,8,256]{2,1,0:T(8,128)}, bf16[2368,256]{1,0:T(8,128)(2,1)S(1)}, f32[2,256]{1,0:T(2,128)S(1)}) custom-call(s32[4]{0:T(128)S(1)} %get-tuple-element.152.refs_0_.me, f32[3]{0:T(128)S(1)} %get-tuple-element.154.refs_1_.refs_2_.refs_14_, f32[296,8,256]{2,1,0:T(8,128)S(1)} %get-tuple-element.238.refs_2_, ...), custom_call_target="tpu_custom_call" | custom-call | tf_op jit(solution)/shard_map/back_reduce/pallas_call | solution.py:295
  360.5 3.2 dw_reduce.1
  366.0 3.7 collective-permute-done.77
  372.5 2.6 collective-permute-start.86
  377.7 2.6 collective-permute-done.79.refs_2_
  381.5 3.2 collective-permute-start.82
  (341 shorter events, 156.4 us)
Async XLA Ops:
  7.2 394.9 %all-reduce.3.cloned.1.call-start = ((), (), s32[]{:S(2)}) async-start(), calls=%async_computation | async-start | bytes 3145728 | tf_op jit(solution)/shard_map/psum | solution.py:1614
  7.3 40.1 %collective-permute-start = (bf16[1568,256]{1,0:T(8,128)(2,1)}, bf16[1568,256]{1,0:T(8,128)(2,1)}, u32[]{:S(2)}, u32[]{:S(2)}) collective-permute-start(bf16[1568,256]{1,0:T(8,128)(2,1)} %bitcast.91), channel_id=1, source_target_pairs={{0,1},{1,0},{2,3},{3,2},{4,5},{5,4},{6,7},{7,6},{8,9},{9,8},{10,11... | collective-permute-start | bytes 2408456 | tf_op jit(solution)/shard_map/ppermute | solution.py:1129
  7.8 24.5 %collective-permute-start.1 = (bf16[1568,256]{1,0:T(8,128)(2,1)}, bf16[1568,256]{1,0:T(8,128)(2,1)}, u32[]{:S(2)}, u32[]{:S(2)}) collective-permute-start(bf16[1568,256]{1,0:T(8,128)(2,1)} %bitcast.92), channel_id=1, source_target_pairs={{0,2},{1,3},{2,0},{3,1},{4,6},{5,7},{6,4},{7,5},{8,10},{9,11},{10,... | collective-permute-start | bytes 2408456 | tf_op jit(solution)/shard_map/ppermute | solution.py:1129
  16.0 13.6 %collective-permute-start.11 = (f32[26,128]{1,0:T(8,128)S(1)}, f32[26,128]{1,0:T(8,128)S(1)}, u32[]{:S(2)}, u32[]{:S(2)}) collective-permute-start(f32[26,128]{1,0:T(8,128)S(1)} %bitcast.131), channel_id=1, source_target_pairs={{0,2},{1,3},{2,0},{3,1},{4,6},{5,7},{6,4},{7,5},{8,10},{9,11},{10,... | collective-permute-start | bytes 39944 | tf_op jit(solution)/shard_map/ppermute | solution.py:1129
  16.1 15.0 %collective-permute-start.10 = (f32[26,128]{1,0:T(8,128)S(1)}, f32[26,128]{1,0:T(8,128)S(1)}, u32[]{:S(2)}, u32[]{:S(2)}) collective-permute-start(f32[26,128]{1,0:T(8,128)S(1)} %bitcast.132), channel_id=1, source_target_pairs={{0,1},{1,0},{2,3},{3,2},{4,5},{5,4},{6,7},{7,6},{8,9},{9,8},{10,11... | collective-permute-start | bytes 39944 | tf_op jit(solution)/shard_map/ppermute | solution.py:1129
  21.4 25.9 %collective-permute-start.4 = (bf16[1632,256]{1,0:T(8,128)(2,1)S(1)}, bf16[1632,256]{1,0:T(8,128)(2,1)S(1)}, u32[]{:S(2)}, u32[]{:S(2)}) collective-permute-start(bf16[1632,256]{1,0:T(8,128)(2,1)S(1)} %slice_dynamic-update-slice_fusion.refs_6_.refs_10_.refs_7_.refs_16_.refs_13_.x0s), channel_id=1, source_target_pairs={{0,2},{1,3},{2,0},{3,1},{4,6},{5,7},{6,4},{7,5},{8,10},{9,11},{10,... | collective-permute-start | bytes 2506760 | tf_op jit(solution)/shard_map/ppermute | solution.py:1129
  31.1 16.2 %collective-permute-start.3 = (bf16[1632,256]{1,0:T(8,128)(2,1)S(1)}, bf16[1632,256]{1,0:T(8,128)(2,1)S(1)}, u32[]{:S(2)}, u32[]{:S(2)}) collective-permute-start(bf16[1632,256]{1,0:T(8,128)(2,1)S(1)} %slice_dynamic-update-slice_fusion.refs_6_.refs_10_.refs_7_.refs_16_.refs_13_.x0s), channel_id=1, source_target_pairs={{0,1},{1,0},{2,3},{3,2},{4,5},{5,4},{6,7},{7,6},{8,9},{9,8},{10,11... | collective-permute-start | bytes 2506760 | tf_op jit(solution)/shard_map/ppermute | solution.py:1129
  32.3 15.1 %collective-permute-start.2 = (bf16[1568,256]{1,0:T(8,128)(2,1)}, bf16[1568,256]{1,0:T(8,128)(2,1)S(1)}, u32[]{:S(2)}, u32[]{:S(2)}) collective-permute-start(bf16[1568,256]{1,0:T(8,128)(2,1)} %collective-permute-done.1.refs_4_.refs_5_.refs_14_.x2b), channel_id=1, source_target_pairs={{0,1},{1,0},{2,3},{3,2},{4,5},{5,4},{6,7},{7,6},{8,9},{9,8},{10,11... | collective-permute-start | bytes 2408456 | tf_op jit(solution)/shard_map/ppermute | solution.py:1129
  59.2 26.6 %collective-permute-start.13 = (bf16[1536,128]{1,0:T(8,128)(2,1)}, bf16[1536,128]{1,0:T(8,128)(2,1)S(1)}, u32[]{:S(2)}, u32[]{:S(2)}) collective-permute-start(bf16[1536,128]{1,0:T(8,128)(2,1)} %pad_maximum_fusion.1.refs_6_.refs_14_.refs_25_.refs_13_), channel_id=1, source_target_pairs={{0,2},{1,3},{2,0},{3,1},{4,6},{5,7},{6,4},{7,5},{8,10},{9,11},{10,... | collective-permute-start | bytes 1179656 | tf_op jit(solution)/shard_map/ppermute | solution.py:1129
  85.9 26.4 %collective-permute-start.20 = (bf16[4608,128]{1,0:T(8,128)(2,1)}, bf16[4608,128]{1,0:T(8,128)(2,1)}, u32[]{:S(2)}, u32[]{:S(2)}) collective-permute-start(bf16[4608,128]{1,0:T(8,128)(2,1)} %bitcast.16.refs_8_.refs_15_), channel_id=1, source_target_pairs={{0,2},{1,3},{2,0},{3,1},{4,6},{5,7},{6,4},{7,5},{8,10},{9,11},{10,... | collective-permute-start | bytes 3538952 | tf_op jit(solution)/shard_map/ppermute | solution.py:1129
  87.0 8.2 %collective-permute-start.18 = (bf16[1536,128]{1,0:T(8,128)(2,1)}, bf16[1536,128]{1,0:T(8,128)(2,1)}, u32[]{:S(2)}, u32[]{:S(2)}) collective-permute-start(bf16[1536,128]{1,0:T(8,128)(2,1)} %pad_maximum_fusion.1.refs_6_.refs_14_.refs_25_.refs_13_), channel_id=1, source_target_pairs={{0,1},{1,0},{2,3},{3,2},{4,5},{5,4},{6,7},{7,6},{8,9},{9,8},{10,11... | collective-permute-start | bytes 1179656 | tf_op jit(solution)/shard_map/ppermute | solution.py:1129
  90.1 6.9 %collective-permute-start.19 = (bf16[1536,128]{1,0:T(8,128)(2,1)S(1)}, bf16[1536,128]{1,0:T(8,128)(2,1)}, u32[]{:S(2)}, u32[]{:S(2)}) collective-permute-start(bf16[1536,128]{1,0:T(8,128)(2,1)S(1)} %collective-permute-done.13.refs_8_.refs_16_.refs_27_.refs_15_), channel_id=1, source_target_pairs={{0,1},{1,0},{2,3},{3,2},{4,5},{5,4},{6,7},{7,6},{8,9},{9,8},{10,11... | collective-permute-start | bytes 1179656 | tf_op jit(solution)/shard_map/ppermute | solution.py:1129
  112.3 47.9 %collective-permute-start.31 = (bf16[2128,512]{1,0:T(8,128)(2,1)S(1)}, bf16[2128,512]{1,0:T(8,128)(2,1)S(1)}, u32[]{:S(2)}, u32[]{:S(2)}) collective-permute-start(bf16[2128,512]{1,0:T(8,128)(2,1)S(1)} %copy-done.25), channel_id=1, source_target_pairs={{0,2},{1,3},{2,0},{3,1},{4,6},{5,7},{6,4},{7,5},{8,10},{9,11},{10,... | collective-permute-start | bytes 6537224 | tf_op jit(solution)/shard_map/ppermute | solution.py:1129
  112.8 35.8 %collective-permute-start.29 = (bf16[4608,128]{1,0:T(8,128)(2,1)}, bf16[4608,128]{1,0:T(8,128)(2,1)S(1)}, u32[]{:S(2)}, u32[]{:S(2)}) collective-permute-start(bf16[4608,128]{1,0:T(8,128)(2,1)} %bitcast.16.refs_8_.refs_15_), channel_id=1, source_target_pairs={{0,1},{1,0},{2,3},{3,2},{4,5},{5,4},{6,7},{7,6},{8,9},{9,8},{10,11... | collective-permute-start | bytes 3538952 | tf_op jit(solution)/shard_map/ppermute | solution.py:1129
  112.8 37.6 %collective-permute-start.30 = (bf16[4608,128]{1,0:T(8,128)(2,1)}, bf16[4608,128]{1,0:T(8,128)(2,1)S(1)}, u32[]{:S(2)}, u32[]{:S(2)}) collective-permute-start(bf16[4608,128]{1,0:T(8,128)(2,1)} %collective-permute-done.20.refs_10_.refs_17_), channel_id=1, source_target_pairs={{0,1},{1,0},{2,3},{3,2},{4,5},{5,4},{6,7},{7,6},{8,9},{9,8},{10,11... | collective-permute-start | bytes 3538952 | tf_op jit(solution)/shard_map/ppermute | solution.py:1129
  166.1 6.8 %collective-permute-start.35 = (f32[2,512]{1,0:T(2,128)S(1)}, f32[2,512]{1,0:T(2,128)S(1)}, u32[]{:S(2)}, u32[]{:S(2)}) collective-permute-start(f32[2,512]{1,0:T(2,128)S(1)} %merge.10.refs_3_.sa5.refs_4_), channel_id=1, source_target_pairs={{0,16},{4,20},{8,24},{12,28},{16,0},{20,4},{24,8},{28,12},{1,17},{... | collective-permute-start | bytes 12296 | tf_op jit(solution)/shard_map/ppermute | solution.py:1139
  212.6 43.1 %collective-permute-start.53 = (bf16[74,8,1024]{2,1,0:T(8,128)(2,1)S(1)}, bf16[74,8,1024]{2,1,0:T(8,128)(2,1)}, u32[]{:S(2)}, u32[]{:S(2)}) collective-permute-start(bf16[74,8,1024]{2,1,0:T(8,128)(2,1)S(1)} %back_short.1.refs_23_), channel_id=1, source_target_pairs={{0,1},{1,0},{2,3},{3,2},{4,5},{5,4},{6,7},{7,6},{8,9},{9,8},{10,11... | collective-permute-start | bytes 3637256 | tf_op jit(solution)/shard_map/ppermute | solution.py:1129
  216.7 5.9 %collective-permute-start.45 = (f32[2,512]{1,0:T(2,128)S(1)}, f32[2,512]{1,0:T(2,128)S(1)}, u32[]{:S(2)}, u32[]{:S(2)}) collective-permute-start(f32[2,512]{1,0:T(2,128)S(1)} %get-tuple-element.190.refs_0_), channel_id=1, source_target_pairs={{0,4},{4,0},{8,12},{12,8},{16,20},{20,16},{24,28},{28,24},{1,5},{5... | collective-permute-start | bytes 12296 | tf_op jit(solution)/shard_map/ppermute | solution.py:1139
  243.3 9.8 %collective-permute-start.49 = (f32[2,512]{1,0:T(2,128)S(1)}, f32[2,512]{1,0:T(2,128)S(1)}, u32[]{:S(2)}, u32[]{:S(2)}) collective-permute-start(f32[2,512]{1,0:T(2,128)S(1)} %get-tuple-element.203.refs_0_), channel_id=1, source_target_pairs={{0,4},{4,0},{8,12},{12,8},{16,20},{20,16},{24,28},{28,24},{1,5},{5... | collective-permute-start | bytes 12296 | tf_op jit(solution)/shard_map/ppermute | solution.py:1139
  243.8 9.3 %collective-permute-start.50 = (f32[2,512]{1,0:T(2,128)S(1)}, f32[2,512]{1,0:T(2,128)S(1)}, u32[]{:S(2)}, u32[]{:S(2)}) collective-permute-start(f32[2,512]{1,0:T(2,128)S(1)} %get-tuple-element.203.refs_0_), channel_id=1, source_target_pairs={{0,8},{4,12},{8,0},{12,4},{16,24},{20,28},{24,16},{28,20},{1,9},{5... | collective-permute-start | bytes 12296 | tf_op jit(solution)/shard_map/ppermute | solution.py:1139
  244.8 8.4 %collective-permute-start.51 = (f32[2,512]{1,0:T(2,128)S(1)}, f32[2,512]{1,0:T(2,128)S(1)}, u32[]{:S(2)}, u32[]{:S(2)}) collective-permute-start(f32[2,512]{1,0:T(2,128)S(1)} %get-tuple-element.203.refs_0_), channel_id=1, source_target_pairs={{0,12},{4,8},{8,4},{12,0},{16,28},{20,24},{24,20},{28,16},{1,13},{... | collective-permute-start | bytes 12296 | tf_op jit(solution)/shard_map/ppermute | solution.py:1139
  253.2 25.4 %collective-permute-start.54 = (bf16[2304,128]{1,0:T(8,128)(2,1)}, bf16[2304,128]{1,0:T(8,128)(2,1)S(1)}, u32[]{:S(2)}, u32[]{:S(2)}) collective-permute-start(bf16[2304,128]{1,0:T(8,128)(2,1)} %get-tuple-element.213), channel_id=1, source_target_pairs={{0,4},{4,0},{8,12},{12,8},{16,20},{20,16},{24,28},{28,24},{1,5},{5... | collective-permute-start | bytes 1769480 | tf_op jit(solution)/shard_map/ppermute | solution.py:1126
  285.3 5.3 %collective-permute-start.58 = (f32[2,1024]{1,0:T(2,128)S(1)}, f32[2,1024]{1,0:T(2,128)S(1)}, u32[]{:S(2)}, u32[]{:S(2)}) collective-permute-start(f32[2,1024]{1,0:T(2,128)S(1)} %add.68.refs_7_), channel_id=1, source_target_pairs={{0,16},{4,20},{8,24},{12,28},{16,0},{20,4},{24,8},{28,12},{1,17},{... | collective-permute-start | bytes 24584 | tf_op jit(solution)/shard_map/ppermute | solution.py:1139
  290.6 15.2 %collective-permute-start.59 = (bf16[576,128]{1,0:T(8,128)(2,1)S(1)}, bf16[576,128]{1,0:T(8,128)(2,1)S(1)}, u32[]{:S(2)}, u32[]{:S(2)}) collective-permute-start(bf16[576,128]{1,0:T(8,128)(2,1)S(1)} %get-tuple-element.223), channel_id=1, source_target_pairs={{0,8},{4,12},{8,0},{12,4},{16,24},{20,28},{24,16},{28,20},{1,9},{5... | collective-permute-start | bytes 442376 | tf_op jit(solution)/shard_map/ppermute | solution.py:1187
  291.5 14.3 %collective-permute-start.60 = (bf16[576,128]{1,0:T(8,128)(2,1)S(1)}, bf16[576,128]{1,0:T(8,128)(2,1)S(1)}, u32[]{:S(2)}, u32[]{:S(2)}) collective-permute-start(bf16[576,128]{1,0:T(8,128)(2,1)S(1)} %get-tuple-element.224), channel_id=1, source_target_pairs={{0,16},{4,20},{8,24},{12,28},{16,0},{20,4},{24,8},{28,12},{1,17},{... | collective-permute-start | bytes 442376 | tf_op jit(solution)/shard_map/ppermute | solution.py:1187
  295.7 10.1 %collective-permute-start.61 = (bf16[576,128]{1,0:T(8,128)(2,1)S(1)}, bf16[576,128]{1,0:T(8,128)(2,1)S(1)}, u32[]{:S(2)}, u32[]{:S(2)}) collective-permute-start(bf16[576,128]{1,0:T(8,128)(2,1)S(1)} %get-tuple-element.225), channel_id=1, source_target_pairs={{0,24},{4,28},{8,16},{12,20},{16,8},{20,12},{24,0},{28,4},{1,25},{... | collective-permute-start | bytes 442376 | tf_op jit(solution)/shard_map/ppermute | solution.py:1187
  305.9 7.4 %collective-permute-start.62 = (f32[2,256]{1,0:T(2,128)S(1)}, f32[2,256]{1,0:T(2,128)S(1)}, u32[]{:S(2)}, u32[]{:S(2)}) collective-permute-start(f32[2,256]{1,0:T(2,128)S(1)} %get-tuple-element.226.refs_0_), channel_id=1, source_target_pairs={{0,4},{4,0},{8,12},{12,8},{16,20},{20,16},{24,28},{28,24},{1,5},{5... | collective-permute-start | bytes 6152 | tf_op jit(solution)/shard_map/ppermute | solution.py:1139
  306.2 7.1 %collective-permute-start.63 = (f32[2,256]{1,0:T(2,128)S(1)}, f32[2,256]{1,0:T(2,128)S(1)}, u32[]{:S(2)}, u32[]{:S(2)}) collective-permute-start(f32[2,256]{1,0:T(2,128)S(1)} %get-tuple-element.226.refs_0_), channel_id=1, source_target_pairs={{0,8},{4,12},{8,0},{12,4},{16,24},{20,28},{24,16},{28,20},{1,9},{5... | collective-permute-start | bytes 6152 | tf_op jit(solution)/shard_map/ppermute | solution.py:1139
  306.6 6.7 %collective-permute-start.64 = (f32[2,256]{1,0:T(2,128)S(1)}, f32[2,256]{1,0:T(2,128)S(1)}, u32[]{:S(2)}, u32[]{:S(2)}) collective-permute-start(f32[2,256]{1,0:T(2,128)S(1)} %get-tuple-element.226.refs_0_), channel_id=1, source_target_pairs={{0,12},{4,8},{8,4},{12,0},{16,28},{20,24},{24,20},{28,16},{1,13},{... | collective-permute-start | bytes 6152 | tf_op jit(solution)/shard_map/ppermute | solution.py:1139
  316.4 16.7 %collective-permute-start.69 = (bf16[768,128]{1,0:T(8,128)(2,1)S(1)}, bf16[768,128]{1,0:T(8,128)(2,1)S(1)}, u32[]{:S(2)}, u32[]{:S(2)}) collective-permute-start(bf16[768,128]{1,0:T(8,128)(2,1)S(1)} %get-tuple-element.241), channel_id=1, source_target_pairs={{0,4},{4,0},{8,12},{12,8},{16,20},{20,16},{24,28},{28,24},{1,5},{5... | collective-permute-start | bytes 589832 | tf_op jit(solution)/shard_map/ppermute | solution.py:1126
  317.9 15.2 %collective-permute-start.66 = (bf16[576,128]{1,0:T(8,128)(2,1)S(1)}, bf16[576,128]{1,0:T(8,128)(2,1)S(1)}, u32[]{:S(2)}, u32[]{:S(2)}) collective-permute-start(bf16[576,128]{1,0:T(8,128)(2,1)S(1)} %stride_sum.1.refs_0_), channel_id=1, source_target_pairs={{0,8},{4,12},{8,0},{12,4},{16,24},{20,28},{24,16},{28,20},{1,9},{5... | collective-permute-start | bytes 442376 | tf_op jit(solution)/shard_map/ppermute | solution.py:1187
  319.3 13.8 %collective-permute-start.67 = (bf16[576,128]{1,0:T(8,128)(2,1)S(1)}, bf16[576,128]{1,0:T(8,128)(2,1)S(1)}, u32[]{:S(2)}, u32[]{:S(2)}) collective-permute-start(bf16[576,128]{1,0:T(8,128)(2,1)S(1)} %stride_sum.1.refs_0_), channel_id=1, source_target_pairs={{0,16},{4,20},{8,24},{12,28},{16,0},{20,4},{24,8},{28,12},{1,17},{... | collective-permute-start | bytes 442376 | tf_op jit(solution)/shard_map/ppermute | solution.py:1187
  322.3 10.9 %collective-permute-start.68 = (bf16[576,128]{1,0:T(8,128)(2,1)S(1)}, bf16[576,128]{1,0:T(8,128)(2,1)S(1)}, u32[]{:S(2)}, u32[]{:S(2)}) collective-permute-start(bf16[576,128]{1,0:T(8,128)(2,1)S(1)} %stride_sum.1.refs_0_), channel_id=1, source_target_pairs={{0,24},{4,28},{8,16},{12,20},{16,8},{20,12},{24,0},{28,4},{1,25},{... | collective-permute-start | bytes 442376 | tf_op jit(solution)/shard_map/ppermute | solution.py:1187
  344.6 15.9 %collective-permute-start.74 = (bf16[192,128]{1,0:T(8,128)(2,1)S(1)}, bf16[192,128]{1,0:T(8,128)(2,1)S(1)}, u32[]{:S(2)}, u32[]{:S(2)}) collective-permute-start(bf16[192,128]{1,0:T(8,128)(2,1)S(1)} %get-tuple-element.258), channel_id=1, source_target_pairs={{0,8},{4,12},{8,0},{12,4},{16,24},{20,28},{24,16},{28,20},{1,9},{5... | collective-permute-start | bytes 147464 | tf_op jit(solution)/shard_map/ppermute | solution.py:1187
  344.9 15.5 %collective-permute-start.75 = (bf16[192,128]{1,0:T(8,128)(2,1)S(1)}, bf16[192,128]{1,0:T(8,128)(2,1)S(1)}, u32[]{:S(2)}, u32[]{:S(2)}) collective-permute-start(bf16[192,128]{1,0:T(8,128)(2,1)S(1)} %get-tuple-element.259), channel_id=1, source_target_pairs={{0,16},{4,20},{8,24},{12,28},{16,0},{20,4},{24,8},{28,12},{1,17},{... | collective-permute-start | bytes 147464 | tf_op jit(solution)/shard_map/ppermute | solution.py:1187
  347.3 13.2 %collective-permute-start.76 = (bf16[192,128]{1,0:T(8,128)(2,1)S(1)}, bf16[192,128]{1,0:T(8,128)(2,1)S(1)}, u32[]{:S(2)}, u32[]{:S(2)}) collective-permute-start(bf16[192,128]{1,0:T(8,128)(2,1)S(1)} %get-tuple-element.260), channel_id=1, source_target_pairs={{0,24},{4,28},{8,16},{12,20},{16,8},{20,12},{24,0},{28,4},{1,25},{... | collective-permute-start | bytes 147464 | tf_op jit(solution)/shard_map/ppermute | solution.py:1187
  363.7 5.9 %collective-permute-start.77 = (bf16[832,128]{1,0:T(8,128)(2,1)S(1)}, bf16[832,128]{1,0:T(8,128)(2,1)S(1)}, u32[]{:S(2)}, u32[]{:S(2)}) collective-permute-start(bf16[832,128]{1,0:T(8,128)(2,1)S(1)} %get-tuple-element.263), channel_id=1, source_target_pairs={{0,4},{4,0},{8,12},{12,8},{16,20},{20,16},{24,28},{28,24},{1,5},{5... | collective-permute-start | bytes 638984 | tf_op jit(solution)/shard_map/ppermute | solution.py:1126
  365.0 34.8 %collective-permute-start.89 = (bf16[2304,128]{1,0:T(8,128)(2,1)S(1)}, bf16[2304,128]{1,0:T(8,128)(2,1)S(1)}, u32[]{:S(2)}, u32[]{:S(2)}) collective-permute-start(bf16[2304,128]{1,0:T(8,128)(2,1)S(1)} %bitcast.99), channel_id=1, source_target_pairs={{0,4},{4,0},{8,12},{12,8},{16,20},{20,16},{24,28},{28,24},{1,5},{5... | collective-permute-start | bytes 1769480 | tf_op jit(solution)/shard_map/ppermute | solution.py:1126
  370.4 11.1 %collective-permute-start.85 = (bf16[192,128]{1,0:T(8,128)(2,1)S(1)}, bf16[192,128]{1,0:T(8,128)(2,1)S(1)}, u32[]{:S(2)}, u32[]{:S(2)}) collective-permute-start(bf16[192,128]{1,0:T(8,128)(2,1)S(1)} %mid_sum.1.refs_0_), channel_id=1, source_target_pairs={{0,8},{4,12},{8,0},{12,4},{16,24},{20,28},{24,16},{28,20},{1,9},{5... | collective-permute-start | bytes 147464 | tf_op jit(solution)/shard_map/ppermute | solution.py:1187
  372.5 12.3 %collective-permute-start.86 = (bf16[192,128]{1,0:T(8,128)(2,1)S(1)}, bf16[192,128]{1,0:T(8,128)(2,1)S(1)}, u32[]{:S(2)}, u32[]{:S(2)}) collective-permute-start(bf16[192,128]{1,0:T(8,128)(2,1)S(1)} %mid_sum.1.refs_0_), channel_id=1, source_target_pairs={{0,16},{4,20},{8,24},{12,28},{16,0},{20,4},{24,8},{28,12},{1,17},{... | collective-permute-start | bytes 147464 | tf_op jit(solution)/shard_map/ppermute | solution.py:1187
  375.0 5.2 %collective-permute-start.79 = (bf16[208,128]{1,0:T(8,128)(2,1)S(1)}, bf16[208,128]{1,0:T(8,128)(2,1)S(1)}, u32[]{:S(2)}, u32[]{:S(2)}) collective-permute-start(bf16[208,128]{1,0:T(8,128)(2,1)S(1)} %get-tuple-element.266), channel_id=1, source_target_pairs={{0,16},{4,20},{8,24},{12,28},{16,0},{20,4},{24,8},{28,12},{1,17},{... | collective-permute-start | bytes 159752 | tf_op jit(solution)/shard_map/ppermute | solution.py:1187
  375.4 6.0 %collective-permute-start.80 = (bf16[208,128]{1,0:T(8,128)(2,1)S(1)}, bf16[208,128]{1,0:T(8,128)(2,1)S(1)}, u32[]{:S(2)}, u32[]{:S(2)}) collective-permute-start(bf16[208,128]{1,0:T(8,128)(2,1)S(1)} %get-tuple-element.267), channel_id=1, source_target_pairs={{0,24},{4,28},{8,16},{12,20},{16,8},{20,12},{24,0},{28,4},{1,25},{... | collective-permute-start | bytes 159752 | tf_op jit(solution)/shard_map/ppermute | solution.py:1187
  380.3 6.2 %collective-permute-start.87 = (bf16[192,128]{1,0:T(8,128)(2,1)S(1)}, bf16[192,128]{1,0:T(8,128)(2,1)S(1)}, u32[]{:S(2)}, u32[]{:S(2)}) collective-permute-start(bf16[192,128]{1,0:T(8,128)(2,1)S(1)} %mid_sum.1.refs_0_), channel_id=1, source_target_pairs={{0,24},{4,28},{8,16},{12,20},{16,8},{20,12},{24,0},{28,4},{1,25},{... | collective-permute-start | bytes 147464 | tf_op jit(solution)/shard_map/ppermute | solution.py:1187
  381.4 7.3 %collective-permute-start.81 = (bf16[208,128]{1,0:T(8,128)(2,1)S(1)}, bf16[208,128]{1,0:T(8,128)(2,1)S(1)}, u32[]{:S(2)}, u32[]{:S(2)}) collective-permute-start(bf16[208,128]{1,0:T(8,128)(2,1)S(1)} %last_sum.1.refs_0_), channel_id=1, source_target_pairs={{0,8},{4,12},{8,0},{12,4},{16,24},{20,28},{24,16},{28,20},{1,9},{5... | collective-permute-start | bytes 159752 | tf_op jit(solution)/shard_map/ppermute | solution.py:1187
  381.5 7.2 %collective-permute-start.82 = (bf16[208,128]{1,0:T(8,128)(2,1)S(1)}, bf16[208,128]{1,0:T(8,128)(2,1)S(1)}, u32[]{:S(2)}, u32[]{:S(2)}) collective-permute-start(bf16[208,128]{1,0:T(8,128)(2,1)S(1)} %last_sum.1.refs_0_), channel_id=1, source_target_pairs={{0,16},{4,20},{8,24},{12,28},{16,0},{20,4},{24,8},{28,12},{1,17},{... | collective-permute-start | bytes 159752 | tf_op jit(solution)/shard_map/ppermute | solution.py:1187
  384.8 5.9 %collective-permute-start.83 = (bf16[208,128]{1,0:T(8,128)(2,1)S(1)}, bf16[208,128]{1,0:T(8,128)(2,1)S(1)}, u32[]{:S(2)}, u32[]{:S(2)}) collective-permute-start(bf16[208,128]{1,0:T(8,128)(2,1)S(1)} %last_sum.1.refs_0_), channel_id=1, source_target_pairs={{0,24},{4,28},{8,16},{12,20},{16,8},{20,12},{24,0},{28,4},{1,25},{... | collective-permute-start | bytes 159752 | tf_op jit(solution)/shard_map/ppermute | solution.py:1187
  387.0 6.8 %collective-permute-start.88 = (bf16[768,128]{1,0:T(8,128)(2,1)S(1)}, bf16[768,128]{1,0:T(8,128)(2,1)S(1)}, u32[]{:S(2)}, u32[]{:S(2)}) collective-permute-start(bf16[768,128]{1,0:T(8,128)(2,1)S(1)} %bitcast.103), channel_id=1, source_target_pairs={{0,4},{4,0},{8,12},{12,8},{16,20},{20,16},{24,28},{28,24},{1,5},{5... | collective-permute-start | bytes 589832 | tf_op jit(solution)/shard_map/ppermute | solution.py:1126
  391.3 5.9 %collective-permute-start.84 = (bf16[832,128]{1,0:T(8,128)(2,1)S(1)}, bf16[832,128]{1,0:T(8,128)(2,1)S(1)}, u32[]{:S(2)}, u32[]{:S(2)}) collective-permute-start(bf16[832,128]{1,0:T(8,128)(2,1)S(1)} %bitcast.101), channel_id=1, source_target_pairs={{0,4},{4,0},{8,12},{12,8},{16,20},{20,16},{24,28},{28,24},{1,5},{5... | collective-permute-start | bytes 638984 | tf_op jit(solution)/shard_map/ppermute | solution.py:1126
  (84 other events, 543.0 us)
Sparse Core Ops, SparseCore 0:
  255.1 99.7 all-reduce.2
